TPU v7x, 32 devices: a whole 2x2x4 slice. The times are simulated.
32 devices in a mesh: rep: 16 (over z, y, x), sp: 2 (over core).
Axes of the slice: x: 2, y: 2, z: 4, core: 2. Of those that a mesh axis runs over, the one named last changes fastest.
Arguments:
- level_four: bfloat16 [16, 96, 96, 256], P('rep', 'sp'), may hold values from -25 to 25
- level_six: bfloat16 [16, 24, 24, 256], P('rep', 'sp'), may hold values from -25 to 25
- conv_weight: bfloat16 [9, 256, 256], replicated, may hold values from -0.125 to 0.125
- bn_gain: float32 [2, 256], replicated, may hold values from 0.1 to 1.9
- bn_shift: float32 [2, 256], replicated, may hold values from -3 to 3
- cotan_four: bfloat16 [16, 96, 96, 256], P('rep', 'sp'), may hold values from -6 to 6
- cotan_six: bfloat16 [16, 24, 24, 256], P('rep', 'sp'), may hold values from -6 to 6
Outputs:
- grad_four: bfloat16 [16, 96, 96, 256], P('rep', 'sp')
- grad_six: bfloat16 [16, 24, 24, 256], P('rep', 'sp')
- grad_weight: float32 [9, 256, 256], P(None, 'sp')
- grad_gain: float32 [2, 256], replicated
- grad_shift: float32 [2, 256], replicated
All inputs are finite; a program needn't handle non-finite values.
Results may differ from a plain program's by a relative error of at most 0.0052.
Values may be sent and summed in bfloat16 or wider, within the bound.
No kernel may reach another device: no remote copies, remote signals or barrier semaphores. Data moves between devices by JAX's collectives and lax.ppermute only.
A program may use at most 128 MiB of HBM per device.

v0:
```python
import functools
from typing import NamedTuple

import jax
import jax.numpy as jnp
from jax import lax
from jax.experimental import pallas as pl
from jax.experimental.pallas import tpu as pltpu
from jax.sharding import PartitionSpec as P

GROUP = 16
RADIX = 4
FAR_FIRST = (3, 2, 1)
FIRST_TAPS = 4
EARLY_TAPS = 6
EPSILON = 1e-05
F32 = jnp.float32
BF16 = jnp.bfloat16
VMEM_LIMIT = 20 * 1024 * 1024
EDGE_LIMIT = 60 * 1024 * 1024


def chunk_of(rows, most, multiple=1):
    sizes = [size for size in range(1, most + 1) if rows % size == 0 and size % multiple == 0]
    return max(sizes) if sizes else rows


def pitch_of(cols):
    return -(-cols // 16) * 16


def parity(rep):
    return ((rep >> 2) ^ (rep >> 3)) & 1


def chunks_of(rows, most, multiple=1):
    size = chunk_of(rows, most, multiple)
    return [(start, start + size) for start in range(0, rows, size)]


def widen(cells, pitch):
    cells = cells.astype(F32)
    extra = pitch - cells.shape[0]
    if extra:
        cells = jnp.concatenate([cells, jnp.zeros((extra, cells.shape[1]), F32)], 0)
    return cells


def put_three(three, row, cells, cols, turned):
    pitch, chan = cells.shape
    left, right = pltpu.roll(cells, 1, 0), pltpu.roll(cells, pitch - 1, 0)
    if pitch == cols:
        col = lax.broadcasted_iota(jnp.int32, (8, chan), 0)
        left = jnp.concatenate([jnp.where(col == 0, 0.0, left[:8]), left[8:]], 0)
        right = jnp.concatenate([right[:-8], jnp.where(col == 7, 0.0, right[-8:])], 0)
    parts = (right, cells, left) if turned else (left, cells, right)
    for place, part in enumerate(parts):
        three[row, :, place * chan : (place + 1) * chan] = part.astype(BF16)


def beside(three, starts, size):
    pitch, width = three.shape[1:]
    return jnp.concatenate([three[start : start + size].reshape(size * pitch, width) for start in starts], 1)


def edges_valid(sp_count):
    index = lax.axis_index("sp")
    return jnp.where(index > 0, 1.0, 0.0), jnp.where(index < sp_count - 1, 1.0, 0.0)


def level_coefs(moments, gain, shift, count):
    mean = moments[0:1] / count
    spread = moments[1:2] / count - mean * mean
    return mean, lax.rsqrt(spread + EPSILON), gain, shift


def slope_of(conv, cotan, coefs):
    mean, rstd, gain, shift = coefs
    centred = conv.astype(F32) - mean
    half = centred * (0.5 * rstd * gain) + 0.5 * shift
    turn = jnp.tanh(half)
    return centred, cotan.astype(F32) * ((1.0 + turn) * (1.0 + half * (1.0 - turn)))


def masked(cells, cols):
    if cells.shape[0] == cols:
        return cells
    col = lax.broadcasted_iota(jnp.int32, cells.shape, 0)
    return jnp.where(col < cols, cells, 0.0)


def staged(fills, dots):
    fills[0]()
    for index, dot in enumerate(dots):
        if index + 1 < len(fills):
            fills[index + 1]()
        dot()


def conv_rows(lhs, w_ref):
    return jnp.dot(lhs, w_ref[...].reshape(lhs.shape[1], -1), preferred_element_type=F32).astype(BF16)


def add_moments(sums, conv, cols):
    chan = conv.shape[2]
    conv = conv.astype(F32)
    if conv.shape[1] != cols:
        conv = conv[:, :cols]
    conv = conv.reshape(-1, 8, chan)
    sums[0].append(jnp.sum(conv, 0))
    sums[1].append(jnp.sum(conv * conv, 0))


def folded(parts):
    total = parts[0]
    for part in parts[1:]:
        total = total + part
    return jnp.sum(total, 0, keepdims=True)


def inner_level(x_ref, w_ref, conv_ref, three, sums, most):
    rows, cols = x_ref.shape[:2]
    pitch = three.shape[1]

    def fill_row(row):
        put_three(three, row, widen(x_ref[row], pitch), cols, False)

    def dot(start, end):
        conv = conv_rows(beside(three, (start, start + 1, start + 2), end - start), w_ref)
        conv = conv.reshape(end - start, pitch, -1)
        conv_ref[start:end] = conv
        add_moments(sums, conv, cols)

    inner = rows - 2
    count = max(1, inner // most)
    bounds = [index * inner // count for index in range(count + 1)]
    fills, dots, done = [], [], 0
    for start, end in zip(bounds[:-1], bounds[1:]):
        fills.append(lambda todo=range(done, end + 2): [fill_row(row) for row in todo])
        done = end + 2
        dots.append(functools.partial(dot, start, end))
    return fills, dots


def inner_kernel(four_ref, six_ref, w_ref, conv_four_ref, conv_six_ref, moments_ref, three_four, three_six):
    sums_four, sums_six = ([], []), ([], [])
    fills_six, dots_six = inner_level(six_ref, w_ref, conv_six_ref, three_six, sums_six, 10)
    fills_four, dots_four = inner_level(four_ref, w_ref, conv_four_ref, three_four, sums_four, 8)
    staged(fills_six + fills_four, dots_six + dots_four)
    moments_ref[...] = jnp.concatenate([folded(parts) for parts in sums_four + sums_six], 0)


def outer_level(x_ref, top, bottom, valid, three):
    rows, cols = x_ref.shape[:2]
    pitch = three.shape[1]
    for edge in range(2):
        put_three(three, edge, top(edge) * valid[0], cols, False)
        put_three(three, 2 + edge, widen(x_ref[edge], pitch), cols, False)
        put_three(three, 4 + edge, widen(x_ref[rows - 2 + edge], pitch), cols, False)
        put_three(three, 6 + edge, bottom(edge) * valid[1], cols, False)
    return [beside(three, (start, start + 1, start + 2), 2) for start in (0, 4)]


def outer_kernel(
    sp_count, four_ref, six_ref, above_ref, below_ref, w_ref, inner_ref,
    conv_four_ref, conv_six_ref, moments_ref, three_four, three_six,
):
    cols_four = four_ref.shape[1]
    valid = edges_valid(sp_count)
    base, pitch_six = 3 * cols_four, three_six.shape[1]

    def reader(ref, start, pitch):
        return lambda edge: ref[start + edge * pitch : start + (edge + 1) * pitch].astype(F32)

    lhs = outer_level(
        four_ref, reader(above_ref, 0, cols_four), reader(below_ref, 0, cols_four), valid, three_four
    ) + outer_level(
        six_ref, reader(above_ref, base, pitch_six), reader(below_ref, base, pitch_six), valid, three_six
    )
    conv = conv_rows(jnp.concatenate(lhs, 0), w_ref)
    sums, begin = [], 0
    for conv_ref, cols in ((conv_four_ref, cols_four), (conv_six_ref, six_ref.shape[1])):
        cells = conv_ref.shape[0] * conv_ref.shape[1]
        rows = conv[begin : begin + cells].reshape(conv_ref.shape)
        begin += cells
        conv_ref[...] = rows
        parts = ([], [])
        add_moments(parts, rows[1:3], cols)
        sums += [folded(part) for part in parts]
    moments_ref[...] = inner_ref[...] + jnp.concatenate(sums, 0)


def turn_kernel(four_ref, six_ref, w_ref, turned_ref, turned_w_ref):
    rows_four, cols_four, chan = four_ref.shape
    rows_six, cols_six = six_ref.shape[:2]
    pitch = pitch_of(cols_six)
    for start, end in chunks_of(rows_four, 8, 4):
        cells = four_ref[start:end].reshape((end - start) * cols_four, chan)
        turned_ref[:, start * cols_four : end * cols_four] = cells.T
    cells = six_ref[...].astype(F32)
    cells = jnp.concatenate([cells, jnp.zeros((rows_six, pitch - cols_six, chan), F32)], 1).astype(BF16)
    turned_ref[:, rows_four * cols_four :] = cells.reshape(rows_six * pitch, chan).T
    for tap in range(9):
        turned_w_ref[tap * chan : (tap + 1) * chan] = w_ref[tap].T


def slope_level(inner_ref, outer_ref, cotan_ref, above, below, coefs, slope_ref):
    rows, cols, chan = cotan_ref.shape
    pitch = inner_ref.shape[1]

    def put(row, conv, cotan):
        centred, slope = slope_of(conv, widen(cotan, pitch), coefs)
        slope_ref[row] = slope
        return centred, slope

    def add(sums, pair):
        centred, slope = pair
        first = jnp.sum(slope.reshape(-1, 8, chan), 0)
        second = jnp.sum((slope * centred).reshape(-1, 8, chan), 0)
        return sums[0] + first, sums[1] + second

    def step(row, sums):
        return add(sums, put(row + 2, inner_ref[row], cotan_ref[row + 1]))

    put(0, outer_ref[0], above)
    put(rows + 1, outer_ref[3], below)
    zero = jnp.zeros((8, chan), F32)
    sums = add((zero, zero), put(1, outer_ref[1], cotan_ref[0]))
    sums = add(sums, put(rows, outer_ref[2], cotan_ref[rows - 1]))
    for row in range(rows - 2):
        sums = step(row, sums)
    first = 0.5 * jnp.sum(sums[0], 0, keepdims=True)
    return first, 0.5 * coefs[1] * jnp.sum(sums[1], 0, keepdims=True)


def slope_kernel(
    counts, inner_four_ref, inner_six_ref, outer_four_ref, outer_six_ref, cotan_four_ref, cotan_six_ref,
    above_ref, below_ref, moments_ref, gain_ref, shift_ref, slope_four_ref, slope_six_ref, slopes_ref,
):
    sums = ()
    cols_four = cotan_four_ref.shape[1]
    starts = (2 * cols_four, 3 * cols_four + 2 * inner_six_ref.shape[1])
    for level, (inner_ref, outer_ref, cotan_ref, slope_ref) in enumerate(
        (
            (inner_four_ref, outer_four_ref, cotan_four_ref, slope_four_ref),
            (inner_six_ref, outer_six_ref, cotan_six_ref, slope_six_ref),
        )
    ):
        pair = moments_ref[2 * level : 2 * level + 2]
        here = slice(level, level + 1)
        edge = slice(starts[level], starts[level] + inner_ref.shape[1])
        coefs = level_coefs(pair, gain_ref[here], shift_ref[here], counts[level])
        sums += slope_level(inner_ref, outer_ref, cotan_ref, above_ref[edge], below_ref[edge], coefs, slope_ref)
    slopes_ref[...] = jnp.concatenate(sums, 0)


def backward_level(cols, inner_ref, outer_ref, slope_ref, valid, coefs, slopes, count, three):
    rows = inner_ref.shape[0] + 2
    pitch = three.shape[1]
    mean, rstd, gain, shift = coefs
    lead = gain * rstd
    offset, factor = lead * (slopes[0:1] / count), lead * rstd * (slopes[1:2] / count)

    def fill_row(row):
        if 2 <= row < rows:
            conv = inner_ref[row - 2]
        else:
            conv = outer_ref[row if row < 2 else row - rows + 2]
        centred = conv.astype(F32) - mean
        dconv = masked((0.5 * lead) * slope_ref[row] - (offset + centred * factor), cols)
        if row == 0:
            dconv = dconv * valid[0]
        elif row == rows + 1:
            dconv = dconv * valid[1]
        put_three(three, row, dconv, cols, True)

    return fill_row


def taps_beside(three, start, end, taps):
    pitch, width = three.shape[1:]
    chan = width // 3
    parts = []
    for row_tap in range(3):
        low, high = max(taps[0] - 3 * row_tap, 0), min(taps[1] - 3 * row_tap, 3)
        if low < high:
            first = start + 2 - row_tap
            rows = three[first : first + end - start, :, low * chan : high * chan]
            parts.append(rows.reshape((end - start) * pitch, (high - low) * chan))
    return jnp.concatenate(parts, 1)


def backward_bounds(rows):
    bounds = [0, min(4, rows), min(16, rows)]
    while bounds[-1] < rows:
        bounds.append(min(bounds[-1] + 16, rows))
    return sorted(set(bounds))


def weight_dot(turned_ref, three_four, three_six, total, taps, start, end):
    rows_four, rows_six = three_four.shape[0] - 2, three_six.shape[0] - 2
    pitch = three_four.shape[1]
    first, last = start * pitch, end * pitch
    rhs = taps_beside(three_four, start, end, taps)
    if end == rows_four:
        rhs = jnp.concatenate([rhs, taps_beside(three_six, 0, rows_six, taps)], 0)
        last = turned_ref.shape[1]
    term = jnp.dot(turned_ref[:, first:last], rhs, preferred_element_type=F32)
    total[...] = total[...] + term if start else term


def put_shares(totals, sp_count, own_ref, sent_ref):
    taps, share, chan = own_ref.shape
    places = [(total, start) for total in totals for start in range(0, total.shape[1], chan)][:taps]
    place = lax.axis_index("sp") ^ parity(lax.axis_index("rep"))
    for step in range(sp_count):
        begin = pl.multiple_of((place ^ step) * share, share)
        for tap, (total, start) in enumerate(places):
            part = total[pl.ds(begin, share), start : start + chan]
            if step == 0:
                own_ref[tap] = part
            else:
                sent_ref[step - 1, tap] = part


def backward_kernel(
    counts, sp_count, cols, turned_ref, inner_four_ref, inner_six_ref, outer_four_ref, outer_six_ref,
    slope_four_ref, slope_six_ref, moments_ref, slopes_ref, gain_ref, shift_ref, three_four, three_six, own_ref,
    sent_ref, rest_ref, grad_gain_ref, grad_shift_ref, total,
):
    valid = edges_valid(sp_count)
    grad_gain_ref[...] = jnp.concatenate([slopes_ref[1:2], slopes_ref[3:4]], 0)
    grad_shift_ref[...] = jnp.concatenate([slopes_ref[0:1], slopes_ref[2:3]], 0)
    parts = []
    for level, inner_ref, outer_ref, slope_ref, three in (
        (0, inner_four_ref, outer_four_ref, slope_four_ref, three_four),
        (1, inner_six_ref, outer_six_ref, slope_six_ref, three_six),
    ):
        here = slice(level, level + 1)
        pair = slice(2 * level, 2 * level + 2)
        coefs = level_coefs(moments_ref[pair], gain_ref[here], shift_ref[here], counts[level])
        parts.append(
            backward_level(
                cols[level], inner_ref, outer_ref, slope_ref, valid, coefs, slopes_ref[pair], counts[level], three
            )
        )
    fill_four, fill_six = parts
    rows_four, rows_six = three_four.shape[0] - 2, three_six.shape[0] - 2
    bounds = backward_bounds(rows_four)
    fills, dots, done = [], [], 0
    for start, end in zip(bounds[:-1], bounds[1:]):
        todo = [functools.partial(fill_four, row) for row in range(done, end + 2)]
        if end == rows_four:
            todo += [functools.partial(fill_six, row) for row in range(rows_six + 2)]
        fills.append(lambda todo=todo: [fill() for fill in todo])
        done = end + 2
        dots.append(
            functools.partial(weight_dot, turned_ref, three_four, three_six, total, (0, EARLY_TAPS), start, end)
        )
    staged(fills, dots)
    put_shares([total], sp_count, own_ref, sent_ref)
    rest_ref[...] = total[:, FIRST_TAPS * rest_ref.shape[0] :]


def weight_kernel(sp_count, turned_ref, three_four, three_six, rest_ref, own_ref, sent_ref, total):
    for start, end in chunks_of(three_four.shape[0] - 2, 16, 4):
        weight_dot(turned_ref, three_four, three_six, total, (EARLY_TAPS, 9), start, end)
    put_shares([rest_ref, total], sp_count, own_ref, sent_ref)


def input_chunks(three, turned, grad, chunks, offset, sent=None):
    cols, chan = grad.shape[1:]
    pitch = three.shape[1]
    for index, (start, end) in enumerate(chunks):
        size = end - start
        lhs = beside(three, (start + 2, start + 1, start), size)
        term = jnp.dot(lhs, turned[...], preferred_element_type=F32)
        grad[start - offset : end - offset] = term.reshape(size, pitch, chan)[:, :cols].astype(BF16)
        if sent is not None:
            sent(index, start, end)


def input_kernel(chunks, three_four, turned, grad_ref):
    input_chunks(three_four, turned, grad_ref, chunks, chunks[0][0])


def input_last_kernel(chunks, bounds, three_four, three_six, turned, *rest):
    count = len(bounds) - 1
    earlier, rest = rest[:count], rest[count:]
    grad_four_ref, grad_six_ref, grad_four, grad_six, sems, sems_four, sems_six = rest
    copies = [
        pltpu.make_async_copy(part, grad_four_ref.at[bounds[index] : bounds[index + 1]], sems.at[index])
        for index, part in enumerate(earlier)
    ]
    for copy in copies:
        copy.start()

    def sender(grad, grad_ref, offset, sems):
        def sent(index, start, end):
            copy = pltpu.make_async_copy(grad.at[start - offset : end - offset], grad_ref.at[start:end], sems.at[index])
            copy.start()
            copies.append(copy)

        return sent

    six_chunks = chunks_of(grad_six.shape[0], 12)
    input_chunks(three_six, turned, grad_six, six_chunks, 0, sender(grad_six, grad_six_ref, 0, sems_six))
    done = bounds[-1]
    input_chunks(three_four, turned, grad_four, chunks, done, sender(grad_four, grad_four_ref, done, sems_four))
    for copy in copies:
        copy.wait()


def swap(array, axis, stride):
    count = lax.axis_size(axis)
    return lax.ppermute(array, axis, [(i, i ^ stride) for i in range(count)])


def edge_kernel(starts, four_ref, six_ref, cotan_four_ref, cotan_six_ref, *rest):
    outs, six_rows, sems = rest[:-2], rest[-2], rest[-1]
    rows_four, cols_four = four_ref.shape[:2]
    rows_six = six_ref.shape[0]
    pitch = pitch_of(six_ref.shape[1])
    copies = []
    for number, (start, out_ref) in enumerate(zip(starts, outs)):
        last = (1 - jnp.minimum(lax.axis_index("sp"), 1)) if start is None else start
        for part, (ref, row) in enumerate(
            (
                (four_ref, last * (rows_four - 2)),
                (four_ref, last * (rows_four - 2) + 1),
                (cotan_four_ref, last * (rows_four - 1)),
                (six_ref, last * (rows_six - 2)),
                (six_ref, last * (rows_six - 2) + 1),
                (cotan_six_ref, last * (rows_six - 1)),
            )
        ):
            if part < 3:
                target = out_ref.at[part * cols_four : (part + 1) * cols_four]
            else:
                target = six_rows.at[number, part - 3]
            copies.append(pltpu.make_async_copy(ref.at[row], target, sems.at[number, part]))
    for copy in copies:
        copy.start()
    for copy in copies:
        copy.wait()
    for number, out_ref in enumerate(outs):
        for part in range(3):
            begin = 3 * cols_four + part * pitch
            out_ref[begin : begin + pitch] = widen(six_rows[number, part], pitch).astype(BF16)


def edges(four, six, cotan_four, cotan_six):
    count = lax.axis_size("sp")
    starts = (None,) if count == 2 else (0, 1)
    length = 3 * four.shape[1] + 3 * pitch_of(six.shape[1])
    vmem = pl.BlockSpec(memory_space=pltpu.VMEM)
    hbm = pl.BlockSpec(memory_space=pltpu.HBM)
    outs = pl.pallas_call(
        functools.partial(edge_kernel, starts),
        out_shape=tuple(jax.ShapeDtypeStruct((length, four.shape[2]), BF16) for _ in starts),
        in_specs=[hbm] * 4,
        out_specs=tuple(vmem for _ in starts),
        scratch_shapes=[
            pltpu.VMEM((len(starts), 3) + six.shape[1:], BF16),
            pltpu.SemaphoreType.DMA((len(starts), 6)),
        ],
        compiler_params=pltpu.CompilerParams(vmem_limit_bytes=EDGE_LIMIT),
        name="edges",
    )(four, six, cotan_four, cotan_six)
    if count == 2:
        met = swap(outs[0], "sp", 1)
        return met, met
    above = lax.ppermute(outs[1], "sp", [(i, (i + 1) % count) for i in range(count)])
    below = lax.ppermute(outs[0], "sp", [((i + 1) % count, i) for i in range(count)])
    return above, below


def swap_across(array, axis, stride):
    count, sp_count = lax.axis_size("rep"), lax.axis_size("sp")
    rep_stride, sp_stride = (stride, 1) if axis == "rep" else (0, stride ^ 1)
    pairs = [
        (rep * sp_count + sp, (rep ^ rep_stride) * sp_count + (sp ^ sp_stride))
        for rep in range(count)
        for sp in range(sp_count)
    ]
    return lax.ppermute(array, ("rep", "sp"), pairs)


def group_sum(sums):
    sums = sums + swap(sums, "sp", 1)
    stride = 2
    while stride < lax.axis_size("sp"):
        sums = sums + swap_across(sums, "sp", stride)
        stride = 2 * stride
    stride = 1
    while stride < GROUP:
        met = lax.optimization_barrier([swap_across(sums, "rep", k * stride) for k in FAR_FIRST])
        sums = (sums + met[2]) + (met[1] + met[0])
        stride = RADIX * stride
    return sums


def every_group(sums):
    stride = GROUP
    while stride < lax.axis_size("rep"):
        sums = sums + swap(sums, "rep", stride)
        stride = 2 * stride
    return sums


class Places(NamedTuple):
    digits: list
    first: list
    second: list
    odd: jax.Array


def places():
    rep = lax.axis_index("rep")
    digits = [(rep & (RADIX - 1)) ^ k for k in range(RADIX)]
    second = 9 - FIRST_TAPS
    return Places(
        digits,
        [FIRST_TAPS * digit for digit in digits],
        [RADIX * FIRST_TAPS + second * digit for digit in digits],
        parity(rep) == 1,
    )


def piece_of(pieces, index):
    sizes = (1,) + pieces.shape[1:]
    return lax.dynamic_slice(pieces, (index, 0, 0), sizes, allow_negative_indices=False)[0]


def scatter_pieces(own, met, found):
    chan = own.shape[2]
    parts = [part.reshape(RADIX, -1, chan) for part in [own] + met]

    def piece(k):
        total = piece_of(parts[0], found.digits[k])
        for part in parts[1:]:
            total = total + piece_of(part, found.digits[k])
        return total

    return piece(0), [piece(k).astype(BF16) for k in FAR_FIRST]


def added(own, met):
    return (own + met[2].astype(F32)) + (met[1].astype(F32) + met[0].astype(F32))


def fours(pieces, stride):
    return [swap(piece, "rep", k * stride) for k, piece in zip(FAR_FIRST, pieces)]


def swap_high(array, even, odd):
    count, sp_count = lax.axis_size("rep"), lax.axis_size("sp")
    pairs = []
    for rep in range(count):
        for sp in range(sp_count):
            stride = odd if (sp ^ parity(rep)) & 1 else even
            pairs.append((rep * sp_count + sp, (rep ^ stride) * sp_count + (sp ^ 1)))
    return lax.ppermute(array, ("rep", "sp"), pairs)


def bring(array, k):
    count, sp_count = lax.axis_size("rep"), lax.axis_size("sp")
    pairs = [
        (rep * sp_count + sp, (rep ^ k) * sp_count + (sp ^ parity(rep)))
        for rep in range(count)
        for sp in range(sp_count)
    ]
    return lax.ppermute(array, ("rep", "sp"), pairs)


def both(own, met):
    return (own.astype(F32) + met.astype(F32)).astype(BF16)


def every_share(total):
    stride = GROUP
    while stride < lax.axis_size("rep"):
        total = added(total.astype(F32), fours([total] * 3, stride)).astype(BF16)
        stride = RADIX * stride
    return total


def gather(total, found):
    beside = swap(total, "sp", 1)
    return [bring(total, k) for k in FAR_FIRST] + [jnp.where(found.odd, beside, total)], beside


def put_pieces(whole, pieces, starts):
    for k, piece in zip(FAR_FIRST + (0,), pieces):
        piece = piece.reshape((-1,) + whole.shape[1:]).astype(F32)
        whole = lax.dynamic_update_slice(whole, piece, (starts[k], 0, 0), allow_negative_indices=False)
    return whole


def local(level_four, level_six, conv_weight, bn_gain, bn_shift, cotan_four, cotan_six):
    sp_count = lax.axis_size("sp")
    images = level_four.shape[0]
    four, six, cot_four, cot_six = (a[0] for a in (level_four, level_six, cotan_four, cotan_six))
    rows_four, cols_four, chan = four.shape
    rows_six, cols_six = six.shape[:2]
    pitch_four, pitch_six = pitch_of(cols_four), pitch_of(cols_six)
    counts = (
        float(images * GROUP * rows_four * sp_count * cols_four),
        float(images * GROUP * rows_six * sp_count * cols_six),
    )
    found, four = lax.optimization_barrier((places(), four))
    above, below = edges(four, six, cot_four, cot_six)
    vmem = pl.BlockSpec(memory_space=pltpu.VMEM)
    hbm = pl.BlockSpec(memory_space=pltpu.HBM)
    params = pltpu.CompilerParams(vmem_limit_bytes=VMEM_LIMIT)
    framed_four = jax.ShapeDtypeStruct((rows_four + 2, pitch_four, chan), BF16)
    framed_six = jax.ShapeDtypeStruct((rows_six + 2, pitch_six, chan), BF16)
    four_sums = jax.ShapeDtypeStruct((4, chan), F32)
    flops = 2 * 9 * chan * chan * (rows_four * cols_four + rows_six * cols_six)

    def cost(share, size):
        return pl.CostEstimate(flops=int(flops * share), bytes_accessed=size, transcendentals=0)

    inner_four, inner_six, inner_moments = pl.pallas_call(
        inner_kernel,
        out_shape=(
            jax.ShapeDtypeStruct((rows_four - 2, pitch_four, chan), BF16),
            jax.ShapeDtypeStruct((rows_six - 2, pitch_six, chan), BF16),
            four_sums,
        ),
        in_specs=[vmem] * 3,
        out_specs=(vmem, vmem, vmem),
        scratch_shapes=[
            pltpu.VMEM((rows_four, pitch_four, 3 * chan), BF16),
            pltpu.VMEM((rows_six, pitch_six, 3 * chan), BF16),
        ],
        compiler_params=params,
        cost_estimate=cost(1, 4 * four.size),
        name="forward_inner",
    )(four, six, conv_weight)
    outer_four, outer_six, moments = pl.pallas_call(
        functools.partial(outer_kernel, sp_count),
        out_shape=(
            jax.ShapeDtypeStruct((4, pitch_four, chan), BF16),
            jax.ShapeDtypeStruct((4, pitch_six, chan), BF16),
            four_sums,
        ),
        in_specs=[vmem] * 6,
        out_specs=(vmem, vmem, vmem),
        scratch_shapes=[
            pltpu.VMEM((8, pitch_four, 3 * chan), BF16),
            pltpu.VMEM((8, pitch_six, 3 * chan), BF16),
        ],
        compiler_params=params,
        cost_estimate=cost(0.1, four.size),
        name="forward_outer",
    )(four, six, above, below, conv_weight, inner_moments)
    moments, four, six = lax.optimization_barrier((moments, four, six))
    turned, turned_weight = pl.pallas_call(
        turn_kernel,
        out_shape=(
            jax.ShapeDtypeStruct((chan, rows_four * cols_four + rows_six * pitch_six), BF16),
            jax.ShapeDtypeStruct((9 * chan, chan), BF16),
        ),
        in_specs=[vmem] * 3,
        out_specs=(vmem, vmem),
        compiler_params=params,
        cost_estimate=cost(0.3, 4 * four.size),
        name="turn",
    )(four, six, conv_weight)
    moments, turned, turned_weight = lax.optimization_barrier((group_sum(moments), turned, turned_weight))

    slope_four, slope_six, slopes = pl.pallas_call(
        functools.partial(slope_kernel, counts),
        out_shape=(
            jax.ShapeDtypeStruct(framed_four.shape, F32),
            jax.ShapeDtypeStruct(framed_six.shape, F32),
            four_sums,
        ),
        in_specs=[vmem] * 11,
        out_specs=(vmem,) * 3,
        compiler_params=params,
        cost_estimate=cost(0.01, 4 * four.size),
        name="slopes",
    )(
        inner_four, inner_six, outer_four, outer_six, cot_four, cot_six, above, below, moments, bn_gain, bn_shift
    )
    slopes = group_sum(slopes)

    share = chan // sp_count
    wide_four, wide_six = (
        jax.ShapeDtypeStruct(framed.shape[:2] + (3 * chan,), BF16) for framed in (framed_four, framed_six)
    )
    def shares(taps):
        return (
            jax.ShapeDtypeStruct((taps, share, chan), F32),
            jax.ShapeDtypeStruct((sp_count - 1, taps, share, chan), F32),
        )

    three_four, three_six, own_a, sent_a, rest, grad_gain, grad_shift = pl.pallas_call(
        functools.partial(backward_kernel, counts, sp_count, (cols_four, cols_six)),
        out_shape=(wide_four, wide_six)
        + shares(FIRST_TAPS)
        + (jax.ShapeDtypeStruct((chan, (EARLY_TAPS - FIRST_TAPS) * chan), F32),)
        + (jax.ShapeDtypeStruct((2, chan), F32),) * 2,
        in_specs=[vmem] * 11,
        out_specs=(vmem,) * 7,
        scratch_shapes=[pltpu.VMEM((chan, EARLY_TAPS * chan), F32)],
        compiler_params=params,
        cost_estimate=cost(0.6, 8 * four.size),
        name="backward",
    )(
        turned, inner_four, inner_six, outer_four, outer_six, slope_four, slope_six, moments, slopes,
        bn_gain, bn_shift,
    )
    sent_a, three_six = lax.optimization_barrier((sent_a, three_six))
    met_a = [swap(sent_a[step], "sp", step + 1) for step in range(sp_count - 1)]
    own_b, sent_b = pl.pallas_call(
        functools.partial(weight_kernel, sp_count),
        out_shape=shares(9 - FIRST_TAPS),
        in_specs=[vmem] * 4,
        out_specs=(vmem, vmem),
        scratch_shapes=[pltpu.VMEM((chan, (9 - EARLY_TAPS) * chan), F32)],
        compiler_params=params,
        cost_estimate=cost(0.6, 8 * four.size),
        name="weights",
    )(turned, three_four, three_six, rest)
    met_a, sent_b = lax.optimization_barrier((met_a, sent_b))
    met_b = [swap(sent_b[step], "sp", step + 1) for step in range(sp_count - 1)]

    chunks = chunks_of(rows_four, 8)
    cuts = [part * len(chunks) // 3 for part in range(4)]
    groups = [chunks[low:high] for low, high in zip(cuts[:-1], cuts[1:]) if low < high]
    bounds = [group[0][0] for group in groups]

    def inputs(group, three):
        return pl.pallas_call(
            functools.partial(input_kernel, group),
            out_shape=jax.ShapeDtypeStruct((group[-1][1] - group[0][0], cols_four, chan), BF16),
            in_specs=[vmem] * 2,
            out_specs=vmem,
            compiler_params=params,
            cost_estimate=cost(0.3, four.size),
            name="inputs",
        )(three, turned_weight)

    grad_gain, grad_shift = every_group(grad_gain), every_group(grad_shift)

    piece_a, pieces_a = scatter_pieces(own_a, met_a, found)
    met_a = fours(pieces_a, 1)
    piece_b, pieces_b = scatter_pieces(own_b, met_b, found)
    met_b = fours(pieces_b, 1)
    met_a, unused = lax.optimization_barrier((met_a, pieces_b))

    piece_a = added(piece_a, met_a).astype(BF16)
    piece_a, three_four = lax.optimization_barrier((piece_a, three_four))
    met_a = swap_high(piece_a, RADIX, 2 * RADIX)
    earlier = [inputs(groups[0], three_four)] if len(groups) > 1 else []
    met_b, earlier = lax.optimization_barrier((met_b, earlier))

    piece_b = added(piece_b, met_b).astype(BF16)
    met_b = swap_high(piece_b, RADIX, 2 * RADIX)
    met_a, unused = lax.optimization_barrier((met_a, piece_b))

    piece_a = both(piece_a, met_a)
    piece_a, three_four = lax.optimization_barrier((piece_a, three_four))
    met_a = swap_high(piece_a, 2 * RADIX, RADIX)
    if len(groups) > 2:
        earlier = earlier + [inputs(groups[1], three_four)]
    met_b, earlier = lax.optimization_barrier((met_b, earlier))

    piece_b = both(piece_b, met_b)
    met_b = swap_high(piece_b, 2 * RADIX, RADIX)
    met_a, unused = lax.optimization_barrier((met_a, piece_b))

    piece_a = every_share(both(piece_a, met_a))
    pieces_a, unused = gather(piece_a, found)
    piece_b = every_share(both(piece_b, met_b))
    pieces_b, beside = gather(piece_b, found)
    unused, three_four = lax.optimization_barrier(((beside, pieces_a[0]), three_four))
    done = bounds[-1]
    grad_four, grad_six = pl.pallas_call(
        functools.partial(input_last_kernel, groups[-1], bounds),
        out_shape=(
            jax.ShapeDtypeStruct(four.shape, BF16),
            jax.ShapeDtypeStruct(six.shape, BF16),
        ),
        in_specs=[vmem] * (3 + len(earlier)),
        out_specs=(hbm, hbm),
        scratch_shapes=[
            pltpu.VMEM((rows_four - done, cols_four, chan), BF16),
            pltpu.VMEM(six.shape, BF16),
            pltpu.SemaphoreType.DMA((len(groups),)),
            pltpu.SemaphoreType.DMA((len(chunks),)),
            pltpu.SemaphoreType.DMA((len(chunks_of(rows_six, 12)),)),
        ],
        compiler_params=params,
        cost_estimate=cost(0.4, 2 * four.size),
        name="inputs_last",
    )(three_four, three_six, turned_weight, *earlier)
    pieces_a, grad_six = lax.optimization_barrier((pieces_a, grad_six))
    whole = jnp.zeros((9 * RADIX, share // RADIX, chan), F32)
    whole = put_pieces(whole, pieces_a, found.first)
    whole = put_pieces(whole, pieces_b, found.second)
    grad_weight = whole.reshape(9, share, chan)
    return (grad_four[None], grad_six[None], grad_weight, grad_gain, grad_shift)


def solution(mesh):
    placed = (
        P("rep", "sp", None, None),
        P("rep", "sp", None, None),
        P(),
        P(),
        P(),
        P("rep", "sp", None, None),
        P("rep", "sp", None, None),
    )
    return jax.shard_map(
        local,
        mesh=mesh,
        in_specs=placed,
        out_specs=(
            P("rep", "sp", None, None),
            P("rep", "sp", None, None),
            P(None, "sp", None),
            P(),
            P(),
        ),
        check_vma=False,
    )
```

profile of v0, /device:TPU:0, one launch (start us, length us, event | category | flops | bytes accessed | tf_op | source)
XLA Modules:
  0.0 80.6 jit_solution(525290212357403841)
XLA Ops:
  0.7 1.7 %edges.1 = bf16[384,256]{1,0:T(8,128)(2,1)} custom-call(bf16[48,96,256]{2,1,0:T(8,128)(2,1)} %bitcast.51, bf16[12,24,256]{2,1,0:T(8,128)(2,1)} %bitcast.59, bf16[48,96,256]{2,1,0:T(8,128)(2,1)} %bitcast.55, bf16[12,24,256]{2,1,0:T(8,128)(2,1)} %bitcast.63), custom_call_target="tpu_custom_call" | custom-call | tf_op jit(solution)/shard_map/edges/pallas_call | solution.py:458
  2.4 0.5 collective-permute-start
  3.0 5.8 %forward_inner.1 = (bf16[46,96,256]{2,1,0:T(8,128)(2,1)S(1)}, bf16[10,32,256]{2,1,0:T(8,128)(2,1)S(1)}, f32[4,256]{1,0:T(4,128)S(1)}) custom-call(bf16[48,96,256]{2,1,0:T(8,128)(2,1)S(1)} %bitcast.52, bf16[12,24,256]{2,1,0:T(8,128)(2,1)S(1)} %bitcast.60, bf16[9,256,256]{2,1,0:T(8,128)(2,1)S(1)} %copy-done.2), custom_call_target="tpu_custom_call" | custom-call | flops 5775556608 | bytes 4718592 | tf_op jit(solution)/shard_map/forward_inner/pallas_call | solution.py:624
  8.8 0.8 forward_outer.1
  9.6 0.4 collective-permute-start.1
  10.0 0.9 %collective-permute-done.1 = f32[4,256]{1,0:T(4,128)S(1)} collective-permute-done((f32[4,256]{1,0:T(4,128)S(1)}, f32[4,256]{1,0:T(4,128)S(1)}, u32[]{:S(2)}, u32[]{:S(2)}) %collective-permute-start.1) | collective-permute-done | bytes 4128 | tf_op jit(solution)/shard_map/ppermute | solution.py:416
  10.8 3.6 %collective-permute-start.2 = (f32[4,256]{1,0:T(4,128)S(1)}, f32[4,256]{1,0:T(4,128)S(1)}, u32[]{:S(2)}, u32[]{:S(2)}) collective-permute-start(f32[4,256]{1,0:T(4,128)S(1)} %add.124), channel_id=1, source_target_pairs={{0,7},{1,6},{2,5},{3,4},{4,3},{5,2},{6,1},{7,0},{8,15},{9,14},{10,... | collective-permute-start | bytes 12296 | tf_op jit(solution)/shard_map/ppermute | solution.py:486
  14.4 0.4 collective-permute-start.3
  14.8 0.1 collective-permute-start.4
  14.9 0.9 %collective-permute-done.2 = f32[4,256]{1,0:T(4,128)S(1)} collective-permute-done((f32[4,256]{1,0:T(4,128)S(1)}, f32[4,256]{1,0:T(4,128)S(1)}, u32[]{:S(2)}, u32[]{:S(2)}) %collective-permute-start.2) | collective-permute-done | bytes 4128 | tf_op jit(solution)/shard_map/ppermute | solution.py:486
  15.7 1.7 %collective-permute-done.3 = f32[4,256]{1,0:T(4,128)S(1)} collective-permute-done((f32[4,256]{1,0:T(4,128)S(1)}, f32[4,256]{1,0:T(4,128)S(1)}, u32[]{:S(2)}, u32[]{:S(2)}) %collective-permute-start.3) | collective-permute-done | bytes 4128 | tf_op jit(solution)/shard_map/ppermute | solution.py:486
  17.4 0.4 collective-permute-done.4
  17.9 3.5 %collective-permute-start.5 = (f32[4,256]{1,0:T(4,128)S(1)}, f32[4,256]{1,0:T(4,128)S(1)}, u32[]{:S(2)}, u32[]{:S(2)}) collective-permute-start(f32[4,256]{1,0:T(4,128)S(1)} %add_add_fusion.3), channel_id=1, source_target_pairs={{0,25},{1,24},{2,27},{3,26},{4,29},{5,28},{6,31},{7,30},{8,17},{9,... | collective-permute-start | bytes 12296 | tf_op jit(solution)/shard_map/ppermute | solution.py:486
  21.4 0.6 collective-permute-start.7
  21.9 1.0 %turn.1 = (bf16[256,4992]{1,0:T(8,128)(2,1)S(1)}, bf16[2304,256]{1,0:T(8,128)(2,1)S(1)}) custom-call(bf16[48,96,256]{2,1,0:T(8,128)(2,1)S(1)} %bitcast.54, bf16[12,24,256]{2,1,0:T(8,128)(2,1)S(1)} %bitcast.62, bf16[9,256,256]{2,1,0:T(8,128)(2,1)S(1)} %copy-done.2), custom_call_target="tpu_custom_call" | custom-call | flops 1732667008 | bytes 4718592 | tf_op jit(solution)/shard_map/turn/pallas_call | solution.py:659
  22.9 2.3 %collective-permute-done.6 = f32[4,256]{1,0:T(4,128)S(1)} collective-permute-done((f32[4,256]{1,0:T(4,128)S(1)}, f32[4,256]{1,0:T(4,128)S(1)}, u32[]{:S(2)}, u32[]{:S(2)}) %collective-permute-start.6) | collective-permute-done | bytes 4128 | tf_op jit(solution)/shard_map/ppermute | solution.py:486
  25.3 2.6 %slopes.1 = (f32[50,96,256]{2,1,0:T(8,128)S(1)}, f32[14,32,256]{2,1,0:T(8,128)S(1)}, f32[4,256]{1,0:T(4,128)S(1)}) custom-call(bf16[46,96,256]{2,1,0:T(8,128)(2,1)S(1)} %get-tuple-element.100.inner_four_ref, bf16[10,32,256]{2,1,0:T(8,128)(2,1)S(1)} %get-tuple-element.101.inner_six_ref, bf16[4,96,256]{2,1,0:T(8,128)(2,1)S(1)} %get-tuple-element.102.outer_four_ref, ...), custom_call_target="tpu_custom_call" | custom-call | flops 57755568 | bytes 4718592 | tf_op jit(solution)/shard_map/slopes/pallas_call | solution.py:673
  28.0 0.4 collective-permute-start.8
  28.3 0.9 %collective-permute-done.8 = f32[4,256]{1,0:T(4,128)S(1)} collective-permute-done((f32[4,256]{1,0:T(4,128)S(1)}, f32[4,256]{1,0:T(4,128)S(1)}, u32[]{:S(2)}, u32[]{:S(2)}) %collective-permute-start.8) | collective-permute-done | bytes 4128 | tf_op jit(solution)/shard_map/ppermute | solution.py:416
  29.2 1.4 %collective-permute-start.10 = (f32[4,256]{1,0:T(4,128)S(1)}, f32[4,256]{1,0:T(4,128)S(1)}, u32[]{:S(2)}, u32[]{:S(2)}) collective-permute-start(f32[4,256]{1,0:T(4,128)S(1)} %add.131), channel_id=1, source_target_pairs={{0,5},{1,4},{2,7},{3,6},{4,1},{5,0},{6,3},{7,2},{8,13},{9,12},{10,... | collective-permute-start | bytes 12296 | tf_op jit(solution)/shard_map/ppermute | solution.py:486
  30.6 0.3 collective-permute-start.11
  31.0 1.3 %collective-permute-start.9 = (f32[4,256]{1,0:T(4,128)S(1)}, f32[4,256]{1,0:T(4,128)S(1)}, u32[]{:S(2)}, u32[]{:S(2)}) collective-permute-start(f32[4,256]{1,0:T(4,128)S(1)} %add.131), channel_id=1, source_target_pairs={{0,7},{1,6},{2,5},{3,4},{4,3},{5,2},{6,1},{7,0},{8,15},{9,14},{10,... | collective-permute-start | bytes 12296 | tf_op jit(solution)/shard_map/ppermute | solution.py:486
  32.3 1.3 %collective-permute-done.11 = f32[4,256]{1,0:T(4,128)S(1)} collective-permute-done((f32[4,256]{1,0:T(4,128)S(1)}, f32[4,256]{1,0:T(4,128)S(1)}, u32[]{:S(2)}, u32[]{:S(2)}) %collective-permute-start.11) | collective-permute-done | bytes 4128 | tf_op jit(solution)/shard_map/ppermute | solution.py:486
  33.7 1.2 %collective-permute-done.9 = f32[4,256]{1,0:T(4,128)S(1)} collective-permute-done((f32[4,256]{1,0:T(4,128)S(1)}, f32[4,256]{1,0:T(4,128)S(1)}, u32[]{:S(2)}, u32[]{:S(2)}) %collective-permute-start.9) | collective-permute-done | bytes 4128 | tf_op jit(solution)/shard_map/ppermute | solution.py:486
  34.9 1.7 %collective-permute-start.12 = (f32[4,256]{1,0:T(4,128)S(1)}, f32[4,256]{1,0:T(4,128)S(1)}, u32[]{:S(2)}, u32[]{:S(2)}) collective-permute-start(f32[4,256]{1,0:T(4,128)S(1)} %add_add_fusion.1), channel_id=1, source_target_pairs={{0,25},{1,24},{2,27},{3,26},{4,29},{5,28},{6,31},{7,30},{8,17},{9,... | collective-permute-start | bytes 12296 | tf_op jit(solution)/shard_map/ppermute | solution.py:486
  36.6 0.1 collective-permute-start.13
  36.7 2.2 %collective-permute-start.14 = (f32[4,256]{1,0:T(4,128)S(1)}, f32[4,256]{1,0:T(4,128)S(1)}, u32[]{:S(2)}, u32[]{:S(2)}) collective-permute-start(f32[4,256]{1,0:T(4,128)S(1)} %add_add_fusion.1), channel_id=1, source_target_pairs={{0,9},{1,8},{2,11},{3,10},{4,13},{5,12},{6,15},{7,14},{8,1},{9,0},... | collective-permute-start | bytes 12296 | tf_op jit(solution)/shard_map/ppermute | solution.py:486
  38.9 0.8 %collective-permute-done.12 = f32[4,256]{1,0:T(4,128)S(1)} collective-permute-done((f32[4,256]{1,0:T(4,128)S(1)}, f32[4,256]{1,0:T(4,128)S(1)}, u32[]{:S(2)}, u32[]{:S(2)}) %collective-permute-start.12) | collective-permute-done | bytes 4128 | tf_op jit(solution)/shard_map/ppermute | solution.py:486
  39.8 0.8 %collective-permute-done.13 = f32[4,256]{1,0:T(4,128)S(1)} collective-permute-done((f32[4,256]{1,0:T(4,128)S(1)}, f32[4,256]{1,0:T(4,128)S(1)}, u32[]{:S(2)}, u32[]{:S(2)}) %collective-permute-start.13) | collective-permute-done | bytes 4128 | tf_op jit(solution)/shard_map/ppermute | solution.py:486
  40.6 5.7 %backward.1 = (bf16[50,96,768]{2,1,0:T(8,128)(2,1)S(1)}, bf16[14,32,768]{2,1,0:T(8,128)(2,1)S(1)}, f32[4,128,256]{2,1,0:T(8,128)S(1)}, f32[1,4,128,256]{3,2,1,0:...) custom-call(bf16[256,4992]{1,0:T(8,128)(2,1)S(1)} %get-tuple-element.99.turned_ref, ...), custom_call_target="tpu_custom_call" | custom-call | flops 3465334016 | bytes 9437184 | tf_op jit(solution)/shard_map/backward/pallas_call | solution.py:700
  46.3 0.2 collective-permute-start.15
  46.5 2.3 %weights.1 = (f32[5,128,256]{2,1,0:T(8,128)S(1)}, f32[1,5,128,256]{3,2,1,0:T(8,128)S(1)}) custom-call(bf16[256,4992]{1,0:T(8,128)(2,1)S(1)} %get-tuple-element.99.turned_ref, bf16[50,96,768]{2,1,0:T(8,128)(2,1)S(1)} %get-tuple-element.144.three_four, bf16[14,32,768]{2,1,0:T(8,128)(2,1)S(1)} %get-tuple-element.117.three_six, ...), custom_call_target="tpu_custom_call" | custom-call | flops 3465334016 | bytes 9437184 | tf_op jit(solution)/shard_map/weights/pallas_call | solution.py:718
  48.7 0.4 collective-permute-start.16
  49.1 0.1 fusion.9
  49.2 1.5 %collective-permute-start.20 = (bf16[128,256]{1,0:T(8,128)(2,1)S(1)}, bf16[128,256]{1,0:T(8,128)(2,1)S(1)}, u32[]{:S(2)}, u32[]{:S(2)}) collective-permute-start(bf16[128,256]{1,0:T(8,128)(2,1)S(1)} %get-tuple-element.170), channel_id=1, source_target_pairs={{0,6},{2,4},{4,2},{6,0},{8,14},{10,12},{12,10},{14,8},{16,22},{18,... | collective-permute-start | bytes 196616 | tf_op jit(solution)/shard_map/ppermute | solution.py:416
  50.7 1.5 %collective-permute-start.21 = (bf16[128,256]{1,0:T(8,128)(2,1)S(1)}, bf16[128,256]{1,0:T(8,128)(2,1)S(1)}, u32[]{:S(2)}, u32[]{:S(2)}) collective-permute-start(bf16[128,256]{1,0:T(8,128)(2,1)S(1)} %get-tuple-element.169), channel_id=1, source_target_pairs={{0,4},{2,6},{4,0},{6,2},{8,12},{10,14},{12,8},{14,10},{16,20},{18,... | collective-permute-start | bytes 196616 | tf_op jit(solution)/shard_map/ppermute | solution.py:416
  52.2 0.5 collective-permute-start.22
  52.7 0.1 fusion.6
  52.8 1.5 %collective-permute-start.17 = (bf16[160,256]{1,0:T(8,128)(2,1)S(1)}, bf16[160,256]{1,0:T(8,128)(2,1)S(1)}, u32[]{:S(2)}, u32[]{:S(2)}) collective-permute-start(bf16[160,256]{1,0:T(8,128)(2,1)S(1)} %get-tuple-element.167), channel_id=1, source_target_pairs={{0,6},{2,4},{4,2},{6,0},{8,14},{10,12},{12,10},{14,8},{16,22},{18,... | collective-permute-start | bytes 245768 | tf_op jit(solution)/shard_map/ppermute | solution.py:416
  54.3 1.5 %collective-permute-start.18 = (bf16[160,256]{1,0:T(8,128)(2,1)S(1)}, bf16[160,256]{1,0:T(8,128)(2,1)S(1)}, u32[]{:S(2)}, u32[]{:S(2)}) collective-permute-start(bf16[160,256]{1,0:T(8,128)(2,1)S(1)} %get-tuple-element.166), channel_id=1, source_target_pairs={{0,4},{2,6},{4,0},{6,2},{8,12},{10,14},{12,8},{14,10},{16,20},{18,... | collective-permute-start | bytes 245768 | tf_op jit(solution)/shard_map/ppermute | solution.py:416
  55.8 0.7 collective-permute-start.19
  56.5 0.2 collective-permute-done.22
  56.8 0.3 collective-permute-start.24
  57.1 2.0 %inputs.2.rest_0_ = bf16[16,96,256]{2,1,0:T(8,128)(2,1)S(1)} custom-call(bf16[50,96,768]{2,1,0:T(8,128)(2,1)S(1)} %get-tuple-element.144.three_four, bf16[2304,256]{1,0:T(8,128)(2,1)S(1)} %get-tuple-element.133.turned), custom_call_target="tpu_custom_call" | custom-call | flops 1732667008 | bytes 1179648 | tf_op jit(solution)/shard_map/inputs/pallas_call | solution.py:737
  59.1 0.3 collective-permute-done.18
  59.4 0.9 %collective-permute-done.19 = bf16[160,256]{1,0:T(8,128)(2,1)S(1)} collective-permute-done((bf16[160,256]{1,0:T(8,128)(2,1)S(1)}, bf16[160,256]{1,0:T(8,128)(2,1)S(1)}, u32[]{:S(2)}, u32[]{:S(2)}) %collective-permute-start.19) | collective-permute-done | bytes 81952 | tf_op jit(solution)/shard_map/ppermute | solution.py:416
  60.3 0.4 collective-permute-start.23
  60.7 0.5 collective-permute-done.24
  61.2 1.6 %collective-permute-start.27 = (bf16[128,256]{1,0:T(8,128)(2,1)S(1)}, bf16[128,256]{1,0:T(8,128)(2,1)S(1)}, u32[]{:S(2)}, u32[]{:S(2)}) collective-permute-start(bf16[128,256]{1,0:T(8,128)(2,1)S(1)} %add_convert_fusion.6), channel_id=1, source_target_pairs={{0,17},{1,8},{2,19},{3,10},{4,21},{5,12},{6,23},{7,14},{8,1},{9,24... | collective-permute-start | bytes 196616 | tf_op jit(solution)/shard_map/ppermute | solution.py:563
  62.8 2.0 %inputs.3.rest_1_ = bf16[16,96,256]{2,1,0:T(8,128)(2,1)S(1)} custom-call(bf16[50,96,768]{2,1,0:T(8,128)(2,1)S(1)} %get-tuple-element.144.three_four, bf16[2304,256]{1,0:T(8,128)(2,1)S(1)} %get-tuple-element.133.turned), custom_call_target="tpu_custom_call" | custom-call | flops 1732667008 | bytes 1179648 | tf_op jit(solution)/shard_map/inputs/pallas_call | solution.py:737
  64.8 1.2 %collective-permute-start.25 = (bf16[160,256]{1,0:T(8,128)(2,1)S(1)}, bf16[160,256]{1,0:T(8,128)(2,1)S(1)}, u32[]{:S(2)}, u32[]{:S(2)}) collective-permute-start(bf16[160,256]{1,0:T(8,128)(2,1)S(1)} %add_convert_fusion.1), channel_id=1, source_target_pairs={{0,17},{1,8},{2,19},{3,10},{4,21},{5,12},{6,23},{7,14},{8,1},{9,24... | collective-permute-start | bytes 245768 | tf_op jit(solution)/shard_map/ppermute | solution.py:563
  66.0 2.1 %collective-permute-done.27 = bf16[128,256]{1,0:T(8,128)(2,1)S(1)} collective-permute-done((bf16[128,256]{1,0:T(8,128)(2,1)S(1)}, bf16[128,256]{1,0:T(8,128)(2,1)S(1)}, u32[]{:S(2)}, u32[]{:S(2)}) %collective-permute-start.27) | collective-permute-done | bytes 65568 | tf_op jit(solution)/shard_map/ppermute | solution.py:563
  68.2 0.3 collective-permute-start.31
  68.5 0.9 %collective-permute-start.28 = (bf16[128,256]{1,0:T(8,128)(2,1)S(1)}, bf16[128,256]{1,0:T(8,128)(2,1)S(1)}, u32[]{:S(2)}, u32[]{:S(2)}) collective-permute-start(bf16[128,256]{1,0:T(8,128)(2,1)S(1)} %add_convert_fusion.5), channel_id=1, source_target_pairs={{0,6},{1,7},{2,4},{3,5},{4,2},{5,3},{6,0},{7,1},{8,15},{9,14},{10,... | collective-permute-start | bytes 196616 | tf_op jit(solution)/shard_map/ppermute | solution.py:573
  69.4 1.5 %collective-permute-start.29 = (bf16[128,256]{1,0:T(8,128)(2,1)S(1)}, bf16[128,256]{1,0:T(8,128)(2,1)S(1)}, u32[]{:S(2)}, u32[]{:S(2)}) collective-permute-start(bf16[128,256]{1,0:T(8,128)(2,1)S(1)} %add_convert_fusion.5), channel_id=1, source_target_pairs={{0,4},{1,5},{2,6},{3,7},{4,0},{5,1},{6,2},{7,3},{8,13},{9,12},{10,... | collective-permute-start | bytes 196616 | tf_op jit(solution)/shard_map/ppermute | solution.py:573
  70.9 1.1 %collective-permute-start.30 = (bf16[128,256]{1,0:T(8,128)(2,1)S(1)}, bf16[128,256]{1,0:T(8,128)(2,1)S(1)}, u32[]{:S(2)}, u32[]{:S(2)}) collective-permute-start(bf16[128,256]{1,0:T(8,128)(2,1)S(1)} %add_convert_fusion.5), channel_id=1, source_target_pairs={{0,2},{1,3},{2,0},{3,1},{4,6},{5,7},{6,4},{7,5},{8,11},{9,10},{10,... | collective-permute-start | bytes 196616 | tf_op jit(solution)/shard_map/ppermute | solution.py:573
  72.0 0.3 collective-permute-start.26
  72.4 0.9 %collective-permute-start.32 = (bf16[160,256]{1,0:T(8,128)(2,1)S(1)}, bf16[160,256]{1,0:T(8,128)(2,1)S(1)}, u32[]{:S(2)}, u32[]{:S(2)}) collective-permute-start(bf16[160,256]{1,0:T(8,128)(2,1)S(1)} %add_convert_fusion), channel_id=1, source_target_pairs={{0,6},{1,7},{2,4},{3,5},{4,2},{5,3},{6,0},{7,1},{8,15},{9,14},{10,... | collective-permute-start | bytes 245768 | tf_op jit(solution)/shard_map/ppermute | solution.py:573
  73.3 0.9 %collective-permute-done.28 = bf16[128,256]{1,0:T(8,128)(2,1)S(1)} collective-permute-done((bf16[128,256]{1,0:T(8,128)(2,1)S(1)}, bf16[128,256]{1,0:T(8,128)(2,1)S(1)}, u32[]{:S(2)}, u32[]{:S(2)}) %collective-permute-start.28) | collective-permute-done | bytes 65568 | tf_op jit(solution)/shard_map/ppermute | solution.py:573
  74.2 0.6 collective-permute-start.33
  74.8 1.1 %collective-permute-start.34 = (bf16[160,256]{1,0:T(8,128)(2,1)S(1)}, bf16[160,256]{1,0:T(8,128)(2,1)S(1)}, u32[]{:S(2)}, u32[]{:S(2)}) collective-permute-start(bf16[160,256]{1,0:T(8,128)(2,1)S(1)} %add_convert_fusion), channel_id=1, source_target_pairs={{0,2},{1,3},{2,0},{3,1},{4,6},{5,7},{6,4},{7,5},{8,11},{9,10},{10,... | collective-permute-start | bytes 245768 | tf_op jit(solution)/shard_map/ppermute | solution.py:573
  75.9 3.3 %inputs_last.1 = (bf16[48,96,256]{2,1,0:T(8,128)(2,1)}, bf16[12,24,256]{2,1,0:T(8,128)(2,1)}) custom-call(bf16[50,96,768]{2,1,0:T(8,128)(2,1)S(1)} %get-tuple-element.144.three_four, bf16[14,32,768]{2,1,0:T(8,128)(2,1)S(1)} %get-tuple-element.117.three_six, bf16[2304,256]{1,0:T(8,128)(2,1)S(1)} %get-tuple-element.133.turned, ...), custom_call_target="tpu_custom_call" | custom-call | flops 2310222592 | bytes 2359296 | tf_op jit(solution)/shard_map/inputs_last/pallas_call | solution.py:782
  79.2 0.1 broadcast_in_dim.11
  79.6 1.0 %copy-done.7 = f32[36,32,256]{2,1,0:T(8,128)} copy-done((f32[36,32,256]{2,1,0:T(8,128)}, f32[36,32,256]{2,1,0:T(8,128)S(1)}, u32[]{:S(2)}) %copy-start.7) | copy-done | bytes 1179672
  (57 shorter events, 0.4 us)
Async XLA Ops:
  0.7 2.3 %copy-start = (bf16[1,48,96,256]{3,2,1,0:T(8,128)(2,1)S(1)}, bf16[1,48,96,256]{3,2,1,0:T(8,128)(2,1)}, u32[]{:S(2)}) copy-start(bf16[1,48,96,256]{3,2,1,0:T(8,128)(2,1)} %param.7) | copy-start | bytes 7077892
  0.7 2.3 %copy-start.2 = (bf16[9,256,256]{2,1,0:T(8,128)(2,1)S(1)}, bf16[9,256,256]{2,1,0:T(8,128)(2,1)}, u32[]{:S(2)}) copy-start(bf16[9,256,256]{2,1,0:T(8,128)(2,1)} %w_ref.5) | copy-start | bytes 3538948
  0.7 2.3 %copy-start.3 = (bf16[1,12,24,256]{3,2,1,0:T(8,128)(2,1)S(1)}, bf16[1,12,24,256]{3,2,1,0:T(8,128)(2,1)}, u32[]{:S(2)}) copy-start(bf16[1,12,24,256]{3,2,1,0:T(8,128)(2,1)} %param.8) | copy-start | bytes 442372
  2.4 6.4 %collective-permute-start = (bf16[384,256]{1,0:T(8,128)(2,1)}, bf16[384,256]{1,0:T(8,128)(2,1)S(1)}, u32[]{:S(2)}, u32[]{:S(2)}) collective-permute-start(bf16[384,256]{1,0:T(8,128)(2,1)} %edges.1), channel_id=1, source_target_pairs={{0,1},{1,0},{2,3},{3,2},{4,5},{5,4},{6,7},{7,6},{8,9},{9,8},{10,11... | collective-permute-start | bytes 589832 | tf_op jit(solution)/shard_map/ppermute | solution.py:416
  9.6 1.2 %collective-permute-start.1 = (f32[4,256]{1,0:T(4,128)S(1)}, f32[4,256]{1,0:T(4,128)S(1)}, u32[]{:S(2)}, u32[]{:S(2)}) collective-permute-start(f32[4,256]{1,0:T(4,128)S(1)} %get-tuple-element.88), channel_id=1, source_target_pairs={{0,1},{1,0},{2,3},{3,2},{4,5},{5,4},{6,7},{7,6},{8,9},{9,8},{10,11... | collective-permute-start | bytes 12296 | tf_op jit(solution)/shard_map/ppermute | solution.py:416
  10.8 4.9 %collective-permute-start.2 = (f32[4,256]{1,0:T(4,128)S(1)}, f32[4,256]{1,0:T(4,128)S(1)}, u32[]{:S(2)}, u32[]{:S(2)}) collective-permute-start(f32[4,256]{1,0:T(4,128)S(1)} %add.124), channel_id=1, source_target_pairs={{0,7},{1,6},{2,5},{3,4},{4,3},{5,2},{6,1},{7,0},{8,15},{9,14},{10,... | collective-permute-start | bytes 12296 | tf_op jit(solution)/shard_map/ppermute | solution.py:486
  14.4 3.0 %collective-permute-start.3 = (f32[4,256]{1,0:T(4,128)S(1)}, f32[4,256]{1,0:T(4,128)S(1)}, u32[]{:S(2)}, u32[]{:S(2)}) collective-permute-start(f32[4,256]{1,0:T(4,128)S(1)} %add.124), channel_id=1, source_target_pairs={{0,5},{1,4},{2,7},{3,6},{4,1},{5,0},{6,3},{7,2},{8,13},{9,12},{10,... | collective-permute-start | bytes 12296 | tf_op jit(solution)/shard_map/ppermute | solution.py:486
  14.8 3.0 %collective-permute-start.4 = (f32[4,256]{1,0:T(4,128)S(1)}, f32[4,256]{1,0:T(4,128)S(1)}, u32[]{:S(2)}, u32[]{:S(2)}) collective-permute-start(f32[4,256]{1,0:T(4,128)S(1)} %add.124), channel_id=1, source_target_pairs={{0,3},{1,2},{2,1},{3,0},{4,7},{5,6},{6,5},{7,4},{8,11},{9,10},{10,... | collective-permute-start | bytes 12296 | tf_op jit(solution)/shard_map/ppermute | solution.py:486
  17.9 7.4 %copy-start.4 = (bf16[1,12,24,256]{3,2,1,0:T(8,128)(2,1)S(1)}, bf16[1,12,24,256]{3,2,1,0:T(8,128)(2,1)}, u32[]{:S(2)}) copy-start(bf16[1,12,24,256]{3,2,1,0:T(8,128)(2,1)} %param.13) | copy-start | bytes 442372
  17.9 7.5 %copy-start.5 = (f32[2,256]{1,0:T(2,128)S(1)}, f32[2,256]{1,0:T(2,128)}, u32[]{:S(2)}) copy-start(f32[2,256]{1,0:T(2,128)} %gain_ref.3) | copy-start | bytes 6148
  17.9 7.5 %copy-start.6 = (f32[2,256]{1,0:T(2,128)S(1)}, f32[2,256]{1,0:T(2,128)}, u32[]{:S(2)}) copy-start(f32[2,256]{1,0:T(2,128)} %shift_ref.3) | copy-start | bytes 6148
  17.9 5.1 %collective-permute-start.5 = (f32[4,256]{1,0:T(4,128)S(1)}, f32[4,256]{1,0:T(4,128)S(1)}, u32[]{:S(2)}, u32[]{:S(2)}) collective-permute-start(f32[4,256]{1,0:T(4,128)S(1)} %add_add_fusion.3), channel_id=1, source_target_pairs={{0,25},{1,24},{2,27},{3,26},{4,29},{5,28},{6,31},{7,30},{8,17},{9,... | collective-permute-start | bytes 12296 | tf_op jit(solution)/shard_map/ppermute | solution.py:486
  21.4 3.9 %collective-permute-start.6 = (f32[4,256]{1,0:T(4,128)S(1)}, f32[4,256]{1,0:T(4,128)S(1)}, u32[]{:S(2)}, u32[]{:S(2)}) collective-permute-start(f32[4,256]{1,0:T(4,128)S(1)} %add_add_fusion.3), channel_id=1, source_target_pairs={{0,17},{1,16},{2,19},{3,18},{4,21},{5,20},{6,23},{7,22},{8,25},{9,... | collective-permute-start | bytes 12296 | tf_op jit(solution)/shard_map/ppermute | solution.py:486
  21.4 3.9 %collective-permute-start.7 = (f32[4,256]{1,0:T(4,128)S(1)}, f32[4,256]{1,0:T(4,128)S(1)}, u32[]{:S(2)}, u32[]{:S(2)}) collective-permute-start(f32[4,256]{1,0:T(4,128)S(1)} %add_add_fusion.3), channel_id=1, source_target_pairs={{0,9},{1,8},{2,11},{3,10},{4,13},{5,12},{6,15},{7,14},{8,1},{9,0},... | collective-permute-start | bytes 12296 | tf_op jit(solution)/shard_map/ppermute | solution.py:486
  21.9 3.4 %copy-start.1 = (bf16[1,48,96,256]{3,2,1,0:T(8,128)(2,1)S(1)}, bf16[1,48,96,256]{3,2,1,0:T(8,128)(2,1)}, u32[]{:S(2)}) copy-start(bf16[1,48,96,256]{3,2,1,0:T(8,128)(2,1)} %param.12) | copy-start | bytes 7077892
  28.0 1.2 %collective-permute-start.8 = (f32[4,256]{1,0:T(4,128)S(1)}, f32[4,256]{1,0:T(4,128)S(1)}, u32[]{:S(2)}, u32[]{:S(2)}) collective-permute-start(f32[4,256]{1,0:T(4,128)S(1)} %get-tuple-element.107), channel_id=1, source_target_pairs={{0,1},{1,0},{2,3},{3,2},{4,5},{5,4},{6,7},{7,6},{8,9},{9,8},{10,11... | collective-permute-start | bytes 12296 | tf_op jit(solution)/shard_map/ppermute | solution.py:416
  29.2 3.1 %collective-permute-start.10 = (f32[4,256]{1,0:T(4,128)S(1)}, f32[4,256]{1,0:T(4,128)S(1)}, u32[]{:S(2)}, u32[]{:S(2)}) collective-permute-start(f32[4,256]{1,0:T(4,128)S(1)} %add.131), channel_id=1, source_target_pairs={{0,5},{1,4},{2,7},{3,6},{4,1},{5,0},{6,3},{7,2},{8,13},{9,12},{10,... | collective-permute-start | bytes 12296 | tf_op jit(solution)/shard_map/ppermute | solution.py:486
  30.6 3.0 %collective-permute-start.11 = (f32[4,256]{1,0:T(4,128)S(1)}, f32[4,256]{1,0:T(4,128)S(1)}, u32[]{:S(2)}, u32[]{:S(2)}) collective-permute-start(f32[4,256]{1,0:T(4,128)S(1)} %add.131), channel_id=1, source_target_pairs={{0,3},{1,2},{2,1},{3,0},{4,7},{5,6},{6,5},{7,4},{8,11},{9,10},{10,... | collective-permute-start | bytes 12296 | tf_op jit(solution)/shard_map/ppermute | solution.py:486
  31.0 3.9 %collective-permute-start.9 = (f32[4,256]{1,0:T(4,128)S(1)}, f32[4,256]{1,0:T(4,128)S(1)}, u32[]{:S(2)}, u32[]{:S(2)}) collective-permute-start(f32[4,256]{1,0:T(4,128)S(1)} %add.131), channel_id=1, source_target_pairs={{0,7},{1,6},{2,5},{3,4},{4,3},{5,2},{6,1},{7,0},{8,15},{9,14},{10,... | collective-permute-start | bytes 12296 | tf_op jit(solution)/shard_map/ppermute | solution.py:486
  34.9 4.8 %collective-permute-start.12 = (f32[4,256]{1,0:T(4,128)S(1)}, f32[4,256]{1,0:T(4,128)S(1)}, u32[]{:S(2)}, u32[]{:S(2)}) collective-permute-start(f32[4,256]{1,0:T(4,128)S(1)} %add_add_fusion.1), channel_id=1, source_target_pairs={{0,25},{1,24},{2,27},{3,26},{4,29},{5,28},{6,31},{7,30},{8,17},{9,... | collective-permute-start | bytes 12296 | tf_op jit(solution)/shard_map/ppermute | solution.py:486
  36.6 3.9 %collective-permute-start.13 = (f32[4,256]{1,0:T(4,128)S(1)}, f32[4,256]{1,0:T(4,128)S(1)}, u32[]{:S(2)}, u32[]{:S(2)}) collective-permute-start(f32[4,256]{1,0:T(4,128)S(1)} %add_add_fusion.1), channel_id=1, source_target_pairs={{0,17},{1,16},{2,19},{3,18},{4,21},{5,20},{6,23},{7,22},{8,25},{9,... | collective-permute-start | bytes 12296 | tf_op jit(solution)/shard_map/ppermute | solution.py:486
  36.7 3.8 %collective-permute-start.14 = (f32[4,256]{1,0:T(4,128)S(1)}, f32[4,256]{1,0:T(4,128)S(1)}, u32[]{:S(2)}, u32[]{:S(2)}) collective-permute-start(f32[4,256]{1,0:T(4,128)S(1)} %add_add_fusion.1), channel_id=1, source_target_pairs={{0,9},{1,8},{2,11},{3,10},{4,13},{5,12},{6,15},{7,14},{8,1},{9,0},... | collective-permute-start | bytes 12296 | tf_op jit(solution)/shard_map/ppermute | solution.py:486
  46.3 2.5 %collective-permute-start.15 = (f32[4,128,256]{2,1,0:T(8,128)S(1)}, f32[4,128,256]{2,1,0:T(8,128)S(1)}, u32[]{:S(2)}, u32[]{:S(2)}) collective-permute-start(f32[4,128,256]{2,1,0:T(8,128)S(1)} %bitcast.66), channel_id=1, source_target_pairs={{0,1},{1,0},{2,3},{3,2},{4,5},{5,4},{6,7},{7,6},{8,9},{9,8},{10,11... | collective-permute-start | bytes 1572872 | tf_op jit(solution)/shard_map/ppermute | solution.py:416
  48.7 4.0 %collective-permute-start.16 = (f32[5,128,256]{2,1,0:T(8,128)S(1)}, f32[5,128,256]{2,1,0:T(8,128)S(1)}, u32[]{:S(2)}, u32[]{:S(2)}) collective-permute-start(f32[5,128,256]{2,1,0:T(8,128)S(1)} %bitcast.65), channel_id=1, source_target_pairs={{0,1},{1,0},{2,3},{3,2},{4,5},{5,4},{6,7},{7,6},{8,9},{9,8},{10,11... | collective-permute-start | bytes 1966088 | tf_op jit(solution)/shard_map/ppermute | solution.py:416
  49.2 6.6 %collective-permute-start.20 = (bf16[128,256]{1,0:T(8,128)(2,1)S(1)}, bf16[128,256]{1,0:T(8,128)(2,1)S(1)}, u32[]{:S(2)}, u32[]{:S(2)}) collective-permute-start(bf16[128,256]{1,0:T(8,128)(2,1)S(1)} %get-tuple-element.170), channel_id=1, source_target_pairs={{0,6},{2,4},{4,2},{6,0},{8,14},{10,12},{12,10},{14,8},{16,22},{18,... | collective-permute-start | bytes 196616 | tf_op jit(solution)/shard_map/ppermute | solution.py:416
  50.7 5.9 %collective-permute-start.21 = (bf16[128,256]{1,0:T(8,128)(2,1)S(1)}, bf16[128,256]{1,0:T(8,128)(2,1)S(1)}, u32[]{:S(2)}, u32[]{:S(2)}) collective-permute-start(bf16[128,256]{1,0:T(8,128)(2,1)S(1)} %get-tuple-element.169), channel_id=1, source_target_pairs={{0,4},{2,6},{4,0},{6,2},{8,12},{10,14},{12,8},{14,10},{16,20},{18,... | collective-permute-start | bytes 196616 | tf_op jit(solution)/shard_map/ppermute | solution.py:416
  52.2 4.5 %collective-permute-start.22 = (bf16[128,256]{1,0:T(8,128)(2,1)S(1)}, bf16[128,256]{1,0:T(8,128)(2,1)S(1)}, u32[]{:S(2)}, u32[]{:S(2)}) collective-permute-start(bf16[128,256]{1,0:T(8,128)(2,1)S(1)} %get-tuple-element.168), channel_id=1, source_target_pairs={{0,2},{2,0},{4,6},{6,4},{8,10},{10,8},{12,14},{14,12},{16,18},{18,... | collective-permute-start | bytes 196616 | tf_op jit(solution)/shard_map/ppermute | solution.py:416
  52.8 6.3 %collective-permute-start.17 = (bf16[160,256]{1,0:T(8,128)(2,1)S(1)}, bf16[160,256]{1,0:T(8,128)(2,1)S(1)}, u32[]{:S(2)}, u32[]{:S(2)}) collective-permute-start(bf16[160,256]{1,0:T(8,128)(2,1)S(1)} %get-tuple-element.167), channel_id=1, source_target_pairs={{0,6},{2,4},{4,2},{6,0},{8,14},{10,12},{12,10},{14,8},{16,22},{18,... | collective-permute-start | bytes 245768 | tf_op jit(solution)/shard_map/ppermute | solution.py:416
  54.3 5.1 %collective-permute-start.18 = (bf16[160,256]{1,0:T(8,128)(2,1)S(1)}, bf16[160,256]{1,0:T(8,128)(2,1)S(1)}, u32[]{:S(2)}, u32[]{:S(2)}) collective-permute-start(bf16[160,256]{1,0:T(8,128)(2,1)S(1)} %get-tuple-element.166), channel_id=1, source_target_pairs={{0,4},{2,6},{4,0},{6,2},{8,12},{10,14},{12,8},{14,10},{16,20},{18,... | collective-permute-start | bytes 245768 | tf_op jit(solution)/shard_map/ppermute | solution.py:416
  55.8 4.4 %collective-permute-start.19 = (bf16[160,256]{1,0:T(8,128)(2,1)S(1)}, bf16[160,256]{1,0:T(8,128)(2,1)S(1)}, u32[]{:S(2)}, u32[]{:S(2)}) collective-permute-start(bf16[160,256]{1,0:T(8,128)(2,1)S(1)} %get-tuple-element.165), channel_id=1, source_target_pairs={{0,2},{2,0},{4,6},{6,4},{8,10},{10,8},{12,14},{14,12},{16,18},{18,... | collective-permute-start | bytes 245768 | tf_op jit(solution)/shard_map/ppermute | solution.py:416
  56.8 4.5 %collective-permute-start.24 = (bf16[128,256]{1,0:T(8,128)(2,1)S(1)}, bf16[128,256]{1,0:T(8,128)(2,1)S(1)}, u32[]{:S(2)}, u32[]{:S(2)}) collective-permute-start(bf16[128,256]{1,0:T(8,128)(2,1)S(1)} %fusion.3), channel_id=1, source_target_pairs={{0,9},{1,16},{2,11},{3,18},{4,13},{5,20},{6,15},{7,22},{8,25},{9,0... | collective-permute-start | bytes 196616 | tf_op jit(solution)/shard_map/ppermute | solution.py:563
  60.3 4.5 %collective-permute-start.23 = (bf16[160,256]{1,0:T(8,128)(2,1)S(1)}, bf16[160,256]{1,0:T(8,128)(2,1)S(1)}, u32[]{:S(2)}, u32[]{:S(2)}) collective-permute-start(bf16[160,256]{1,0:T(8,128)(2,1)S(1)} %fusion.1), channel_id=1, source_target_pairs={{0,9},{1,16},{2,11},{3,18},{4,13},{5,20},{6,15},{7,22},{8,25},{9,0... | collective-permute-start | bytes 245768 | tf_op jit(solution)/shard_map/ppermute | solution.py:563
  61.2 6.9 %collective-permute-start.27 = (bf16[128,256]{1,0:T(8,128)(2,1)S(1)}, bf16[128,256]{1,0:T(8,128)(2,1)S(1)}, u32[]{:S(2)}, u32[]{:S(2)}) collective-permute-start(bf16[128,256]{1,0:T(8,128)(2,1)S(1)} %add_convert_fusion.6), channel_id=1, source_target_pairs={{0,17},{1,8},{2,19},{3,10},{4,21},{5,12},{6,23},{7,14},{8,1},{9,24... | collective-permute-start | bytes 196616 | tf_op jit(solution)/shard_map/ppermute | solution.py:563
  64.8 7.2 %collective-permute-start.25 = (bf16[160,256]{1,0:T(8,128)(2,1)S(1)}, bf16[160,256]{1,0:T(8,128)(2,1)S(1)}, u32[]{:S(2)}, u32[]{:S(2)}) collective-permute-start(bf16[160,256]{1,0:T(8,128)(2,1)S(1)} %add_convert_fusion.1), channel_id=1, source_target_pairs={{0,17},{1,8},{2,19},{3,10},{4,21},{5,12},{6,23},{7,14},{8,1},{9,24... | collective-permute-start | bytes 245768 | tf_op jit(solution)/shard_map/ppermute | solution.py:563
  68.2 4.1 %collective-permute-start.31 = (bf16[128,256]{1,0:T(8,128)(2,1)S(1)}, bf16[128,256]{1,0:T(8,128)(2,1)S(1)}, u32[]{:S(2)}, u32[]{:S(2)}) collective-permute-start(bf16[128,256]{1,0:T(8,128)(2,1)S(1)} %add_convert_fusion.5), channel_id=1, source_target_pairs={{0,1},{1,0},{2,3},{3,2},{4,5},{5,4},{6,7},{7,6},{8,9},{9,8},{10,11... | collective-permute-start | bytes 196616 | tf_op jit(solution)/shard_map/ppermute | solution.py:416
  68.5 5.7 %collective-permute-start.28 = (bf16[128,256]{1,0:T(8,128)(2,1)S(1)}, bf16[128,256]{1,0:T(8,128)(2,1)S(1)}, u32[]{:S(2)}, u32[]{:S(2)}) collective-permute-start(bf16[128,256]{1,0:T(8,128)(2,1)S(1)} %add_convert_fusion.5), channel_id=1, source_target_pairs={{0,6},{1,7},{2,4},{3,5},{4,2},{5,3},{6,0},{7,1},{8,15},{9,14},{10,... | collective-permute-start | bytes 196616 | tf_op jit(solution)/shard_map/ppermute | solution.py:573
  69.4 9.9 %collective-permute-start.29 = (bf16[128,256]{1,0:T(8,128)(2,1)S(1)}, bf16[128,256]{1,0:T(8,128)(2,1)S(1)}, u32[]{:S(2)}, u32[]{:S(2)}) collective-permute-start(bf16[128,256]{1,0:T(8,128)(2,1)S(1)} %add_convert_fusion.5), channel_id=1, source_target_pairs={{0,4},{1,5},{2,6},{3,7},{4,0},{5,1},{6,2},{7,3},{8,13},{9,12},{10,... | collective-permute-start | bytes 196616 | tf_op jit(solution)/shard_map/ppermute | solution.py:573
  70.9 8.4 %collective-permute-start.30 = (bf16[128,256]{1,0:T(8,128)(2,1)S(1)}, bf16[128,256]{1,0:T(8,128)(2,1)S(1)}, u32[]{:S(2)}, u32[]{:S(2)}) collective-permute-start(bf16[128,256]{1,0:T(8,128)(2,1)S(1)} %add_convert_fusion.5), channel_id=1, source_target_pairs={{0,2},{1,3},{2,0},{3,1},{4,6},{5,7},{6,4},{7,5},{8,11},{9,10},{10,... | collective-permute-start | bytes 196616 | tf_op jit(solution)/shard_map/ppermute | solution.py:573
  72.0 2.8 %collective-permute-start.26 = (bf16[160,256]{1,0:T(8,128)(2,1)S(1)}, bf16[160,256]{1,0:T(8,128)(2,1)S(1)}, u32[]{:S(2)}, u32[]{:S(2)}) collective-permute-start(bf16[160,256]{1,0:T(8,128)(2,1)S(1)} %add_convert_fusion), channel_id=1, source_target_pairs={{0,1},{1,0},{2,3},{3,2},{4,5},{5,4},{6,7},{7,6},{8,9},{9,8},{10,11... | collective-permute-start | bytes 245768 | tf_op jit(solution)/shard_map/ppermute | solution.py:416
  72.4 7.1 %collective-permute-start.32 = (bf16[160,256]{1,0:T(8,128)(2,1)S(1)}, bf16[160,256]{1,0:T(8,128)(2,1)S(1)}, u32[]{:S(2)}, u32[]{:S(2)}) collective-permute-start(bf16[160,256]{1,0:T(8,128)(2,1)S(1)} %add_convert_fusion), channel_id=1, source_target_pairs={{0,6},{1,7},{2,4},{3,5},{4,2},{5,3},{6,0},{7,1},{8,15},{9,14},{10,... | collective-permute-start | bytes 245768 | tf_op jit(solution)/shard_map/ppermute | solution.py:573
  74.2 5.3 %collective-permute-start.33 = (bf16[160,256]{1,0:T(8,128)(2,1)S(1)}, bf16[160,256]{1,0:T(8,128)(2,1)S(1)}, u32[]{:S(2)}, u32[]{:S(2)}) collective-permute-start(bf16[160,256]{1,0:T(8,128)(2,1)S(1)} %add_convert_fusion), channel_id=1, source_target_pairs={{0,4},{1,5},{2,6},{3,7},{4,0},{5,1},{6,2},{7,3},{8,13},{9,12},{10,... | collective-permute-start | bytes 245768 | tf_op jit(solution)/shard_map/ppermute | solution.py:573
  74.8 4.7 %collective-permute-start.34 = (bf16[160,256]{1,0:T(8,128)(2,1)S(1)}, bf16[160,256]{1,0:T(8,128)(2,1)S(1)}, u32[]{:S(2)}, u32[]{:S(2)}) collective-permute-start(bf16[160,256]{1,0:T(8,128)(2,1)S(1)} %add_convert_fusion), channel_id=1, source_target_pairs={{0,2},{1,3},{2,0},{3,1},{4,6},{5,7},{6,4},{7,5},{8,11},{9,10},{10,... | collective-permute-start | bytes 245768 | tf_op jit(solution)/shard_map/ppermute | solution.py:573
  79.6 1.0 %copy-start.7 = (f32[36,32,256]{2,1,0:T(8,128)}, f32[36,32,256]{2,1,0:T(8,128)S(1)}, u32[]{:S(2)}) copy-start(f32[36,32,256]{2,1,0:T(8,128)S(1)} %convert_dynamic-update-slice_fusion) | copy-start | bytes 3538948
where the time goes:
time: 80.8 us; the launch traced here: 80.6 us
  starting transfers between devices  34.5 us (43%)
  Pallas kernels  27.2 us (34%)
  waiting for transfers between devices  16.2 us (20%)
  local copies, waits for them, and re-layouts  1.16 us (1%)
  between operations  1.03 us (1%)
    ppermute x12, starting transfers between devices, swap_across(): return lax.ppermute(array, ('rep', 'sp'), pairs)  15.2 us
    ppermute x13, starting transfers between devices, swap(): return lax.ppermute(array, axis, [(i, i ^ stride) for i in range(count)])  9.72 us
    ppermute x12, waiting for transfers between devices, swap_across(): return lax.ppermute(array, ('rep', 'sp'), pairs)  9.53 us
    ppermute x6, starting transfers between devices, bring(): return lax.ppermute(array, ('rep', 'sp'), pairs)  6.1 us
    pallas_call x1, Pallas kernels, local(): pl.pallas_call(inner_kernel, out_shape=(jax.ShapeDtypeStruct((rows_four -...  5.83 us
    pallas_call x1, Pallas kernels, local(): pl.pallas_call(functools.partial(backward_kernel, counts, sp_count, (cols...  5.7 us
    pallas_call x2, Pallas kernels, inputs(): pl.pallas_call(functools.partial(input_kernel, group), out_shape=jax.Shap...  3.96 us
    ppermute x4, starting transfers between devices, swap_high(): return lax.ppermute(array, ('rep', 'sp'), pairs)  3.49 us
  transfers between devices with their start and end apart: 35, of which 16 were waited for; matrix products, arithmetic and copies ran while one was open for 1% of the time, Pallas kernels for 20%

commit v1 on v0

--- a/solution.py
+++ b/solution.py
@@ -118,35 +118,44 @@
     return jnp.sum(total, 0, keepdims=True)
 
 
-def inner_level(x_ref, w_ref, conv_ref, three, sums, most):
-    rows, cols = x_ref.shape[:2]
-    pitch = three.shape[1]
-
-    def fill_row(row):
-        put_three(three, row, widen(x_ref[row], pitch), cols, False)
+def inner_kernel(four_ref, six_ref, w_ref, conv_four_ref, conv_six_ref, moments_ref, three_four, three_six):
+    rows_four, cols_four = four_ref.shape[:2]
+    rows_six, cols_six = six_ref.shape[:2]
+    pitch_four, pitch_six = three_four.shape[1], three_six.shape[1]
+    sums_four, sums_six = ([], []), ([], [])
+    inner = rows_four - 2
+    count = max(1, inner // 9)
+    bounds = [index * inner // count for index in range(count + 1)]
+
+    def fill_four(row):
+        put_three(three_four, row, four_ref[row].astype(F32), cols_four, False)
+
+    def fill_six(row):
+        put_three(three_six, row, widen(six_ref[row], pitch_six), cols_six, False)
 
     def dot(start, end):
-        conv = conv_rows(beside(three, (start, start + 1, start + 2), end - start), w_ref)
-        conv = conv.reshape(end - start, pitch, -1)
-        conv_ref[start:end] = conv
-        add_moments(sums, conv, cols)
-
-    inner = rows - 2
-    count = max(1, inner // most)
-    bounds = [index * inner // count for index in range(count + 1)]
+        lhs = beside(three_four, (start, start + 1, start + 2), end - start)
+        cells = lhs.shape[0]
+        if end == inner:
+            lhs = jnp.concatenate([lhs, beside(three_six, (0, 1, 2), rows_six - 2)], 0)
+        conv = conv_rows(lhs, w_ref)
+        four = conv[:cells].reshape(end - start, pitch_four, -1)
+        conv_four_ref[start:end] = four
+        add_moments(sums_four, four, cols_four)
+        if end == inner:
+            six = conv[cells:].reshape(rows_six - 2, pitch_six, -1)
+            conv_six_ref[...] = six
+            add_moments(sums_six, six, cols_six)
+
     fills, dots, done = [], [], 0
     for start, end in zip(bounds[:-1], bounds[1:]):
-        fills.append(lambda todo=range(done, end + 2): [fill_row(row) for row in todo])
+        todo = [functools.partial(fill_four, row) for row in range(done, end + 2)]
+        if end == inner:
+            todo += [functools.partial(fill_six, row) for row in range(rows_six)]
+        fills.append(lambda todo=todo: [fill() for fill in todo])
         done = end + 2
         dots.append(functools.partial(dot, start, end))
-    return fills, dots
-
-
-def inner_kernel(four_ref, six_ref, w_ref, conv_four_ref, conv_six_ref, moments_ref, three_four, three_six):
-    sums_four, sums_six = ([], []), ([], [])
-    fills_six, dots_six = inner_level(six_ref, w_ref, conv_six_ref, three_six, sums_six, 10)
-    fills_four, dots_four = inner_level(four_ref, w_ref, conv_four_ref, three_four, sums_four, 8)
-    staged(fills_six + fills_four, dots_six + dots_four)
+    staged(fills, dots)
     moments_ref[...] = jnp.concatenate([folded(parts) for parts in sums_four + sums_six], 0)
 
 
@@ -291,10 +300,10 @@
 
 
 def backward_bounds(rows):
-    bounds = [0, min(4, rows), min(16, rows)]
+    bounds = [0, min(8, rows)]
     while bounds[-1] < rows:
         bounds.append(min(bounds[-1] + 16, rows))
-    return sorted(set(bounds))
+    return bounds
 
 
 def weight_dot(turned_ref, three_four, three_six, total, taps, start, end):

time: 80.8 us -> 80.8 us (level)
  no operation moved by 1% of the time
where the time goes in v1:
time: 80.8 us; the launch traced here: 80.6 us
  starting transfers between devices  34.6 us (43%)
  Pallas kernels  27.1 us (34%)
  waiting for transfers between devices  16.2 us (20%)
  local copies, waits for them, and re-layouts  1.16 us (1%)
  between operations  1.03 us (1%)
    ppermute x12, starting transfers between devices, swap_across(): return lax.ppermute(array, ('rep', 'sp'), pairs)  15.2 us
    ppermute x13, starting transfers between devices, swap(): return lax.ppermute(array, axis, [(i, i ^ stride) for i in range(count)])  9.74 us
    ppermute x12, waiting for transfers between devices, swap_across(): return lax.ppermute(array, ('rep', 'sp'), pairs)  9.51 us
    ppermute x6, starting transfers between devices, bring(): return lax.ppermute(array, ('rep', 'sp'), pairs)  6.11 us
    pallas_call x1, Pallas kernels, local(): pl.pallas_call(inner_kernel, out_shape=(jax.ShapeDtypeStruct((rows_four -...  5.87 us
    pallas_call x1, Pallas kernels, local(): pl.pallas_call(functools.partial(backward_kernel, counts, sp_count, (cols...  5.58 us
    pallas_call x2, Pallas kernels, inputs(): pl.pallas_call(functools.partial(input_kernel, group), out_shape=jax.Shap...  3.95 us
    ppermute x4, starting transfers between devices, swap_high(): return lax.ppermute(array, ('rep', 'sp'), pairs)  3.49 us
  transfers between devices with their start and end apart: 35, of which 16 were waited for; matrix products, arithmetic and copies ran while one was open for 1% of the time, Pallas kernels for 20%

profile of v1, /device:TPU:0, one launch (start us, length us, event | category | flops | bytes accessed | tf_op | source)
XLA Modules:
  0.0 80.6 jit_solution(12591964200701023219)
XLA Ops:
  0.7 1.7 %edges.1 = bf16[384,256]{1,0:T(8,128)(2,1)} custom-call(bf16[48,96,256]{2,1,0:T(8,128)(2,1)} %bitcast.51, bf16[12,24,256]{2,1,0:T(8,128)(2,1)} %bitcast.59, bf16[48,96,256]{2,1,0:T(8,128)(2,1)} %bitcast.55, bf16[12,24,256]{2,1,0:T(8,128)(2,1)} %bitcast.63), custom_call_target="tpu_custom_call" | custom-call | tf_op jit(solution)/shard_map/edges/pallas_call | solution.py:467
  2.4 0.5 collective-permute-start
  3.0 5.9 %forward_inner.1 = (bf16[46,96,256]{2,1,0:T(8,128)(2,1)S(1)}, bf16[10,32,256]{2,1,0:T(8,128)(2,1)S(1)}, f32[4,256]{1,0:T(4,128)S(1)}) custom-call(bf16[48,96,256]{2,1,0:T(8,128)(2,1)S(1)} %bitcast.52, bf16[12,24,256]{2,1,0:T(8,128)(2,1)S(1)} %bitcast.60, bf16[9,256,256]{2,1,0:T(8,128)(2,1)S(1)} %copy-done.2), custom_call_target="tpu_custom_call" | custom-call | flops 5775556608 | bytes 4718592 | tf_op jit(solution)/shard_map/forward_inner/pallas_call | solution.py:633
  8.9 0.8 forward_outer.1
  9.6 0.4 collective-permute-start.1
  10.0 0.8 %collective-permute-done.1 = f32[4,256]{1,0:T(4,128)S(1)} collective-permute-done((f32[4,256]{1,0:T(4,128)S(1)}, f32[4,256]{1,0:T(4,128)S(1)}, u32[]{:S(2)}, u32[]{:S(2)}) %collective-permute-start.1) | collective-permute-done | bytes 4128 | tf_op jit(solution)/shard_map/ppermute | solution.py:425
  10.9 3.6 %collective-permute-start.2 = (f32[4,256]{1,0:T(4,128)S(1)}, f32[4,256]{1,0:T(4,128)S(1)}, u32[]{:S(2)}, u32[]{:S(2)}) collective-permute-start(f32[4,256]{1,0:T(4,128)S(1)} %add.124), channel_id=1, source_target_pairs={{0,7},{1,6},{2,5},{3,4},{4,3},{5,2},{6,1},{7,0},{8,15},{9,14},{10,... | collective-permute-start | bytes 12296 | tf_op jit(solution)/shard_map/ppermute | solution.py:495
  14.4 0.4 collective-permute-start.3
  14.9 0.1 collective-permute-start.4
  14.9 0.8 %collective-permute-done.2 = f32[4,256]{1,0:T(4,128)S(1)} collective-permute-done((f32[4,256]{1,0:T(4,128)S(1)}, f32[4,256]{1,0:T(4,128)S(1)}, u32[]{:S(2)}, u32[]{:S(2)}) %collective-permute-start.2) | collective-permute-done | bytes 4128 | tf_op jit(solution)/shard_map/ppermute | solution.py:495
  15.8 1.7 %collective-permute-done.3 = f32[4,256]{1,0:T(4,128)S(1)} collective-permute-done((f32[4,256]{1,0:T(4,128)S(1)}, f32[4,256]{1,0:T(4,128)S(1)}, u32[]{:S(2)}, u32[]{:S(2)}) %collective-permute-start.3) | collective-permute-done | bytes 4128 | tf_op jit(solution)/shard_map/ppermute | solution.py:495
  17.5 0.4 collective-permute-done.4
  17.9 3.5 %collective-permute-start.5 = (f32[4,256]{1,0:T(4,128)S(1)}, f32[4,256]{1,0:T(4,128)S(1)}, u32[]{:S(2)}, u32[]{:S(2)}) collective-permute-start(f32[4,256]{1,0:T(4,128)S(1)} %add_add_fusion.3), channel_id=1, source_target_pairs={{0,25},{1,24},{2,27},{3,26},{4,29},{5,28},{6,31},{7,30},{8,17},{9,... | collective-permute-start | bytes 12296 | tf_op jit(solution)/shard_map/ppermute | solution.py:495
  21.4 0.6 collective-permute-start.7
  21.9 1.0 %turn.1 = (bf16[256,4992]{1,0:T(8,128)(2,1)S(1)}, bf16[2304,256]{1,0:T(8,128)(2,1)S(1)}) custom-call(bf16[48,96,256]{2,1,0:T(8,128)(2,1)S(1)} %bitcast.54, bf16[12,24,256]{2,1,0:T(8,128)(2,1)S(1)} %bitcast.62, bf16[9,256,256]{2,1,0:T(8,128)(2,1)S(1)} %copy-done.2), custom_call_target="tpu_custom_call" | custom-call | flops 1732667008 | bytes 4718592 | tf_op jit(solution)/shard_map/turn/pallas_call | solution.py:668
  23.0 2.4 %collective-permute-done.6 = f32[4,256]{1,0:T(4,128)S(1)} collective-permute-done((f32[4,256]{1,0:T(4,128)S(1)}, f32[4,256]{1,0:T(4,128)S(1)}, u32[]{:S(2)}, u32[]{:S(2)}) %collective-permute-start.6) | collective-permute-done | bytes 4128 | tf_op jit(solution)/shard_map/ppermute | solution.py:495
  25.4 2.6 %slopes.1 = (f32[50,96,256]{2,1,0:T(8,128)S(1)}, f32[14,32,256]{2,1,0:T(8,128)S(1)}, f32[4,256]{1,0:T(4,128)S(1)}) custom-call(bf16[46,96,256]{2,1,0:T(8,128)(2,1)S(1)} %get-tuple-element.100.inner_four_ref, bf16[10,32,256]{2,1,0:T(8,128)(2,1)S(1)} %get-tuple-element.101.inner_six_ref, bf16[4,96,256]{2,1,0:T(8,128)(2,1)S(1)} %get-tuple-element.102.outer_four_ref, ...), custom_call_target="tpu_custom_call" | custom-call | flops 57755568 | bytes 4718592 | tf_op jit(solution)/shard_map/slopes/pallas_call | solution.py:682
  28.0 0.4 collective-permute-start.8
  28.4 0.9 %collective-permute-done.8 = f32[4,256]{1,0:T(4,128)S(1)} collective-permute-done((f32[4,256]{1,0:T(4,128)S(1)}, f32[4,256]{1,0:T(4,128)S(1)}, u32[]{:S(2)}, u32[]{:S(2)}) %collective-permute-start.8) | collective-permute-done | bytes 4128 | tf_op jit(solution)/shard_map/ppermute | solution.py:425
  29.2 1.4 %collective-permute-start.10 = (f32[4,256]{1,0:T(4,128)S(1)}, f32[4,256]{1,0:T(4,128)S(1)}, u32[]{:S(2)}, u32[]{:S(2)}) collective-permute-start(f32[4,256]{1,0:T(4,128)S(1)} %add.131), channel_id=1, source_target_pairs={{0,5},{1,4},{2,7},{3,6},{4,1},{5,0},{6,3},{7,2},{8,13},{9,12},{10,... | collective-permute-start | bytes 12296 | tf_op jit(solution)/shard_map/ppermute | solution.py:495
  30.7 0.3 collective-permute-start.11
  31.0 1.3 %collective-permute-start.9 = (f32[4,256]{1,0:T(4,128)S(1)}, f32[4,256]{1,0:T(4,128)S(1)}, u32[]{:S(2)}, u32[]{:S(2)}) collective-permute-start(f32[4,256]{1,0:T(4,128)S(1)} %add.131), channel_id=1, source_target_pairs={{0,7},{1,6},{2,5},{3,4},{4,3},{5,2},{6,1},{7,0},{8,15},{9,14},{10,... | collective-permute-start | bytes 12296 | tf_op jit(solution)/shard_map/ppermute | solution.py:495
  32.4 1.3 %collective-permute-done.11 = f32[4,256]{1,0:T(4,128)S(1)} collective-permute-done((f32[4,256]{1,0:T(4,128)S(1)}, f32[4,256]{1,0:T(4,128)S(1)}, u32[]{:S(2)}, u32[]{:S(2)}) %collective-permute-start.11) | collective-permute-done | bytes 4128 | tf_op jit(solution)/shard_map/ppermute | solution.py:495
  33.7 1.2 %collective-permute-done.9 = f32[4,256]{1,0:T(4,128)S(1)} collective-permute-done((f32[4,256]{1,0:T(4,128)S(1)}, f32[4,256]{1,0:T(4,128)S(1)}, u32[]{:S(2)}, u32[]{:S(2)}) %collective-permute-start.9) | collective-permute-done | bytes 4128 | tf_op jit(solution)/shard_map/ppermute | solution.py:495
  35.0 1.7 %collective-permute-start.12 = (f32[4,256]{1,0:T(4,128)S(1)}, f32[4,256]{1,0:T(4,128)S(1)}, u32[]{:S(2)}, u32[]{:S(2)}) collective-permute-start(f32[4,256]{1,0:T(4,128)S(1)} %add_add_fusion.1), channel_id=1, source_target_pairs={{0,25},{1,24},{2,27},{3,26},{4,29},{5,28},{6,31},{7,30},{8,17},{9,... | collective-permute-start | bytes 12296 | tf_op jit(solution)/shard_map/ppermute | solution.py:495
  36.7 0.1 collective-permute-start.13
  36.8 2.2 %collective-permute-start.14 = (f32[4,256]{1,0:T(4,128)S(1)}, f32[4,256]{1,0:T(4,128)S(1)}, u32[]{:S(2)}, u32[]{:S(2)}) collective-permute-start(f32[4,256]{1,0:T(4,128)S(1)} %add_add_fusion.1), channel_id=1, source_target_pairs={{0,9},{1,8},{2,11},{3,10},{4,13},{5,12},{6,15},{7,14},{8,1},{9,0},... | collective-permute-start | bytes 12296 | tf_op jit(solution)/shard_map/ppermute | solution.py:495
  39.0 0.8 %collective-permute-done.12 = f32[4,256]{1,0:T(4,128)S(1)} collective-permute-done((f32[4,256]{1,0:T(4,128)S(1)}, f32[4,256]{1,0:T(4,128)S(1)}, u32[]{:S(2)}, u32[]{:S(2)}) %collective-permute-start.12) | collective-permute-done | bytes 4128 | tf_op jit(solution)/shard_map/ppermute | solution.py:495
  39.8 0.8 %collective-permute-done.13 = f32[4,256]{1,0:T(4,128)S(1)} collective-permute-done((f32[4,256]{1,0:T(4,128)S(1)}, f32[4,256]{1,0:T(4,128)S(1)}, u32[]{:S(2)}, u32[]{:S(2)}) %collective-permute-start.13) | collective-permute-done | bytes 4128 | tf_op jit(solution)/shard_map/ppermute | solution.py:495
  40.6 5.6 %backward.1 = (bf16[50,96,768]{2,1,0:T(8,128)(2,1)S(1)}, bf16[14,32,768]{2,1,0:T(8,128)(2,1)S(1)}, f32[4,128,256]{2,1,0:T(8,128)S(1)}, f32[1,4,128,256]{3,2,1,0:...) custom-call(bf16[256,4992]{1,0:T(8,128)(2,1)S(1)} %get-tuple-element.99.turned_ref, ...), custom_call_target="tpu_custom_call" | custom-call | flops 3465334016 | bytes 9437184 | tf_op jit(solution)/shard_map/backward/pallas_call | solution.py:709
  46.2 0.2 collective-permute-start.15
  46.4 2.3 %weights.1 = (f32[5,128,256]{2,1,0:T(8,128)S(1)}, f32[1,5,128,256]{3,2,1,0:T(8,128)S(1)}) custom-call(bf16[256,4992]{1,0:T(8,128)(2,1)S(1)} %get-tuple-element.99.turned_ref, bf16[50,96,768]{2,1,0:T(8,128)(2,1)S(1)} %get-tuple-element.144.three_four, bf16[14,32,768]{2,1,0:T(8,128)(2,1)S(1)} %get-tuple-element.117.three_six, ...), custom_call_target="tpu_custom_call" | custom-call | flops 3465334016 | bytes 9437184 | tf_op jit(solution)/shard_map/weights/pallas_call | solution.py:727
  48.7 0.4 collective-permute-start.16
  49.0 0.1 fusion.9
  49.1 1.5 %collective-permute-start.20 = (bf16[128,256]{1,0:T(8,128)(2,1)S(1)}, bf16[128,256]{1,0:T(8,128)(2,1)S(1)}, u32[]{:S(2)}, u32[]{:S(2)}) collective-permute-start(bf16[128,256]{1,0:T(8,128)(2,1)S(1)} %get-tuple-element.170), channel_id=1, source_target_pairs={{0,6},{2,4},{4,2},{6,0},{8,14},{10,12},{12,10},{14,8},{16,22},{18,... | collective-permute-start | bytes 196616 | tf_op jit(solution)/shard_map/ppermute | solution.py:425
  50.6 1.5 %collective-permute-start.21 = (bf16[128,256]{1,0:T(8,128)(2,1)S(1)}, bf16[128,256]{1,0:T(8,128)(2,1)S(1)}, u32[]{:S(2)}, u32[]{:S(2)}) collective-permute-start(bf16[128,256]{1,0:T(8,128)(2,1)S(1)} %get-tuple-element.169), channel_id=1, source_target_pairs={{0,4},{2,6},{4,0},{6,2},{8,12},{10,14},{12,8},{14,10},{16,20},{18,... | collective-permute-start | bytes 196616 | tf_op jit(solution)/shard_map/ppermute | solution.py:425
  52.1 0.5 collective-permute-start.22
  52.7 0.1 fusion.6
  52.7 1.5 %collective-permute-start.17 = (bf16[160,256]{1,0:T(8,128)(2,1)S(1)}, bf16[160,256]{1,0:T(8,128)(2,1)S(1)}, u32[]{:S(2)}, u32[]{:S(2)}) collective-permute-start(bf16[160,256]{1,0:T(8,128)(2,1)S(1)} %get-tuple-element.167), channel_id=1, source_target_pairs={{0,6},{2,4},{4,2},{6,0},{8,14},{10,12},{12,10},{14,8},{16,22},{18,... | collective-permute-start | bytes 245768 | tf_op jit(solution)/shard_map/ppermute | solution.py:425
  54.2 1.5 %collective-permute-start.18 = (bf16[160,256]{1,0:T(8,128)(2,1)S(1)}, bf16[160,256]{1,0:T(8,128)(2,1)S(1)}, u32[]{:S(2)}, u32[]{:S(2)}) collective-permute-start(bf16[160,256]{1,0:T(8,128)(2,1)S(1)} %get-tuple-element.166), channel_id=1, source_target_pairs={{0,4},{2,6},{4,0},{6,2},{8,12},{10,14},{12,8},{14,10},{16,20},{18,... | collective-permute-start | bytes 245768 | tf_op jit(solution)/shard_map/ppermute | solution.py:425
  55.8 0.7 collective-permute-start.19
  56.5 0.2 collective-permute-done.22
  56.7 0.3 collective-permute-start.24
  57.0 2.0 %inputs.2.rest_0_ = bf16[16,96,256]{2,1,0:T(8,128)(2,1)S(1)} custom-call(bf16[50,96,768]{2,1,0:T(8,128)(2,1)S(1)} %get-tuple-element.144.three_four, bf16[2304,256]{1,0:T(8,128)(2,1)S(1)} %get-tuple-element.133.turned), custom_call_target="tpu_custom_call" | custom-call | flops 1732667008 | bytes 1179648 | tf_op jit(solution)/shard_map/inputs/pallas_call | solution.py:746
  59.0 0.3 collective-permute-done.18
  59.3 0.9 %collective-permute-done.19 = bf16[160,256]{1,0:T(8,128)(2,1)S(1)} collective-permute-done((bf16[160,256]{1,0:T(8,128)(2,1)S(1)}, bf16[160,256]{1,0:T(8,128)(2,1)S(1)}, u32[]{:S(2)}, u32[]{:S(2)}) %collective-permute-start.19) | collective-permute-done | bytes 81952 | tf_op jit(solution)/shard_map/ppermute | solution.py:425
  60.2 0.4 collective-permute-start.23
  60.6 0.5 collective-permute-done.24
  61.2 1.6 %collective-permute-start.27 = (bf16[128,256]{1,0:T(8,128)(2,1)S(1)}, bf16[128,256]{1,0:T(8,128)(2,1)S(1)}, u32[]{:S(2)}, u32[]{:S(2)}) collective-permute-start(bf16[128,256]{1,0:T(8,128)(2,1)S(1)} %add_convert_fusion.6), channel_id=1, source_target_pairs={{0,17},{1,8},{2,19},{3,10},{4,21},{5,12},{6,23},{7,14},{8,1},{9,24... | collective-permute-start | bytes 196616 | tf_op jit(solution)/shard_map/ppermute | solution.py:572
  62.7 2.0 %inputs.3.rest_1_ = bf16[16,96,256]{2,1,0:T(8,128)(2,1)S(1)} custom-call(bf16[50,96,768]{2,1,0:T(8,128)(2,1)S(1)} %get-tuple-element.144.three_four, bf16[2304,256]{1,0:T(8,128)(2,1)S(1)} %get-tuple-element.133.turned), custom_call_target="tpu_custom_call" | custom-call | flops 1732667008 | bytes 1179648 | tf_op jit(solution)/shard_map/inputs/pallas_call | solution.py:746
  64.7 1.2 %collective-permute-start.25 = (bf16[160,256]{1,0:T(8,128)(2,1)S(1)}, bf16[160,256]{1,0:T(8,128)(2,1)S(1)}, u32[]{:S(2)}, u32[]{:S(2)}) collective-permute-start(bf16[160,256]{1,0:T(8,128)(2,1)S(1)} %add_convert_fusion.1), channel_id=1, source_target_pairs={{0,17},{1,8},{2,19},{3,10},{4,21},{5,12},{6,23},{7,14},{8,1},{9,24... | collective-permute-start | bytes 245768 | tf_op jit(solution)/shard_map/ppermute | solution.py:572
  66.0 2.1 %collective-permute-done.27 = bf16[128,256]{1,0:T(8,128)(2,1)S(1)} collective-permute-done((bf16[128,256]{1,0:T(8,128)(2,1)S(1)}, bf16[128,256]{1,0:T(8,128)(2,1)S(1)}, u32[]{:S(2)}, u32[]{:S(2)}) %collective-permute-start.27) | collective-permute-done | bytes 65568 | tf_op jit(solution)/shard_map/ppermute | solution.py:572
  68.1 0.3 collective-permute-start.31
  68.4 0.9 %collective-permute-start.28 = (bf16[128,256]{1,0:T(8,128)(2,1)S(1)}, bf16[128,256]{1,0:T(8,128)(2,1)S(1)}, u32[]{:S(2)}, u32[]{:S(2)}) collective-permute-start(bf16[128,256]{1,0:T(8,128)(2,1)S(1)} %add_convert_fusion.5), channel_id=1, source_target_pairs={{0,6},{1,7},{2,4},{3,5},{4,2},{5,3},{6,0},{7,1},{8,15},{9,14},{10,... | collective-permute-start | bytes 196616 | tf_op jit(solution)/shard_map/ppermute | solution.py:582
  69.3 1.5 %collective-permute-start.29 = (bf16[128,256]{1,0:T(8,128)(2,1)S(1)}, bf16[128,256]{1,0:T(8,128)(2,1)S(1)}, u32[]{:S(2)}, u32[]{:S(2)}) collective-permute-start(bf16[128,256]{1,0:T(8,128)(2,1)S(1)} %add_convert_fusion.5), channel_id=1, source_target_pairs={{0,4},{1,5},{2,6},{3,7},{4,0},{5,1},{6,2},{7,3},{8,13},{9,12},{10,... | collective-permute-start | bytes 196616 | tf_op jit(solution)/shard_map/ppermute | solution.py:582
  70.8 1.1 %collective-permute-start.30 = (bf16[128,256]{1,0:T(8,128)(2,1)S(1)}, bf16[128,256]{1,0:T(8,128)(2,1)S(1)}, u32[]{:S(2)}, u32[]{:S(2)}) collective-permute-start(bf16[128,256]{1,0:T(8,128)(2,1)S(1)} %add_convert_fusion.5), channel_id=1, source_target_pairs={{0,2},{1,3},{2,0},{3,1},{4,6},{5,7},{6,4},{7,5},{8,11},{9,10},{10,... | collective-permute-start | bytes 196616 | tf_op jit(solution)/shard_map/ppermute | solution.py:582
  71.9 0.3 collective-permute-start.26
  72.3 0.9 %collective-permute-start.32 = (bf16[160,256]{1,0:T(8,128)(2,1)S(1)}, bf16[160,256]{1,0:T(8,128)(2,1)S(1)}, u32[]{:S(2)}, u32[]{:S(2)}) collective-permute-start(bf16[160,256]{1,0:T(8,128)(2,1)S(1)} %add_convert_fusion), channel_id=1, source_target_pairs={{0,6},{1,7},{2,4},{3,5},{4,2},{5,3},{6,0},{7,1},{8,15},{9,14},{10,... | collective-permute-start | bytes 245768 | tf_op jit(solution)/shard_map/ppermute | solution.py:582
  73.2 0.9 %collective-permute-done.28 = bf16[128,256]{1,0:T(8,128)(2,1)S(1)} collective-permute-done((bf16[128,256]{1,0:T(8,128)(2,1)S(1)}, bf16[128,256]{1,0:T(8,128)(2,1)S(1)}, u32[]{:S(2)}, u32[]{:S(2)}) %collective-permute-start.28) | collective-permute-done | bytes 65568 | tf_op jit(solution)/shard_map/ppermute | solution.py:582
  74.1 0.6 collective-permute-start.33
  74.7 1.1 %collective-permute-start.34 = (bf16[160,256]{1,0:T(8,128)(2,1)S(1)}, bf16[160,256]{1,0:T(8,128)(2,1)S(1)}, u32[]{:S(2)}, u32[]{:S(2)}) collective-permute-start(bf16[160,256]{1,0:T(8,128)(2,1)S(1)} %add_convert_fusion), channel_id=1, source_target_pairs={{0,2},{1,3},{2,0},{3,1},{4,6},{5,7},{6,4},{7,5},{8,11},{9,10},{10,... | collective-permute-start | bytes 245768 | tf_op jit(solution)/shard_map/ppermute | solution.py:582
  75.8 3.3 %inputs_last.1 = (bf16[48,96,256]{2,1,0:T(8,128)(2,1)}, bf16[12,24,256]{2,1,0:T(8,128)(2,1)}) custom-call(bf16[50,96,768]{2,1,0:T(8,128)(2,1)S(1)} %get-tuple-element.144.three_four, bf16[14,32,768]{2,1,0:T(8,128)(2,1)S(1)} %get-tuple-element.117.three_six, bf16[2304,256]{1,0:T(8,128)(2,1)S(1)} %get-tuple-element.133.turned, ...), custom_call_target="tpu_custom_call" | custom-call | flops 2310222592 | bytes 2359296 | tf_op jit(solution)/shard_map/inputs_last/pallas_call | solution.py:791
  79.2 0.1 broadcast_in_dim.11
  79.6 1.0 %copy-done.7 = f32[36,32,256]{2,1,0:T(8,128)} copy-done((f32[36,32,256]{2,1,0:T(8,128)}, f32[36,32,256]{2,1,0:T(8,128)S(1)}, u32[]{:S(2)}) %copy-start.7) | copy-done | bytes 1179672
  (57 shorter events, 0.4 us)
Async XLA Ops:
  0.7 2.3 %copy-start = (bf16[1,48,96,256]{3,2,1,0:T(8,128)(2,1)S(1)}, bf16[1,48,96,256]{3,2,1,0:T(8,128)(2,1)}, u32[]{:S(2)}) copy-start(bf16[1,48,96,256]{3,2,1,0:T(8,128)(2,1)} %param.7) | copy-start | bytes 7077892
  0.7 2.3 %copy-start.2 = (bf16[9,256,256]{2,1,0:T(8,128)(2,1)S(1)}, bf16[9,256,256]{2,1,0:T(8,128)(2,1)}, u32[]{:S(2)}) copy-start(bf16[9,256,256]{2,1,0:T(8,128)(2,1)} %w_ref.5) | copy-start | bytes 3538948
  0.7 2.3 %copy-start.3 = (bf16[1,12,24,256]{3,2,1,0:T(8,128)(2,1)S(1)}, bf16[1,12,24,256]{3,2,1,0:T(8,128)(2,1)}, u32[]{:S(2)}) copy-start(bf16[1,12,24,256]{3,2,1,0:T(8,128)(2,1)} %param.8) | copy-start | bytes 442372
  2.4 6.4 %collective-permute-start = (bf16[384,256]{1,0:T(8,128)(2,1)}, bf16[384,256]{1,0:T(8,128)(2,1)S(1)}, u32[]{:S(2)}, u32[]{:S(2)}) collective-permute-start(bf16[384,256]{1,0:T(8,128)(2,1)} %edges.1), channel_id=1, source_target_pairs={{0,1},{1,0},{2,3},{3,2},{4,5},{5,4},{6,7},{7,6},{8,9},{9,8},{10,11... | collective-permute-start | bytes 589832 | tf_op jit(solution)/shard_map/ppermute | solution.py:425
  9.6 1.2 %collective-permute-start.1 = (f32[4,256]{1,0:T(4,128)S(1)}, f32[4,256]{1,0:T(4,128)S(1)}, u32[]{:S(2)}, u32[]{:S(2)}) collective-permute-start(f32[4,256]{1,0:T(4,128)S(1)} %get-tuple-element.88), channel_id=1, source_target_pairs={{0,1},{1,0},{2,3},{3,2},{4,5},{5,4},{6,7},{7,6},{8,9},{9,8},{10,11... | collective-permute-start | bytes 12296 | tf_op jit(solution)/shard_map/ppermute | solution.py:425
  10.9 4.9 %collective-permute-start.2 = (f32[4,256]{1,0:T(4,128)S(1)}, f32[4,256]{1,0:T(4,128)S(1)}, u32[]{:S(2)}, u32[]{:S(2)}) collective-permute-start(f32[4,256]{1,0:T(4,128)S(1)} %add.124), channel_id=1, source_target_pairs={{0,7},{1,6},{2,5},{3,4},{4,3},{5,2},{6,1},{7,0},{8,15},{9,14},{10,... | collective-permute-start | bytes 12296 | tf_op jit(solution)/shard_map/ppermute | solution.py:495
  14.4 3.0 %collective-permute-start.3 = (f32[4,256]{1,0:T(4,128)S(1)}, f32[4,256]{1,0:T(4,128)S(1)}, u32[]{:S(2)}, u32[]{:S(2)}) collective-permute-start(f32[4,256]{1,0:T(4,128)S(1)} %add.124), channel_id=1, source_target_pairs={{0,5},{1,4},{2,7},{3,6},{4,1},{5,0},{6,3},{7,2},{8,13},{9,12},{10,... | collective-permute-start | bytes 12296 | tf_op jit(solution)/shard_map/ppermute | solution.py:495
  14.9 3.0 %collective-permute-start.4 = (f32[4,256]{1,0:T(4,128)S(1)}, f32[4,256]{1,0:T(4,128)S(1)}, u32[]{:S(2)}, u32[]{:S(2)}) collective-permute-start(f32[4,256]{1,0:T(4,128)S(1)} %add.124), channel_id=1, source_target_pairs={{0,3},{1,2},{2,1},{3,0},{4,7},{5,6},{6,5},{7,4},{8,11},{9,10},{10,... | collective-permute-start | bytes 12296 | tf_op jit(solution)/shard_map/ppermute | solution.py:495
  17.9 7.4 %copy-start.4 = (bf16[1,12,24,256]{3,2,1,0:T(8,128)(2,1)S(1)}, bf16[1,12,24,256]{3,2,1,0:T(8,128)(2,1)}, u32[]{:S(2)}) copy-start(bf16[1,12,24,256]{3,2,1,0:T(8,128)(2,1)} %param.13) | copy-start | bytes 442372
  17.9 7.4 %copy-start.5 = (f32[2,256]{1,0:T(2,128)S(1)}, f32[2,256]{1,0:T(2,128)}, u32[]{:S(2)}) copy-start(f32[2,256]{1,0:T(2,128)} %gain_ref.3) | copy-start | bytes 6148
  17.9 7.5 %copy-start.6 = (f32[2,256]{1,0:T(2,128)S(1)}, f32[2,256]{1,0:T(2,128)}, u32[]{:S(2)}) copy-start(f32[2,256]{1,0:T(2,128)} %shift_ref.3) | copy-start | bytes 6148
  17.9 5.0 %collective-permute-start.5 = (f32[4,256]{1,0:T(4,128)S(1)}, f32[4,256]{1,0:T(4,128)S(1)}, u32[]{:S(2)}, u32[]{:S(2)}) collective-permute-start(f32[4,256]{1,0:T(4,128)S(1)} %add_add_fusion.3), channel_id=1, source_target_pairs={{0,25},{1,24},{2,27},{3,26},{4,29},{5,28},{6,31},{7,30},{8,17},{9,... | collective-permute-start | bytes 12296 | tf_op jit(solution)/shard_map/ppermute | solution.py:495
  21.4 3.9 %collective-permute-start.6 = (f32[4,256]{1,0:T(4,128)S(1)}, f32[4,256]{1,0:T(4,128)S(1)}, u32[]{:S(2)}, u32[]{:S(2)}) collective-permute-start(f32[4,256]{1,0:T(4,128)S(1)} %add_add_fusion.3), channel_id=1, source_target_pairs={{0,17},{1,16},{2,19},{3,18},{4,21},{5,20},{6,23},{7,22},{8,25},{9,... | collective-permute-start | bytes 12296 | tf_op jit(solution)/shard_map/ppermute | solution.py:495
  21.4 3.9 %collective-permute-start.7 = (f32[4,256]{1,0:T(4,128)S(1)}, f32[4,256]{1,0:T(4,128)S(1)}, u32[]{:S(2)}, u32[]{:S(2)}) collective-permute-start(f32[4,256]{1,0:T(4,128)S(1)} %add_add_fusion.3), channel_id=1, source_target_pairs={{0,9},{1,8},{2,11},{3,10},{4,13},{5,12},{6,15},{7,14},{8,1},{9,0},... | collective-permute-start | bytes 12296 | tf_op jit(solution)/shard_map/ppermute | solution.py:495
  21.9 3.4 %copy-start.1 = (bf16[1,48,96,256]{3,2,1,0:T(8,128)(2,1)S(1)}, bf16[1,48,96,256]{3,2,1,0:T(8,128)(2,1)}, u32[]{:S(2)}) copy-start(bf16[1,48,96,256]{3,2,1,0:T(8,128)(2,1)} %param.12) | copy-start | bytes 7077892
  28.0 1.2 %collective-permute-start.8 = (f32[4,256]{1,0:T(4,128)S(1)}, f32[4,256]{1,0:T(4,128)S(1)}, u32[]{:S(2)}, u32[]{:S(2)}) collective-permute-start(f32[4,256]{1,0:T(4,128)S(1)} %get-tuple-element.107), channel_id=1, source_target_pairs={{0,1},{1,0},{2,3},{3,2},{4,5},{5,4},{6,7},{7,6},{8,9},{9,8},{10,11... | collective-permute-start | bytes 12296 | tf_op jit(solution)/shard_map/ppermute | solution.py:425
  29.2 3.1 %collective-permute-start.10 = (f32[4,256]{1,0:T(4,128)S(1)}, f32[4,256]{1,0:T(4,128)S(1)}, u32[]{:S(2)}, u32[]{:S(2)}) collective-permute-start(f32[4,256]{1,0:T(4,128)S(1)} %add.131), channel_id=1, source_target_pairs={{0,5},{1,4},{2,7},{3,6},{4,1},{5,0},{6,3},{7,2},{8,13},{9,12},{10,... | collective-permute-start | bytes 12296 | tf_op jit(solution)/shard_map/ppermute | solution.py:495
  30.7 3.0 %collective-permute-start.11 = (f32[4,256]{1,0:T(4,128)S(1)}, f32[4,256]{1,0:T(4,128)S(1)}, u32[]{:S(2)}, u32[]{:S(2)}) collective-permute-start(f32[4,256]{1,0:T(4,128)S(1)} %add.131), channel_id=1, source_target_pairs={{0,3},{1,2},{2,1},{3,0},{4,7},{5,6},{6,5},{7,4},{8,11},{9,10},{10,... | collective-permute-start | bytes 12296 | tf_op jit(solution)/shard_map/ppermute | solution.py:495
  31.0 3.9 %collective-permute-start.9 = (f32[4,256]{1,0:T(4,128)S(1)}, f32[4,256]{1,0:T(4,128)S(1)}, u32[]{:S(2)}, u32[]{:S(2)}) collective-permute-start(f32[4,256]{1,0:T(4,128)S(1)} %add.131), channel_id=1, source_target_pairs={{0,7},{1,6},{2,5},{3,4},{4,3},{5,2},{6,1},{7,0},{8,15},{9,14},{10,... | collective-permute-start | bytes 12296 | tf_op jit(solution)/shard_map/ppermute | solution.py:495
  35.0 4.8 %collective-permute-start.12 = (f32[4,256]{1,0:T(4,128)S(1)}, f32[4,256]{1,0:T(4,128)S(1)}, u32[]{:S(2)}, u32[]{:S(2)}) collective-permute-start(f32[4,256]{1,0:T(4,128)S(1)} %add_add_fusion.1), channel_id=1, source_target_pairs={{0,25},{1,24},{2,27},{3,26},{4,29},{5,28},{6,31},{7,30},{8,17},{9,... | collective-permute-start | bytes 12296 | tf_op jit(solution)/shard_map/ppermute | solution.py:495
  36.7 3.9 %collective-permute-start.13 = (f32[4,256]{1,0:T(4,128)S(1)}, f32[4,256]{1,0:T(4,128)S(1)}, u32[]{:S(2)}, u32[]{:S(2)}) collective-permute-start(f32[4,256]{1,0:T(4,128)S(1)} %add_add_fusion.1), channel_id=1, source_target_pairs={{0,17},{1,16},{2,19},{3,18},{4,21},{5,20},{6,23},{7,22},{8,25},{9,... | collective-permute-start | bytes 12296 | tf_op jit(solution)/shard_map/ppermute | solution.py:495
  36.8 3.8 %collective-permute-start.14 = (f32[4,256]{1,0:T(4,128)S(1)}, f32[4,256]{1,0:T(4,128)S(1)}, u32[]{:S(2)}, u32[]{:S(2)}) collective-permute-start(f32[4,256]{1,0:T(4,128)S(1)} %add_add_fusion.1), channel_id=1, source_target_pairs={{0,9},{1,8},{2,11},{3,10},{4,13},{5,12},{6,15},{7,14},{8,1},{9,0},... | collective-permute-start | bytes 12296 | tf_op jit(solution)/shard_map/ppermute | solution.py:495
  46.2 2.5 %collective-permute-start.15 = (f32[4,128,256]{2,1,0:T(8,128)S(1)}, f32[4,128,256]{2,1,0:T(8,128)S(1)}, u32[]{:S(2)}, u32[]{:S(2)}) collective-permute-start(f32[4,128,256]{2,1,0:T(8,128)S(1)} %bitcast.66), channel_id=1, source_target_pairs={{0,1},{1,0},{2,3},{3,2},{4,5},{5,4},{6,7},{7,6},{8,9},{9,8},{10,11... | collective-permute-start | bytes 1572872 | tf_op jit(solution)/shard_map/ppermute | solution.py:425
  48.7 4.0 %collective-permute-start.16 = (f32[5,128,256]{2,1,0:T(8,128)S(1)}, f32[5,128,256]{2,1,0:T(8,128)S(1)}, u32[]{:S(2)}, u32[]{:S(2)}) collective-permute-start(f32[5,128,256]{2,1,0:T(8,128)S(1)} %bitcast.65), channel_id=1, source_target_pairs={{0,1},{1,0},{2,3},{3,2},{4,5},{5,4},{6,7},{7,6},{8,9},{9,8},{10,11... | collective-permute-start | bytes 1966088 | tf_op jit(solution)/shard_map/ppermute | solution.py:425
  49.1 6.7 %collective-permute-start.20 = (bf16[128,256]{1,0:T(8,128)(2,1)S(1)}, bf16[128,256]{1,0:T(8,128)(2,1)S(1)}, u32[]{:S(2)}, u32[]{:S(2)}) collective-permute-start(bf16[128,256]{1,0:T(8,128)(2,1)S(1)} %get-tuple-element.170), channel_id=1, source_target_pairs={{0,6},{2,4},{4,2},{6,0},{8,14},{10,12},{12,10},{14,8},{16,22},{18,... | collective-permute-start | bytes 196616 | tf_op jit(solution)/shard_map/ppermute | solution.py:425
  50.6 5.9 %collective-permute-start.21 = (bf16[128,256]{1,0:T(8,128)(2,1)S(1)}, bf16[128,256]{1,0:T(8,128)(2,1)S(1)}, u32[]{:S(2)}, u32[]{:S(2)}) collective-permute-start(bf16[128,256]{1,0:T(8,128)(2,1)S(1)} %get-tuple-element.169), channel_id=1, source_target_pairs={{0,4},{2,6},{4,0},{6,2},{8,12},{10,14},{12,8},{14,10},{16,20},{18,... | collective-permute-start | bytes 196616 | tf_op jit(solution)/shard_map/ppermute | solution.py:425
  52.1 4.5 %collective-permute-start.22 = (bf16[128,256]{1,0:T(8,128)(2,1)S(1)}, bf16[128,256]{1,0:T(8,128)(2,1)S(1)}, u32[]{:S(2)}, u32[]{:S(2)}) collective-permute-start(bf16[128,256]{1,0:T(8,128)(2,1)S(1)} %get-tuple-element.168), channel_id=1, source_target_pairs={{0,2},{2,0},{4,6},{6,4},{8,10},{10,8},{12,14},{14,12},{16,18},{18,... | collective-permute-start | bytes 196616 | tf_op jit(solution)/shard_map/ppermute | solution.py:425
  52.7 6.3 %collective-permute-start.17 = (bf16[160,256]{1,0:T(8,128)(2,1)S(1)}, bf16[160,256]{1,0:T(8,128)(2,1)S(1)}, u32[]{:S(2)}, u32[]{:S(2)}) collective-permute-start(bf16[160,256]{1,0:T(8,128)(2,1)S(1)} %get-tuple-element.167), channel_id=1, source_target_pairs={{0,6},{2,4},{4,2},{6,0},{8,14},{10,12},{12,10},{14,8},{16,22},{18,... | collective-permute-start | bytes 245768 | tf_op jit(solution)/shard_map/ppermute | solution.py:425
  54.2 5.1 %collective-permute-start.18 = (bf16[160,256]{1,0:T(8,128)(2,1)S(1)}, bf16[160,256]{1,0:T(8,128)(2,1)S(1)}, u32[]{:S(2)}, u32[]{:S(2)}) collective-permute-start(bf16[160,256]{1,0:T(8,128)(2,1)S(1)} %get-tuple-element.166), channel_id=1, source_target_pairs={{0,4},{2,6},{4,0},{6,2},{8,12},{10,14},{12,8},{14,10},{16,20},{18,... | collective-permute-start | bytes 245768 | tf_op jit(solution)/shard_map/ppermute | solution.py:425
  55.8 4.4 %collective-permute-start.19 = (bf16[160,256]{1,0:T(8,128)(2,1)S(1)}, bf16[160,256]{1,0:T(8,128)(2,1)S(1)}, u32[]{:S(2)}, u32[]{:S(2)}) collective-permute-start(bf16[160,256]{1,0:T(8,128)(2,1)S(1)} %get-tuple-element.165), channel_id=1, source_target_pairs={{0,2},{2,0},{4,6},{6,4},{8,10},{10,8},{12,14},{14,12},{16,18},{18,... | collective-permute-start | bytes 245768 | tf_op jit(solution)/shard_map/ppermute | solution.py:425
  56.7 4.5 %collective-permute-start.24 = (bf16[128,256]{1,0:T(8,128)(2,1)S(1)}, bf16[128,256]{1,0:T(8,128)(2,1)S(1)}, u32[]{:S(2)}, u32[]{:S(2)}) collective-permute-start(bf16[128,256]{1,0:T(8,128)(2,1)S(1)} %fusion.3), channel_id=1, source_target_pairs={{0,9},{1,16},{2,11},{3,18},{4,13},{5,20},{6,15},{7,22},{8,25},{9,0... | collective-permute-start | bytes 196616 | tf_op jit(solution)/shard_map/ppermute | solution.py:572
  60.2 4.5 %collective-permute-start.23 = (bf16[160,256]{1,0:T(8,128)(2,1)S(1)}, bf16[160,256]{1,0:T(8,128)(2,1)S(1)}, u32[]{:S(2)}, u32[]{:S(2)}) collective-permute-start(bf16[160,256]{1,0:T(8,128)(2,1)S(1)} %fusion.1), channel_id=1, source_target_pairs={{0,9},{1,16},{2,11},{3,18},{4,13},{5,20},{6,15},{7,22},{8,25},{9,0... | collective-permute-start | bytes 245768 | tf_op jit(solution)/shard_map/ppermute | solution.py:572
  61.2 6.9 %collective-permute-start.27 = (bf16[128,256]{1,0:T(8,128)(2,1)S(1)}, bf16[128,256]{1,0:T(8,128)(2,1)S(1)}, u32[]{:S(2)}, u32[]{:S(2)}) collective-permute-start(bf16[128,256]{1,0:T(8,128)(2,1)S(1)} %add_convert_fusion.6), channel_id=1, source_target_pairs={{0,17},{1,8},{2,19},{3,10},{4,21},{5,12},{6,23},{7,14},{8,1},{9,24... | collective-permute-start | bytes 196616 | tf_op jit(solution)/shard_map/ppermute | solution.py:572
  64.7 7.2 %collective-permute-start.25 = (bf16[160,256]{1,0:T(8,128)(2,1)S(1)}, bf16[160,256]{1,0:T(8,128)(2,1)S(1)}, u32[]{:S(2)}, u32[]{:S(2)}) collective-permute-start(bf16[160,256]{1,0:T(8,128)(2,1)S(1)} %add_convert_fusion.1), channel_id=1, source_target_pairs={{0,17},{1,8},{2,19},{3,10},{4,21},{5,12},{6,23},{7,14},{8,1},{9,24... | collective-permute-start | bytes 245768 | tf_op jit(solution)/shard_map/ppermute | solution.py:572
  68.1 4.1 %collective-permute-start.31 = (bf16[128,256]{1,0:T(8,128)(2,1)S(1)}, bf16[128,256]{1,0:T(8,128)(2,1)S(1)}, u32[]{:S(2)}, u32[]{:S(2)}) collective-permute-start(bf16[128,256]{1,0:T(8,128)(2,1)S(1)} %add_convert_fusion.5), channel_id=1, source_target_pairs={{0,1},{1,0},{2,3},{3,2},{4,5},{5,4},{6,7},{7,6},{8,9},{9,8},{10,11... | collective-permute-start | bytes 196616 | tf_op jit(solution)/shard_map/ppermute | solution.py:425
  68.4 5.7 %collective-permute-start.28 = (bf16[128,256]{1,0:T(8,128)(2,1)S(1)}, bf16[128,256]{1,0:T(8,128)(2,1)S(1)}, u32[]{:S(2)}, u32[]{:S(2)}) collective-permute-start(bf16[128,256]{1,0:T(8,128)(2,1)S(1)} %add_convert_fusion.5), channel_id=1, source_target_pairs={{0,6},{1,7},{2,4},{3,5},{4,2},{5,3},{6,0},{7,1},{8,15},{9,14},{10,... | collective-permute-start | bytes 196616 | tf_op jit(solution)/shard_map/ppermute | solution.py:582
  69.3 9.9 %collective-permute-start.29 = (bf16[128,256]{1,0:T(8,128)(2,1)S(1)}, bf16[128,256]{1,0:T(8,128)(2,1)S(1)}, u32[]{:S(2)}, u32[]{:S(2)}) collective-permute-start(bf16[128,256]{1,0:T(8,128)(2,1)S(1)} %add_convert_fusion.5), channel_id=1, source_target_pairs={{0,4},{1,5},{2,6},{3,7},{4,0},{5,1},{6,2},{7,3},{8,13},{9,12},{10,... | collective-permute-start | bytes 196616 | tf_op jit(solution)/shard_map/ppermute | solution.py:582
  70.8 8.4 %collective-permute-start.30 = (bf16[128,256]{1,0:T(8,128)(2,1)S(1)}, bf16[128,256]{1,0:T(8,128)(2,1)S(1)}, u32[]{:S(2)}, u32[]{:S(2)}) collective-permute-start(bf16[128,256]{1,0:T(8,128)(2,1)S(1)} %add_convert_fusion.5), channel_id=1, source_target_pairs={{0,2},{1,3},{2,0},{3,1},{4,6},{5,7},{6,4},{7,5},{8,11},{9,10},{10,... | collective-permute-start | bytes 196616 | tf_op jit(solution)/shard_map/ppermute | solution.py:582
  71.9 2.8 %collective-permute-start.26 = (bf16[160,256]{1,0:T(8,128)(2,1)S(1)}, bf16[160,256]{1,0:T(8,128)(2,1)S(1)}, u32[]{:S(2)}, u32[]{:S(2)}) collective-permute-start(bf16[160,256]{1,0:T(8,128)(2,1)S(1)} %add_convert_fusion), channel_id=1, source_target_pairs={{0,1},{1,0},{2,3},{3,2},{4,5},{5,4},{6,7},{7,6},{8,9},{9,8},{10,11... | collective-permute-start | bytes 245768 | tf_op jit(solution)/shard_map/ppermute | solution.py:425
  72.3 7.1 %collective-permute-start.32 = (bf16[160,256]{1,0:T(8,128)(2,1)S(1)}, bf16[160,256]{1,0:T(8,128)(2,1)S(1)}, u32[]{:S(2)}, u32[]{:S(2)}) collective-permute-start(bf16[160,256]{1,0:T(8,128)(2,1)S(1)} %add_convert_fusion), channel_id=1, source_target_pairs={{0,6},{1,7},{2,4},{3,5},{4,2},{5,3},{6,0},{7,1},{8,15},{9,14},{10,... | collective-permute-start | bytes 245768 | tf_op jit(solution)/shard_map/ppermute | solution.py:582
  74.1 5.3 %collective-permute-start.33 = (bf16[160,256]{1,0:T(8,128)(2,1)S(1)}, bf16[160,256]{1,0:T(8,128)(2,1)S(1)}, u32[]{:S(2)}, u32[]{:S(2)}) collective-permute-start(bf16[160,256]{1,0:T(8,128)(2,1)S(1)} %add_convert_fusion), channel_id=1, source_target_pairs={{0,4},{1,5},{2,6},{3,7},{4,0},{5,1},{6,2},{7,3},{8,13},{9,12},{10,... | collective-permute-start | bytes 245768 | tf_op jit(solution)/shard_map/ppermute | solution.py:582
  74.7 4.7 %collective-permute-start.34 = (bf16[160,256]{1,0:T(8,128)(2,1)S(1)}, bf16[160,256]{1,0:T(8,128)(2,1)S(1)}, u32[]{:S(2)}, u32[]{:S(2)}) collective-permute-start(bf16[160,256]{1,0:T(8,128)(2,1)S(1)} %add_convert_fusion), channel_id=1, source_target_pairs={{0,2},{1,3},{2,0},{3,1},{4,6},{5,7},{6,4},{7,5},{8,11},{9,10},{10,... | collective-permute-start | bytes 245768 | tf_op jit(solution)/shard_map/ppermute | solution.py:582
  79.5 1.0 %copy-start.7 = (f32[36,32,256]{2,1,0:T(8,128)}, f32[36,32,256]{2,1,0:T(8,128)S(1)}, u32[]{:S(2)}) copy-start(f32[36,32,256]{2,1,0:T(8,128)S(1)} %convert_dynamic-update-slice_fusion) | copy-start | bytes 3538948

commit v2 on v1

--- a/solution.py
+++ b/solution.py
@@ -389,33 +389,33 @@
             sent(index, start, end)
 
 
-def input_kernel(chunks, three_four, turned, grad_ref):
+def input_kernel(chunks, three_four, three_six, turned, grad_ref, *six_refs):
+    for six_ref in six_refs:
+        input_chunks(three_six, turned, six_ref, [(0, six_ref.shape[0])], 0)
     input_chunks(three_four, turned, grad_ref, chunks, chunks[0][0])
 
 
-def input_last_kernel(chunks, bounds, three_four, three_six, turned, *rest):
+def input_last_kernel(chunks, bounds, three_four, turned, six_ref, *rest):
     count = len(bounds) - 1
     earlier, rest = rest[:count], rest[count:]
-    grad_four_ref, grad_six_ref, grad_four, grad_six, sems, sems_four, sems_six = rest
-    copies = [
+    grad_four_ref, grad_six_ref, grad_four, sems, sems_four = rest
+    copies = [pltpu.make_async_copy(six_ref, grad_six_ref, sems.at[count])]
+    copies += [
         pltpu.make_async_copy(part, grad_four_ref.at[bounds[index] : bounds[index + 1]], sems.at[index])
         for index, part in enumerate(earlier)
     ]
     for copy in copies:
         copy.start()
-
-    def sender(grad, grad_ref, offset, sems):
-        def sent(index, start, end):
-            copy = pltpu.make_async_copy(grad.at[start - offset : end - offset], grad_ref.at[start:end], sems.at[index])
-            copy.start()
-            copies.append(copy)
-
-        return sent
-
-    six_chunks = chunks_of(grad_six.shape[0], 12)
-    input_chunks(three_six, turned, grad_six, six_chunks, 0, sender(grad_six, grad_six_ref, 0, sems_six))
     done = bounds[-1]
-    input_chunks(three_four, turned, grad_four, chunks, done, sender(grad_four, grad_four_ref, done, sems_four))
+
+    def sent(index, start, end):
+        copy = pltpu.make_async_copy(
+            grad_four.at[start - done : end - done], grad_four_ref.at[start:end], sems_four.at[index]
+        )
+        copy.start()
+        copies.append(copy)
+
+    input_chunks(three_four, turned, grad_four, chunks, done, sent)
     for copy in copies:
         copy.wait()
 
@@ -742,16 +742,20 @@
     groups = [chunks[low:high] for low, high in zip(cuts[:-1], cuts[1:]) if low < high]
     bounds = [group[0][0] for group in groups]
 
-    def inputs(group, three):
+    def inputs(number, three):
+        group = groups[number]
+        parts = (jax.ShapeDtypeStruct((group[-1][1] - group[0][0], cols_four, chan), BF16),)
+        if number == len(groups) - 2:
+            parts += (jax.ShapeDtypeStruct(six.shape, BF16),)
         return pl.pallas_call(
             functools.partial(input_kernel, group),
-            out_shape=jax.ShapeDtypeStruct((group[-1][1] - group[0][0], cols_four, chan), BF16),
-            in_specs=[vmem] * 2,
-            out_specs=vmem,
+            out_shape=parts,
+            in_specs=[vmem] * 3,
+            out_specs=(vmem,) * len(parts),
             compiler_params=params,
             cost_estimate=cost(0.3, four.size),
             name="inputs",
-        )(three, turned_weight)
+        )(three, three_six, turned_weight)
 
     grad_gain, grad_shift = every_group(grad_gain), every_group(grad_shift)
 
@@ -764,8 +768,9 @@
     piece_a = added(piece_a, met_a).astype(BF16)
     piece_a, three_four = lax.optimization_barrier((piece_a, three_four))
     met_a = swap_high(piece_a, RADIX, 2 * RADIX)
-    earlier = [inputs(groups[0], three_four)] if len(groups) > 1 else []
-    met_b, earlier = lax.optimization_barrier((met_b, earlier))
+    earlier = list(inputs(0, three_four))
+    whole = jnp.zeros((9 * RADIX, share // RADIX, chan), F32)
+    met_b, earlier, whole = lax.optimization_barrier((met_b, earlier, whole))
 
     piece_b = added(piece_b, met_b).astype(BF16)
     met_b = swap_high(piece_b, RADIX, 2 * RADIX)
@@ -775,7 +780,7 @@
     piece_a, three_four = lax.optimization_barrier((piece_a, three_four))
     met_a = swap_high(piece_a, 2 * RADIX, RADIX)
     if len(groups) > 2:
-        earlier = earlier + [inputs(groups[1], three_four)]
+        earlier = earlier + list(inputs(1, three_four))
     met_b, earlier = lax.optimization_barrier((met_b, earlier))
 
     piece_b = both(piece_b, met_b)
@@ -794,21 +799,18 @@
             jax.ShapeDtypeStruct(four.shape, BF16),
             jax.ShapeDtypeStruct(six.shape, BF16),
         ),
-        in_specs=[vmem] * (3 + len(earlier)),
+        in_specs=[vmem] * (2 + len(earlier)),
         out_specs=(hbm, hbm),
         scratch_shapes=[
             pltpu.VMEM((rows_four - done, cols_four, chan), BF16),
-            pltpu.VMEM(six.shape, BF16),
             pltpu.SemaphoreType.DMA((len(groups),)),
             pltpu.SemaphoreType.DMA((len(chunks),)),
-            pltpu.SemaphoreType.DMA((len(chunks_of(rows_six, 12)),)),
         ],
         compiler_params=params,
         cost_estimate=cost(0.4, 2 * four.size),
         name="inputs_last",
-    )(three_four, three_six, turned_weight, *earlier)
+    )(three_four, turned_weight, earlier[-1], *earlier[:-1])
     pieces_a, grad_six = lax.optimization_barrier((pieces_a, grad_six))
-    whole = jnp.zeros((9 * RADIX, share // RADIX, chan), F32)
     whole = put_pieces(whole, pieces_a, found.first)
     whole = put_pieces(whole, pieces_b, found.second)
     grad_weight = whole.reshape(9, share, chan)

time: 80.8 us -> 80.5 us (level)
  transfers between devices with their start and end apart: 35 -> 35, of which waited for: 16 -> 17; matrix products, arithmetic and copies ran while one was open for 1% -> 1% of each run, Pallas kernels for 20% -> 21%
where the time goes in v2:
time: 80.5 us; the launch traced here: 80.3 us
  starting transfers between devices  34.6 us (43%)
  Pallas kernels  27.2 us (34%)
  waiting for transfers between devices  15.9 us (20%)
  local copies, waits for them, and re-layouts  1.16 us (1%)
  between operations  1.02 us (1%)
    ppermute x12, starting transfers between devices, swap_across(): return lax.ppermute(array, ('rep', 'sp'), pairs)  15.2 us
    ppermute x13, starting transfers between devices, swap(): return lax.ppermute(array, axis, [(i, i ^ stride) for i in range(count)])  9.75 us
    ppermute x12, waiting for transfers between devices, swap_across(): return lax.ppermute(array, ('rep', 'sp'), pairs)  9.51 us
    ppermute x6, starting transfers between devices, bring(): return lax.ppermute(array, ('rep', 'sp'), pairs)  6.1 us
    pallas_call x1, Pallas kernels, local(): pl.pallas_call(inner_kernel, out_shape=(jax.ShapeDtypeStruct((rows_four -...  5.87 us
    pallas_call x1, Pallas kernels, local(): pl.pallas_call(functools.partial(backward_kernel, counts, sp_count, (cols...  5.51 us
    pallas_call x2, Pallas kernels, inputs(): pl.pallas_call(functools.partial(input_kernel, group), out_shape=parts, i...  4.43 us
    ppermute x4, starting transfers between devices, swap_high(): return lax.ppermute(array, ('rep', 'sp'), pairs)  3.49 us
  transfers between devices with their start and end apart: 35, of which 17 were waited for; matrix products, arithmetic and copies ran while one was open for 1% of the time, Pallas kernels for 21%

profile of v2, /device:TPU:0, one launch (start us, length us, event | category | flops | bytes accessed | tf_op | source)
XLA Modules:
  0.0 80.3 jit_solution(3536283537065083725)
XLA Ops:
  0.7 1.7 %edges.1 = bf16[384,256]{1,0:T(8,128)(2,1)} custom-call(bf16[48,96,256]{2,1,0:T(8,128)(2,1)} %bitcast.51, bf16[12,24,256]{2,1,0:T(8,128)(2,1)} %bitcast.59, bf16[48,96,256]{2,1,0:T(8,128)(2,1)} %bitcast.55, bf16[12,24,256]{2,1,0:T(8,128)(2,1)} %bitcast.63), custom_call_target="tpu_custom_call" | custom-call | tf_op jit(solution)/shard_map/edges/pallas_call | solution.py:467
  2.4 0.5 collective-permute-start
  3.0 5.9 %forward_inner.1 = (bf16[46,96,256]{2,1,0:T(8,128)(2,1)S(1)}, bf16[10,32,256]{2,1,0:T(8,128)(2,1)S(1)}, f32[4,256]{1,0:T(4,128)S(1)}) custom-call(bf16[48,96,256]{2,1,0:T(8,128)(2,1)S(1)} %bitcast.52, bf16[12,24,256]{2,1,0:T(8,128)(2,1)S(1)} %bitcast.60, bf16[9,256,256]{2,1,0:T(8,128)(2,1)S(1)} %copy-done.2), custom_call_target="tpu_custom_call" | custom-call | flops 5775556608 | bytes 4718592 | tf_op jit(solution)/shard_map/forward_inner/pallas_call | solution.py:633
  8.9 0.8 forward_outer.1
  9.6 0.4 collective-permute-start.1
  10.0 0.8 %collective-permute-done.1 = f32[4,256]{1,0:T(4,128)S(1)} collective-permute-done((f32[4,256]{1,0:T(4,128)S(1)}, f32[4,256]{1,0:T(4,128)S(1)}, u32[]{:S(2)}, u32[]{:S(2)}) %collective-permute-start.1) | collective-permute-done | bytes 4128 | tf_op jit(solution)/shard_map/ppermute | solution.py:425
  10.9 3.6 %collective-permute-start.2 = (f32[4,256]{1,0:T(4,128)S(1)}, f32[4,256]{1,0:T(4,128)S(1)}, u32[]{:S(2)}, u32[]{:S(2)}) collective-permute-start(f32[4,256]{1,0:T(4,128)S(1)} %add.124), channel_id=1, source_target_pairs={{0,7},{1,6},{2,5},{3,4},{4,3},{5,2},{6,1},{7,0},{8,15},{9,14},{10,... | collective-permute-start | bytes 12296 | tf_op jit(solution)/shard_map/ppermute | solution.py:495
  14.4 0.4 collective-permute-start.3
  14.9 0.1 collective-permute-start.4
  14.9 0.8 %collective-permute-done.2 = f32[4,256]{1,0:T(4,128)S(1)} collective-permute-done((f32[4,256]{1,0:T(4,128)S(1)}, f32[4,256]{1,0:T(4,128)S(1)}, u32[]{:S(2)}, u32[]{:S(2)}) %collective-permute-start.2) | collective-permute-done | bytes 4128 | tf_op jit(solution)/shard_map/ppermute | solution.py:495
  15.8 1.7 %collective-permute-done.3 = f32[4,256]{1,0:T(4,128)S(1)} collective-permute-done((f32[4,256]{1,0:T(4,128)S(1)}, f32[4,256]{1,0:T(4,128)S(1)}, u32[]{:S(2)}, u32[]{:S(2)}) %collective-permute-start.3) | collective-permute-done | bytes 4128 | tf_op jit(solution)/shard_map/ppermute | solution.py:495
  17.5 0.4 collective-permute-done.4
  17.9 3.5 %collective-permute-start.5 = (f32[4,256]{1,0:T(4,128)S(1)}, f32[4,256]{1,0:T(4,128)S(1)}, u32[]{:S(2)}, u32[]{:S(2)}) collective-permute-start(f32[4,256]{1,0:T(4,128)S(1)} %add_add_fusion.3), channel_id=1, source_target_pairs={{0,25},{1,24},{2,27},{3,26},{4,29},{5,28},{6,31},{7,30},{8,17},{9,... | collective-permute-start | bytes 12296 | tf_op jit(solution)/shard_map/ppermute | solution.py:495
  21.4 0.6 collective-permute-start.7
  21.9 1.0 %turn.1 = (bf16[256,4992]{1,0:T(8,128)(2,1)S(1)}, bf16[2304,256]{1,0:T(8,128)(2,1)S(1)}) custom-call(bf16[48,96,256]{2,1,0:T(8,128)(2,1)S(1)} %bitcast.54, bf16[12,24,256]{2,1,0:T(8,128)(2,1)S(1)} %bitcast.62, bf16[9,256,256]{2,1,0:T(8,128)(2,1)S(1)} %copy-done.2), custom_call_target="tpu_custom_call" | custom-call | flops 1732667008 | bytes 4718592 | tf_op jit(solution)/shard_map/turn/pallas_call | solution.py:668
  23.0 2.4 %collective-permute-done.6 = f32[4,256]{1,0:T(4,128)S(1)} collective-permute-done((f32[4,256]{1,0:T(4,128)S(1)}, f32[4,256]{1,0:T(4,128)S(1)}, u32[]{:S(2)}, u32[]{:S(2)}) %collective-permute-start.6) | collective-permute-done | bytes 4128 | tf_op jit(solution)/shard_map/ppermute | solution.py:495
  25.4 2.6 %slopes.1 = (f32[50,96,256]{2,1,0:T(8,128)S(1)}, f32[14,32,256]{2,1,0:T(8,128)S(1)}, f32[4,256]{1,0:T(4,128)S(1)}) custom-call(bf16[46,96,256]{2,1,0:T(8,128)(2,1)S(1)} %get-tuple-element.104.inner_four_ref, bf16[10,32,256]{2,1,0:T(8,128)(2,1)S(1)} %get-tuple-element.105.inner_six_ref, bf16[4,96,256]{2,1,0:T(8,128)(2,1)S(1)} %get-tuple-element.106.outer_four_ref, ...), custom_call_target="tpu_custom_call" | custom-call | flops 57755568 | bytes 4718592 | tf_op jit(solution)/shard_map/slopes/pallas_call | solution.py:682
  28.0 0.4 collective-permute-start.8
  28.4 0.9 %collective-permute-done.8 = f32[4,256]{1,0:T(4,128)S(1)} collective-permute-done((f32[4,256]{1,0:T(4,128)S(1)}, f32[4,256]{1,0:T(4,128)S(1)}, u32[]{:S(2)}, u32[]{:S(2)}) %collective-permute-start.8) | collective-permute-done | bytes 4128 | tf_op jit(solution)/shard_map/ppermute | solution.py:425
  29.2 1.4 %collective-permute-start.10 = (f32[4,256]{1,0:T(4,128)S(1)}, f32[4,256]{1,0:T(4,128)S(1)}, u32[]{:S(2)}, u32[]{:S(2)}) collective-permute-start(f32[4,256]{1,0:T(4,128)S(1)} %add.131), channel_id=1, source_target_pairs={{0,5},{1,4},{2,7},{3,6},{4,1},{5,0},{6,3},{7,2},{8,13},{9,12},{10,... | collective-permute-start | bytes 12296 | tf_op jit(solution)/shard_map/ppermute | solution.py:495
  30.7 0.3 collective-permute-start.11
  31.0 1.3 %collective-permute-start.9 = (f32[4,256]{1,0:T(4,128)S(1)}, f32[4,256]{1,0:T(4,128)S(1)}, u32[]{:S(2)}, u32[]{:S(2)}) collective-permute-start(f32[4,256]{1,0:T(4,128)S(1)} %add.131), channel_id=1, source_target_pairs={{0,7},{1,6},{2,5},{3,4},{4,3},{5,2},{6,1},{7,0},{8,15},{9,14},{10,... | collective-permute-start | bytes 12296 | tf_op jit(solution)/shard_map/ppermute | solution.py:495
  32.4 1.3 %collective-permute-done.11 = f32[4,256]{1,0:T(4,128)S(1)} collective-permute-done((f32[4,256]{1,0:T(4,128)S(1)}, f32[4,256]{1,0:T(4,128)S(1)}, u32[]{:S(2)}, u32[]{:S(2)}) %collective-permute-start.11) | collective-permute-done | bytes 4128 | tf_op jit(solution)/shard_map/ppermute | solution.py:495
  33.7 1.2 %collective-permute-done.9 = f32[4,256]{1,0:T(4,128)S(1)} collective-permute-done((f32[4,256]{1,0:T(4,128)S(1)}, f32[4,256]{1,0:T(4,128)S(1)}, u32[]{:S(2)}, u32[]{:S(2)}) %collective-permute-start.9) | collective-permute-done | bytes 4128 | tf_op jit(solution)/shard_map/ppermute | solution.py:495
  35.0 1.7 %collective-permute-start.12 = (f32[4,256]{1,0:T(4,128)S(1)}, f32[4,256]{1,0:T(4,128)S(1)}, u32[]{:S(2)}, u32[]{:S(2)}) collective-permute-start(f32[4,256]{1,0:T(4,128)S(1)} %add_add_fusion.1), channel_id=1, source_target_pairs={{0,25},{1,24},{2,27},{3,26},{4,29},{5,28},{6,31},{7,30},{8,17},{9,... | collective-permute-start | bytes 12296 | tf_op jit(solution)/shard_map/ppermute | solution.py:495
  36.7 0.1 collective-permute-start.13
  36.8 2.2 %collective-permute-start.14 = (f32[4,256]{1,0:T(4,128)S(1)}, f32[4,256]{1,0:T(4,128)S(1)}, u32[]{:S(2)}, u32[]{:S(2)}) collective-permute-start(f32[4,256]{1,0:T(4,128)S(1)} %add_add_fusion.1), channel_id=1, source_target_pairs={{0,9},{1,8},{2,11},{3,10},{4,13},{5,12},{6,15},{7,14},{8,1},{9,0},... | collective-permute-start | bytes 12296 | tf_op jit(solution)/shard_map/ppermute | solution.py:495
  39.0 0.8 %collective-permute-done.12 = f32[4,256]{1,0:T(4,128)S(1)} collective-permute-done((f32[4,256]{1,0:T(4,128)S(1)}, f32[4,256]{1,0:T(4,128)S(1)}, u32[]{:S(2)}, u32[]{:S(2)}) %collective-permute-start.12) | collective-permute-done | bytes 4128 | tf_op jit(solution)/shard_map/ppermute | solution.py:495
  39.8 0.8 %collective-permute-done.13 = f32[4,256]{1,0:T(4,128)S(1)} collective-permute-done((f32[4,256]{1,0:T(4,128)S(1)}, f32[4,256]{1,0:T(4,128)S(1)}, u32[]{:S(2)}, u32[]{:S(2)}) %collective-permute-start.13) | collective-permute-done | bytes 4128 | tf_op jit(solution)/shard_map/ppermute | solution.py:495
  40.6 5.5 %backward.1 = (bf16[50,96,768]{2,1,0:T(8,128)(2,1)S(1)}, bf16[14,32,768]{2,1,0:T(8,128)(2,1)S(1)}, f32[4,128,256]{2,1,0:T(8,128)S(1)}, f32[1,4,128,256]{3,2,1,0:...) custom-call(bf16[256,4992]{1,0:T(8,128)(2,1)S(1)} %get-tuple-element.103.turned_ref, ...), custom_call_target="tpu_custom_call" | custom-call | flops 3465334016 | bytes 9437184 | tf_op jit(solution)/shard_map/backward/pallas_call | solution.py:709
  46.1 0.2 collective-permute-start.15
  46.3 2.3 %weights.1 = (f32[5,128,256]{2,1,0:T(8,128)S(1)}, f32[1,5,128,256]{3,2,1,0:T(8,128)S(1)}) custom-call(bf16[256,4992]{1,0:T(8,128)(2,1)S(1)} %get-tuple-element.103.turned_ref, bf16[50,96,768]{2,1,0:T(8,128)(2,1)S(1)} %get-tuple-element.150.three_four, bf16[14,32,768]{2,1,0:T(8,128)(2,1)S(1)} %get-tuple-element.121.three_six, ...), custom_call_target="tpu_custom_call" | custom-call | flops 3465334016 | bytes 9437184 | tf_op jit(solution)/shard_map/weights/pallas_call | solution.py:727
  48.6 0.4 collective-permute-start.16
  49.0 1.5 %collective-permute-start.20 = (bf16[128,256]{1,0:T(8,128)(2,1)S(1)}, bf16[128,256]{1,0:T(8,128)(2,1)S(1)}, u32[]{:S(2)}, u32[]{:S(2)}) collective-permute-start(bf16[128,256]{1,0:T(8,128)(2,1)S(1)} %get-tuple-element.178), channel_id=1, source_target_pairs={{0,6},{2,4},{4,2},{6,0},{8,14},{10,12},{12,10},{14,8},{16,22},{18,... | collective-permute-start | bytes 196616 | tf_op jit(solution)/shard_map/ppermute | solution.py:425
  50.5 1.5 %collective-permute-start.21 = (bf16[128,256]{1,0:T(8,128)(2,1)S(1)}, bf16[128,256]{1,0:T(8,128)(2,1)S(1)}, u32[]{:S(2)}, u32[]{:S(2)}) collective-permute-start(bf16[128,256]{1,0:T(8,128)(2,1)S(1)} %get-tuple-element.177), channel_id=1, source_target_pairs={{0,4},{2,6},{4,0},{6,2},{8,12},{10,14},{12,8},{14,10},{16,20},{18,... | collective-permute-start | bytes 196616 | tf_op jit(solution)/shard_map/ppermute | solution.py:425
  52.0 0.5 collective-permute-start.22
  52.6 0.1 fusion.6
  52.7 1.5 %collective-permute-start.17 = (bf16[160,256]{1,0:T(8,128)(2,1)S(1)}, bf16[160,256]{1,0:T(8,128)(2,1)S(1)}, u32[]{:S(2)}, u32[]{:S(2)}) collective-permute-start(bf16[160,256]{1,0:T(8,128)(2,1)S(1)} %get-tuple-element.175), channel_id=1, source_target_pairs={{0,6},{2,4},{4,2},{6,0},{8,14},{10,12},{12,10},{14,8},{16,22},{18,... | collective-permute-start | bytes 245768 | tf_op jit(solution)/shard_map/ppermute | solution.py:425
  54.2 1.5 %collective-permute-start.18 = (bf16[160,256]{1,0:T(8,128)(2,1)S(1)}, bf16[160,256]{1,0:T(8,128)(2,1)S(1)}, u32[]{:S(2)}, u32[]{:S(2)}) collective-permute-start(bf16[160,256]{1,0:T(8,128)(2,1)S(1)} %get-tuple-element.174), channel_id=1, source_target_pairs={{0,4},{2,6},{4,0},{6,2},{8,12},{10,14},{12,8},{14,10},{16,20},{18,... | collective-permute-start | bytes 245768 | tf_op jit(solution)/shard_map/ppermute | solution.py:425
  55.7 0.7 collective-permute-start.19
  56.4 0.2 collective-permute-done.22
  56.6 0.3 collective-permute-start.24
  56.9 2.0 %inputs.2.rest_0_ = bf16[16,96,256]{2,1,0:T(8,128)(2,1)S(1)} custom-call(bf16[50,96,768]{2,1,0:T(8,128)(2,1)S(1)} %get-tuple-element.150.three_four, bf16[14,32,768]{2,1,0:T(8,128)(2,1)S(1)} %get-tuple-element.121.three_six, bf16[2304,256]{1,0:T(8,128)(2,1)S(1)} %get-tuple-element.137.turned), custom_call_target="tpu_custom_call" | custom-call | flops 1732667008 | bytes 1179648 | tf_op jit(solution)/shard_map/inputs/pallas_call | solution.py:750
  58.9 0.3 collective-permute-done.18
  59.2 0.9 %collective-permute-done.19 = bf16[160,256]{1,0:T(8,128)(2,1)S(1)} collective-permute-done((bf16[160,256]{1,0:T(8,128)(2,1)S(1)}, bf16[160,256]{1,0:T(8,128)(2,1)S(1)}, u32[]{:S(2)}, u32[]{:S(2)}) %collective-permute-start.19) | collective-permute-done | bytes 81952 | tf_op jit(solution)/shard_map/ppermute | solution.py:425
  60.2 0.4 collective-permute-start.23
  60.6 0.5 collective-permute-done.24
  61.1 1.6 %collective-permute-start.27 = (bf16[128,256]{1,0:T(8,128)(2,1)S(1)}, bf16[128,256]{1,0:T(8,128)(2,1)S(1)}, u32[]{:S(2)}, u32[]{:S(2)}) collective-permute-start(bf16[128,256]{1,0:T(8,128)(2,1)S(1)} %add_convert_fusion.6), channel_id=1, source_target_pairs={{0,17},{1,8},{2,19},{3,10},{4,21},{5,12},{6,23},{7,14},{8,1},{9,24... | collective-permute-start | bytes 196616 | tf_op jit(solution)/shard_map/ppermute | solution.py:572
  62.6 2.5 %inputs.3 = (bf16[16,96,256]{2,1,0:T(8,128)(2,1)S(1)}, bf16[12,24,256]{2,1,0:T(8,128)(2,1)S(1)}) custom-call(bf16[50,96,768]{2,1,0:T(8,128)(2,1)S(1)} %get-tuple-element.150.three_four, bf16[14,32,768]{2,1,0:T(8,128)(2,1)S(1)} %get-tuple-element.121.three_six, bf16[2304,256]{1,0:T(8,128)(2,1)S(1)} %get-tuple-element.137.turned), custom_call_target="tpu_custom_call" | custom-call | flops 1732667008 | bytes 1179648 | tf_op jit(solution)/shard_map/inputs/pallas_call | solution.py:750
  65.1 1.2 %collective-permute-start.25 = (bf16[160,256]{1,0:T(8,128)(2,1)S(1)}, bf16[160,256]{1,0:T(8,128)(2,1)S(1)}, u32[]{:S(2)}, u32[]{:S(2)}) collective-permute-start(bf16[160,256]{1,0:T(8,128)(2,1)S(1)} %add_convert_fusion.1), channel_id=1, source_target_pairs={{0,17},{1,8},{2,19},{3,10},{4,21},{5,12},{6,23},{7,14},{8,1},{9,24... | collective-permute-start | bytes 245768 | tf_op jit(solution)/shard_map/ppermute | solution.py:572
  66.4 1.7 %collective-permute-done.27 = bf16[128,256]{1,0:T(8,128)(2,1)S(1)} collective-permute-done((bf16[128,256]{1,0:T(8,128)(2,1)S(1)}, bf16[128,256]{1,0:T(8,128)(2,1)S(1)}, u32[]{:S(2)}, u32[]{:S(2)}) %collective-permute-start.27) | collective-permute-done | bytes 65568 | tf_op jit(solution)/shard_map/ppermute | solution.py:572
  68.0 0.3 collective-permute-start.31
  68.3 0.9 %collective-permute-start.28 = (bf16[128,256]{1,0:T(8,128)(2,1)S(1)}, bf16[128,256]{1,0:T(8,128)(2,1)S(1)}, u32[]{:S(2)}, u32[]{:S(2)}) collective-permute-start(bf16[128,256]{1,0:T(8,128)(2,1)S(1)} %add_convert_fusion.5), channel_id=1, source_target_pairs={{0,6},{1,7},{2,4},{3,5},{4,2},{5,3},{6,0},{7,1},{8,15},{9,14},{10,... | collective-permute-start | bytes 196616 | tf_op jit(solution)/shard_map/ppermute | solution.py:582
  69.2 1.5 %collective-permute-start.29 = (bf16[128,256]{1,0:T(8,128)(2,1)S(1)}, bf16[128,256]{1,0:T(8,128)(2,1)S(1)}, u32[]{:S(2)}, u32[]{:S(2)}) collective-permute-start(bf16[128,256]{1,0:T(8,128)(2,1)S(1)} %add_convert_fusion.5), channel_id=1, source_target_pairs={{0,4},{1,5},{2,6},{3,7},{4,0},{5,1},{6,2},{7,3},{8,13},{9,12},{10,... | collective-permute-start | bytes 196616 | tf_op jit(solution)/shard_map/ppermute | solution.py:582
  70.7 1.1 %collective-permute-start.30 = (bf16[128,256]{1,0:T(8,128)(2,1)S(1)}, bf16[128,256]{1,0:T(8,128)(2,1)S(1)}, u32[]{:S(2)}, u32[]{:S(2)}) collective-permute-start(bf16[128,256]{1,0:T(8,128)(2,1)S(1)} %add_convert_fusion.5), channel_id=1, source_target_pairs={{0,2},{1,3},{2,0},{3,1},{4,6},{5,7},{6,4},{7,5},{8,11},{9,10},{10,... | collective-permute-start | bytes 196616 | tf_op jit(solution)/shard_map/ppermute | solution.py:582
  71.9 0.3 collective-permute-start.26
  72.2 0.9 %collective-permute-start.32 = (bf16[160,256]{1,0:T(8,128)(2,1)S(1)}, bf16[160,256]{1,0:T(8,128)(2,1)S(1)}, u32[]{:S(2)}, u32[]{:S(2)}) collective-permute-start(bf16[160,256]{1,0:T(8,128)(2,1)S(1)} %add_convert_fusion), channel_id=1, source_target_pairs={{0,6},{1,7},{2,4},{3,5},{4,2},{5,3},{6,0},{7,1},{8,15},{9,14},{10,... | collective-permute-start | bytes 245768 | tf_op jit(solution)/shard_map/ppermute | solution.py:582
  73.1 0.9 %collective-permute-done.28 = bf16[128,256]{1,0:T(8,128)(2,1)S(1)} collective-permute-done((bf16[128,256]{1,0:T(8,128)(2,1)S(1)}, bf16[128,256]{1,0:T(8,128)(2,1)S(1)}, u32[]{:S(2)}, u32[]{:S(2)}) %collective-permute-start.28) | collective-permute-done | bytes 65568 | tf_op jit(solution)/shard_map/ppermute | solution.py:582
  74.1 0.6 collective-permute-start.33
  74.6 1.1 %collective-permute-start.34 = (bf16[160,256]{1,0:T(8,128)(2,1)S(1)}, bf16[160,256]{1,0:T(8,128)(2,1)S(1)}, u32[]{:S(2)}, u32[]{:S(2)}) collective-permute-start(bf16[160,256]{1,0:T(8,128)(2,1)S(1)} %add_convert_fusion), channel_id=1, source_target_pairs={{0,2},{1,3},{2,0},{3,1},{4,6},{5,7},{6,4},{7,5},{8,11},{9,10},{10,... | collective-permute-start | bytes 245768 | tf_op jit(solution)/shard_map/ppermute | solution.py:582
  75.8 2.9 %inputs_last.1 = (bf16[48,96,256]{2,1,0:T(8,128)(2,1)}, bf16[12,24,256]{2,1,0:T(8,128)(2,1)}) custom-call(bf16[50,96,768]{2,1,0:T(8,128)(2,1)S(1)} %get-tuple-element.150.three_four, bf16[2304,256]{1,0:T(8,128)(2,1)S(1)} %get-tuple-element.137.turned, bf16[12,24,256]{2,1,0:T(8,128)(2,1)S(1)} %get-tuple-element.151.six_ref, ...), custom_call_target="tpu_custom_call" | custom-call | flops 2310222592 | bytes 2359296 | tf_op jit(solution)/shard_map/inputs_last/pallas_call | solution.py:796
  78.7 0.1 broadcast_in_dim.9
  79.0 0.2 collective-permute-done.33
  79.3 1.0 %copy-done.7 = f32[36,32,256]{2,1,0:T(8,128)} copy-done((f32[36,32,256]{2,1,0:T(8,128)}, f32[36,32,256]{2,1,0:T(8,128)S(1)}, u32[]{:S(2)}) %copy-start.7) | copy-done | bytes 1179672
  (57 shorter events, 0.5 us)
Async XLA Ops:
  0.7 2.3 %copy-start = (bf16[1,48,96,256]{3,2,1,0:T(8,128)(2,1)S(1)}, bf16[1,48,96,256]{3,2,1,0:T(8,128)(2,1)}, u32[]{:S(2)}) copy-start(bf16[1,48,96,256]{3,2,1,0:T(8,128)(2,1)} %param.7) | copy-start | bytes 7077892
  0.7 2.3 %copy-start.2 = (bf16[9,256,256]{2,1,0:T(8,128)(2,1)S(1)}, bf16[9,256,256]{2,1,0:T(8,128)(2,1)}, u32[]{:S(2)}) copy-start(bf16[9,256,256]{2,1,0:T(8,128)(2,1)} %w_ref.5) | copy-start | bytes 3538948
  0.7 2.3 %copy-start.3 = (bf16[1,12,24,256]{3,2,1,0:T(8,128)(2,1)S(1)}, bf16[1,12,24,256]{3,2,1,0:T(8,128)(2,1)}, u32[]{:S(2)}) copy-start(bf16[1,12,24,256]{3,2,1,0:T(8,128)(2,1)} %param.8) | copy-start | bytes 442372
  2.4 6.4 %collective-permute-start = (bf16[384,256]{1,0:T(8,128)(2,1)}, bf16[384,256]{1,0:T(8,128)(2,1)S(1)}, u32[]{:S(2)}, u32[]{:S(2)}) collective-permute-start(bf16[384,256]{1,0:T(8,128)(2,1)} %edges.1), channel_id=1, source_target_pairs={{0,1},{1,0},{2,3},{3,2},{4,5},{5,4},{6,7},{7,6},{8,9},{9,8},{10,11... | collective-permute-start | bytes 589832 | tf_op jit(solution)/shard_map/ppermute | solution.py:425
  9.6 1.2 %collective-permute-start.1 = (f32[4,256]{1,0:T(4,128)S(1)}, f32[4,256]{1,0:T(4,128)S(1)}, u32[]{:S(2)}, u32[]{:S(2)}) collective-permute-start(f32[4,256]{1,0:T(4,128)S(1)} %get-tuple-element.92), channel_id=1, source_target_pairs={{0,1},{1,0},{2,3},{3,2},{4,5},{5,4},{6,7},{7,6},{8,9},{9,8},{10,11... | collective-permute-start | bytes 12296 | tf_op jit(solution)/shard_map/ppermute | solution.py:425
  10.9 4.9 %collective-permute-start.2 = (f32[4,256]{1,0:T(4,128)S(1)}, f32[4,256]{1,0:T(4,128)S(1)}, u32[]{:S(2)}, u32[]{:S(2)}) collective-permute-start(f32[4,256]{1,0:T(4,128)S(1)} %add.124), channel_id=1, source_target_pairs={{0,7},{1,6},{2,5},{3,4},{4,3},{5,2},{6,1},{7,0},{8,15},{9,14},{10,... | collective-permute-start | bytes 12296 | tf_op jit(solution)/shard_map/ppermute | solution.py:495
  14.4 3.0 %collective-permute-start.3 = (f32[4,256]{1,0:T(4,128)S(1)}, f32[4,256]{1,0:T(4,128)S(1)}, u32[]{:S(2)}, u32[]{:S(2)}) collective-permute-start(f32[4,256]{1,0:T(4,128)S(1)} %add.124), channel_id=1, source_target_pairs={{0,5},{1,4},{2,7},{3,6},{4,1},{5,0},{6,3},{7,2},{8,13},{9,12},{10,... | collective-permute-start | bytes 12296 | tf_op jit(solution)/shard_map/ppermute | solution.py:495
  14.9 3.0 %collective-permute-start.4 = (f32[4,256]{1,0:T(4,128)S(1)}, f32[4,256]{1,0:T(4,128)S(1)}, u32[]{:S(2)}, u32[]{:S(2)}) collective-permute-start(f32[4,256]{1,0:T(4,128)S(1)} %add.124), channel_id=1, source_target_pairs={{0,3},{1,2},{2,1},{3,0},{4,7},{5,6},{6,5},{7,4},{8,11},{9,10},{10,... | collective-permute-start | bytes 12296 | tf_op jit(solution)/shard_map/ppermute | solution.py:495
  17.9 7.4 %copy-start.4 = (bf16[1,12,24,256]{3,2,1,0:T(8,128)(2,1)S(1)}, bf16[1,12,24,256]{3,2,1,0:T(8,128)(2,1)}, u32[]{:S(2)}) copy-start(bf16[1,12,24,256]{3,2,1,0:T(8,128)(2,1)} %param.13) | copy-start | bytes 442372
  17.9 7.4 %copy-start.5 = (f32[2,256]{1,0:T(2,128)S(1)}, f32[2,256]{1,0:T(2,128)}, u32[]{:S(2)}) copy-start(f32[2,256]{1,0:T(2,128)} %gain_ref.3) | copy-start | bytes 6148
  17.9 7.5 %copy-start.6 = (f32[2,256]{1,0:T(2,128)S(1)}, f32[2,256]{1,0:T(2,128)}, u32[]{:S(2)}) copy-start(f32[2,256]{1,0:T(2,128)} %shift_ref.3) | copy-start | bytes 6148
  17.9 5.0 %collective-permute-start.5 = (f32[4,256]{1,0:T(4,128)S(1)}, f32[4,256]{1,0:T(4,128)S(1)}, u32[]{:S(2)}, u32[]{:S(2)}) collective-permute-start(f32[4,256]{1,0:T(4,128)S(1)} %add_add_fusion.3), channel_id=1, source_target_pairs={{0,25},{1,24},{2,27},{3,26},{4,29},{5,28},{6,31},{7,30},{8,17},{9,... | collective-permute-start | bytes 12296 | tf_op jit(solution)/shard_map/ppermute | solution.py:495
  21.4 3.9 %collective-permute-start.6 = (f32[4,256]{1,0:T(4,128)S(1)}, f32[4,256]{1,0:T(4,128)S(1)}, u32[]{:S(2)}, u32[]{:S(2)}) collective-permute-start(f32[4,256]{1,0:T(4,128)S(1)} %add_add_fusion.3), channel_id=1, source_target_pairs={{0,17},{1,16},{2,19},{3,18},{4,21},{5,20},{6,23},{7,22},{8,25},{9,... | collective-permute-start | bytes 12296 | tf_op jit(solution)/shard_map/ppermute | solution.py:495
  21.4 3.9 %collective-permute-start.7 = (f32[4,256]{1,0:T(4,128)S(1)}, f32[4,256]{1,0:T(4,128)S(1)}, u32[]{:S(2)}, u32[]{:S(2)}) collective-permute-start(f32[4,256]{1,0:T(4,128)S(1)} %add_add_fusion.3), channel_id=1, source_target_pairs={{0,9},{1,8},{2,11},{3,10},{4,13},{5,12},{6,15},{7,14},{8,1},{9,0},... | collective-permute-start | bytes 12296 | tf_op jit(solution)/shard_map/ppermute | solution.py:495
  21.9 3.4 %copy-start.1 = (bf16[1,48,96,256]{3,2,1,0:T(8,128)(2,1)S(1)}, bf16[1,48,96,256]{3,2,1,0:T(8,128)(2,1)}, u32[]{:S(2)}) copy-start(bf16[1,48,96,256]{3,2,1,0:T(8,128)(2,1)} %param.12) | copy-start | bytes 7077892
  28.0 1.2 %collective-permute-start.8 = (f32[4,256]{1,0:T(4,128)S(1)}, f32[4,256]{1,0:T(4,128)S(1)}, u32[]{:S(2)}, u32[]{:S(2)}) collective-permute-start(f32[4,256]{1,0:T(4,128)S(1)} %get-tuple-element.111), channel_id=1, source_target_pairs={{0,1},{1,0},{2,3},{3,2},{4,5},{5,4},{6,7},{7,6},{8,9},{9,8},{10,11... | collective-permute-start | bytes 12296 | tf_op jit(solution)/shard_map/ppermute | solution.py:425
  29.2 3.1 %collective-permute-start.10 = (f32[4,256]{1,0:T(4,128)S(1)}, f32[4,256]{1,0:T(4,128)S(1)}, u32[]{:S(2)}, u32[]{:S(2)}) collective-permute-start(f32[4,256]{1,0:T(4,128)S(1)} %add.131), channel_id=1, source_target_pairs={{0,5},{1,4},{2,7},{3,6},{4,1},{5,0},{6,3},{7,2},{8,13},{9,12},{10,... | collective-permute-start | bytes 12296 | tf_op jit(solution)/shard_map/ppermute | solution.py:495
  30.7 3.0 %collective-permute-start.11 = (f32[4,256]{1,0:T(4,128)S(1)}, f32[4,256]{1,0:T(4,128)S(1)}, u32[]{:S(2)}, u32[]{:S(2)}) collective-permute-start(f32[4,256]{1,0:T(4,128)S(1)} %add.131), channel_id=1, source_target_pairs={{0,3},{1,2},{2,1},{3,0},{4,7},{5,6},{6,5},{7,4},{8,11},{9,10},{10,... | collective-permute-start | bytes 12296 | tf_op jit(solution)/shard_map/ppermute | solution.py:495
  31.0 3.9 %collective-permute-start.9 = (f32[4,256]{1,0:T(4,128)S(1)}, f32[4,256]{1,0:T(4,128)S(1)}, u32[]{:S(2)}, u32[]{:S(2)}) collective-permute-start(f32[4,256]{1,0:T(4,128)S(1)} %add.131), channel_id=1, source_target_pairs={{0,7},{1,6},{2,5},{3,4},{4,3},{5,2},{6,1},{7,0},{8,15},{9,14},{10,... | collective-permute-start | bytes 12296 | tf_op jit(solution)/shard_map/ppermute | solution.py:495
  35.0 4.8 %collective-permute-start.12 = (f32[4,256]{1,0:T(4,128)S(1)}, f32[4,256]{1,0:T(4,128)S(1)}, u32[]{:S(2)}, u32[]{:S(2)}) collective-permute-start(f32[4,256]{1,0:T(4,128)S(1)} %add_add_fusion.1), channel_id=1, source_target_pairs={{0,25},{1,24},{2,27},{3,26},{4,29},{5,28},{6,31},{7,30},{8,17},{9,... | collective-permute-start | bytes 12296 | tf_op jit(solution)/shard_map/ppermute | solution.py:495
  36.7 3.9 %collective-permute-start.13 = (f32[4,256]{1,0:T(4,128)S(1)}, f32[4,256]{1,0:T(4,128)S(1)}, u32[]{:S(2)}, u32[]{:S(2)}) collective-permute-start(f32[4,256]{1,0:T(4,128)S(1)} %add_add_fusion.1), channel_id=1, source_target_pairs={{0,17},{1,16},{2,19},{3,18},{4,21},{5,20},{6,23},{7,22},{8,25},{9,... | collective-permute-start | bytes 12296 | tf_op jit(solution)/shard_map/ppermute | solution.py:495
  36.8 3.8 %collective-permute-start.14 = (f32[4,256]{1,0:T(4,128)S(1)}, f32[4,256]{1,0:T(4,128)S(1)}, u32[]{:S(2)}, u32[]{:S(2)}) collective-permute-start(f32[4,256]{1,0:T(4,128)S(1)} %add_add_fusion.1), channel_id=1, source_target_pairs={{0,9},{1,8},{2,11},{3,10},{4,13},{5,12},{6,15},{7,14},{8,1},{9,0},... | collective-permute-start | bytes 12296 | tf_op jit(solution)/shard_map/ppermute | solution.py:495
  46.1 2.5 %collective-permute-start.15 = (f32[4,128,256]{2,1,0:T(8,128)S(1)}, f32[4,128,256]{2,1,0:T(8,128)S(1)}, u32[]{:S(2)}, u32[]{:S(2)}) collective-permute-start(f32[4,128,256]{2,1,0:T(8,128)S(1)} %bitcast.66), channel_id=1, source_target_pairs={{0,1},{1,0},{2,3},{3,2},{4,5},{5,4},{6,7},{7,6},{8,9},{9,8},{10,11... | collective-permute-start | bytes 1572872 | tf_op jit(solution)/shard_map/ppermute | solution.py:425
  48.6 4.0 %collective-permute-start.16 = (f32[5,128,256]{2,1,0:T(8,128)S(1)}, f32[5,128,256]{2,1,0:T(8,128)S(1)}, u32[]{:S(2)}, u32[]{:S(2)}) collective-permute-start(f32[5,128,256]{2,1,0:T(8,128)S(1)} %bitcast.65), channel_id=1, source_target_pairs={{0,1},{1,0},{2,3},{3,2},{4,5},{5,4},{6,7},{7,6},{8,9},{9,8},{10,11... | collective-permute-start | bytes 1966088 | tf_op jit(solution)/shard_map/ppermute | solution.py:425
  49.0 6.7 %collective-permute-start.20 = (bf16[128,256]{1,0:T(8,128)(2,1)S(1)}, bf16[128,256]{1,0:T(8,128)(2,1)S(1)}, u32[]{:S(2)}, u32[]{:S(2)}) collective-permute-start(bf16[128,256]{1,0:T(8,128)(2,1)S(1)} %get-tuple-element.178), channel_id=1, source_target_pairs={{0,6},{2,4},{4,2},{6,0},{8,14},{10,12},{12,10},{14,8},{16,22},{18,... | collective-permute-start | bytes 196616 | tf_op jit(solution)/shard_map/ppermute | solution.py:425
  50.5 5.9 %collective-permute-start.21 = (bf16[128,256]{1,0:T(8,128)(2,1)S(1)}, bf16[128,256]{1,0:T(8,128)(2,1)S(1)}, u32[]{:S(2)}, u32[]{:S(2)}) collective-permute-start(bf16[128,256]{1,0:T(8,128)(2,1)S(1)} %get-tuple-element.177), channel_id=1, source_target_pairs={{0,4},{2,6},{4,0},{6,2},{8,12},{10,14},{12,8},{14,10},{16,20},{18,... | collective-permute-start | bytes 196616 | tf_op jit(solution)/shard_map/ppermute | solution.py:425
  52.0 4.5 %collective-permute-start.22 = (bf16[128,256]{1,0:T(8,128)(2,1)S(1)}, bf16[128,256]{1,0:T(8,128)(2,1)S(1)}, u32[]{:S(2)}, u32[]{:S(2)}) collective-permute-start(bf16[128,256]{1,0:T(8,128)(2,1)S(1)} %get-tuple-element.176), channel_id=1, source_target_pairs={{0,2},{2,0},{4,6},{6,4},{8,10},{10,8},{12,14},{14,12},{16,18},{18,... | collective-permute-start | bytes 196616 | tf_op jit(solution)/shard_map/ppermute | solution.py:425
  52.7 6.3 %collective-permute-start.17 = (bf16[160,256]{1,0:T(8,128)(2,1)S(1)}, bf16[160,256]{1,0:T(8,128)(2,1)S(1)}, u32[]{:S(2)}, u32[]{:S(2)}) collective-permute-start(bf16[160,256]{1,0:T(8,128)(2,1)S(1)} %get-tuple-element.175), channel_id=1, source_target_pairs={{0,6},{2,4},{4,2},{6,0},{8,14},{10,12},{12,10},{14,8},{16,22},{18,... | collective-permute-start | bytes 245768 | tf_op jit(solution)/shard_map/ppermute | solution.py:425
  54.2 5.1 %collective-permute-start.18 = (bf16[160,256]{1,0:T(8,128)(2,1)S(1)}, bf16[160,256]{1,0:T(8,128)(2,1)S(1)}, u32[]{:S(2)}, u32[]{:S(2)}) collective-permute-start(bf16[160,256]{1,0:T(8,128)(2,1)S(1)} %get-tuple-element.174), channel_id=1, source_target_pairs={{0,4},{2,6},{4,0},{6,2},{8,12},{10,14},{12,8},{14,10},{16,20},{18,... | collective-permute-start | bytes 245768 | tf_op jit(solution)/shard_map/ppermute | solution.py:425
  55.7 4.4 %collective-permute-start.19 = (bf16[160,256]{1,0:T(8,128)(2,1)S(1)}, bf16[160,256]{1,0:T(8,128)(2,1)S(1)}, u32[]{:S(2)}, u32[]{:S(2)}) collective-permute-start(bf16[160,256]{1,0:T(8,128)(2,1)S(1)} %get-tuple-element.173), channel_id=1, source_target_pairs={{0,2},{2,0},{4,6},{6,4},{8,10},{10,8},{12,14},{14,12},{16,18},{18,... | collective-permute-start | bytes 245768 | tf_op jit(solution)/shard_map/ppermute | solution.py:425
  56.6 4.5 %collective-permute-start.24 = (bf16[128,256]{1,0:T(8,128)(2,1)S(1)}, bf16[128,256]{1,0:T(8,128)(2,1)S(1)}, u32[]{:S(2)}, u32[]{:S(2)}) collective-permute-start(bf16[128,256]{1,0:T(8,128)(2,1)S(1)} %fusion.3), channel_id=1, source_target_pairs={{0,9},{1,16},{2,11},{3,18},{4,13},{5,20},{6,15},{7,22},{8,25},{9,0... | collective-permute-start | bytes 196616 | tf_op jit(solution)/shard_map/ppermute | solution.py:572
  60.2 4.9 %collective-permute-start.23 = (bf16[160,256]{1,0:T(8,128)(2,1)S(1)}, bf16[160,256]{1,0:T(8,128)(2,1)S(1)}, u32[]{:S(2)}, u32[]{:S(2)}) collective-permute-start(bf16[160,256]{1,0:T(8,128)(2,1)S(1)} %fusion.1), channel_id=1, source_target_pairs={{0,9},{1,16},{2,11},{3,18},{4,13},{5,20},{6,15},{7,22},{8,25},{9,0... | collective-permute-start | bytes 245768 | tf_op jit(solution)/shard_map/ppermute | solution.py:572
  61.1 6.9 %collective-permute-start.27 = (bf16[128,256]{1,0:T(8,128)(2,1)S(1)}, bf16[128,256]{1,0:T(8,128)(2,1)S(1)}, u32[]{:S(2)}, u32[]{:S(2)}) collective-permute-start(bf16[128,256]{1,0:T(8,128)(2,1)S(1)} %add_convert_fusion.6), channel_id=1, source_target_pairs={{0,17},{1,8},{2,19},{3,10},{4,21},{5,12},{6,23},{7,14},{8,1},{9,24... | collective-permute-start | bytes 196616 | tf_op jit(solution)/shard_map/ppermute | solution.py:572
  65.1 6.7 %collective-permute-start.25 = (bf16[160,256]{1,0:T(8,128)(2,1)S(1)}, bf16[160,256]{1,0:T(8,128)(2,1)S(1)}, u32[]{:S(2)}, u32[]{:S(2)}) collective-permute-start(bf16[160,256]{1,0:T(8,128)(2,1)S(1)} %add_convert_fusion.1), channel_id=1, source_target_pairs={{0,17},{1,8},{2,19},{3,10},{4,21},{5,12},{6,23},{7,14},{8,1},{9,24... | collective-permute-start | bytes 245768 | tf_op jit(solution)/shard_map/ppermute | solution.py:572
  68.0 4.1 %collective-permute-start.31 = (bf16[128,256]{1,0:T(8,128)(2,1)S(1)}, bf16[128,256]{1,0:T(8,128)(2,1)S(1)}, u32[]{:S(2)}, u32[]{:S(2)}) collective-permute-start(bf16[128,256]{1,0:T(8,128)(2,1)S(1)} %add_convert_fusion.5), channel_id=1, source_target_pairs={{0,1},{1,0},{2,3},{3,2},{4,5},{5,4},{6,7},{7,6},{8,9},{9,8},{10,11... | collective-permute-start | bytes 196616 | tf_op jit(solution)/shard_map/ppermute | solution.py:425
  68.3 5.7 %collective-permute-start.28 = (bf16[128,256]{1,0:T(8,128)(2,1)S(1)}, bf16[128,256]{1,0:T(8,128)(2,1)S(1)}, u32[]{:S(2)}, u32[]{:S(2)}) collective-permute-start(bf16[128,256]{1,0:T(8,128)(2,1)S(1)} %add_convert_fusion.5), channel_id=1, source_target_pairs={{0,6},{1,7},{2,4},{3,5},{4,2},{5,3},{6,0},{7,1},{8,15},{9,14},{10,... | collective-permute-start | bytes 196616 | tf_op jit(solution)/shard_map/ppermute | solution.py:582
  69.2 9.5 %collective-permute-start.29 = (bf16[128,256]{1,0:T(8,128)(2,1)S(1)}, bf16[128,256]{1,0:T(8,128)(2,1)S(1)}, u32[]{:S(2)}, u32[]{:S(2)}) collective-permute-start(bf16[128,256]{1,0:T(8,128)(2,1)S(1)} %add_convert_fusion.5), channel_id=1, source_target_pairs={{0,4},{1,5},{2,6},{3,7},{4,0},{5,1},{6,2},{7,3},{8,13},{9,12},{10,... | collective-permute-start | bytes 196616 | tf_op jit(solution)/shard_map/ppermute | solution.py:582
  70.7 8.0 %collective-permute-start.30 = (bf16[128,256]{1,0:T(8,128)(2,1)S(1)}, bf16[128,256]{1,0:T(8,128)(2,1)S(1)}, u32[]{:S(2)}, u32[]{:S(2)}) collective-permute-start(bf16[128,256]{1,0:T(8,128)(2,1)S(1)} %add_convert_fusion.5), channel_id=1, source_target_pairs={{0,2},{1,3},{2,0},{3,1},{4,6},{5,7},{6,4},{7,5},{8,11},{9,10},{10,... | collective-permute-start | bytes 196616 | tf_op jit(solution)/shard_map/ppermute | solution.py:582
  71.9 2.8 %collective-permute-start.26 = (bf16[160,256]{1,0:T(8,128)(2,1)S(1)}, bf16[160,256]{1,0:T(8,128)(2,1)S(1)}, u32[]{:S(2)}, u32[]{:S(2)}) collective-permute-start(bf16[160,256]{1,0:T(8,128)(2,1)S(1)} %add_convert_fusion), channel_id=1, source_target_pairs={{0,1},{1,0},{2,3},{3,2},{4,5},{5,4},{6,7},{7,6},{8,9},{9,8},{10,11... | collective-permute-start | bytes 245768 | tf_op jit(solution)/shard_map/ppermute | solution.py:425
  72.2 6.8 %collective-permute-start.32 = (bf16[160,256]{1,0:T(8,128)(2,1)S(1)}, bf16[160,256]{1,0:T(8,128)(2,1)S(1)}, u32[]{:S(2)}, u32[]{:S(2)}) collective-permute-start(bf16[160,256]{1,0:T(8,128)(2,1)S(1)} %add_convert_fusion), channel_id=1, source_target_pairs={{0,6},{1,7},{2,4},{3,5},{4,2},{5,3},{6,0},{7,1},{8,15},{9,14},{10,... | collective-permute-start | bytes 245768 | tf_op jit(solution)/shard_map/ppermute | solution.py:582
  74.1 5.1 %collective-permute-start.33 = (bf16[160,256]{1,0:T(8,128)(2,1)S(1)}, bf16[160,256]{1,0:T(8,128)(2,1)S(1)}, u32[]{:S(2)}, u32[]{:S(2)}) collective-permute-start(bf16[160,256]{1,0:T(8,128)(2,1)S(1)} %add_convert_fusion), channel_id=1, source_target_pairs={{0,4},{1,5},{2,6},{3,7},{4,0},{5,1},{6,2},{7,3},{8,13},{9,12},{10,... | collective-permute-start | bytes 245768 | tf_op jit(solution)/shard_map/ppermute | solution.py:582
  74.6 4.6 %collective-permute-start.34 = (bf16[160,256]{1,0:T(8,128)(2,1)S(1)}, bf16[160,256]{1,0:T(8,128)(2,1)S(1)}, u32[]{:S(2)}, u32[]{:S(2)}) collective-permute-start(bf16[160,256]{1,0:T(8,128)(2,1)S(1)} %add_convert_fusion), channel_id=1, source_target_pairs={{0,2},{1,3},{2,0},{3,1},{4,6},{5,7},{6,4},{7,5},{8,11},{9,10},{10,... | collective-permute-start | bytes 245768 | tf_op jit(solution)/shard_map/ppermute | solution.py:582
  79.3 1.0 %copy-start.7 = (f32[36,32,256]{2,1,0:T(8,128)}, f32[36,32,256]{2,1,0:T(8,128)S(1)}, u32[]{:S(2)}) copy-start(f32[36,32,256]{2,1,0:T(8,128)S(1)} %convert_dynamic-update-slice_fusion) | copy-start | bytes 3538948

commit v3 on v2

--- a/solution.py
+++ b/solution.py
@@ -594,9 +594,12 @@
     return total
 
 
-def gather(total, found):
-    beside = swap(total, "sp", 1)
-    return [bring(total, k) for k in FAR_FIRST] + [jnp.where(found.odd, beside, total)], beside
+def gather(total, found, tied=False):
+    beside, far = swap(total, "sp", 1), bring(total, FAR_FIRST[0])
+    if tied:
+        beside, total = lax.optimization_barrier((beside, total))
+    own = jnp.where(found.odd, beside, total)
+    return [far] + [bring(total, k) for k in FAR_FIRST[1:]] + [own], beside
 
 
 def put_pieces(whole, pieces, starts):
@@ -790,7 +793,7 @@
     piece_a = every_share(both(piece_a, met_a))
     pieces_a, unused = gather(piece_a, found)
     piece_b = every_share(both(piece_b, met_b))
-    pieces_b, beside = gather(piece_b, found)
+    pieces_b, beside = gather(piece_b, found, True)
     unused, three_four = lax.optimization_barrier(((beside, pieces_a[0]), three_four))
     done = bounds[-1]
     grad_four, grad_six = pl.pallas_call(

time: 80.5 us -> 80.8 us (level)
  starting transfers between devices: 34.6 us -> 35.5 us
    ppermute x6, starting transfers between devices: 6.1 us -> 7.03 us  [bring(): return lax.ppermute(array, ('rep', 'sp'), pairs)]
  transfers between devices with their start and end apart: 35 -> 35, of which waited for: 17 -> 17; matrix products, arithmetic and copies ran while one was open for 1% -> 1% of each run, Pallas kernels for 21% -> 20%
where the time goes in v3:
time: 80.8 us; the launch traced here: 80.6 us
  starting transfers between devices  35.5 us (44%)
  Pallas kernels  27.2 us (34%)
  waiting for transfers between devices  15.3 us (19%)
  local copies, waits for them, and re-layouts  1.16 us (1%)
  between operations  1.02 us (1%)
    ppermute x12, starting transfers between devices, swap_across(): return lax.ppermute(array, ('rep', 'sp'), pairs)  15.2 us
    ppermute x13, starting transfers between devices, swap(): return lax.ppermute(array, axis, [(i, i ^ stride) for i in range(count)])  9.75 us
    ppermute x12, waiting for transfers between devices, swap_across(): return lax.ppermute(array, ('rep', 'sp'), pairs)  9.51 us
    ppermute x6, starting transfers between devices, bring(): return lax.ppermute(array, ('rep', 'sp'), pairs)  7.03 us
    pallas_call x1, Pallas kernels, local(): pl.pallas_call(inner_kernel, out_shape=(jax.ShapeDtypeStruct((rows_four -...  5.87 us
    pallas_call x1, Pallas kernels, local(): pl.pallas_call(functools.partial(backward_kernel, counts, sp_count, (cols...  5.51 us
    pallas_call x2, Pallas kernels, inputs(): pl.pallas_call(functools.partial(input_kernel, group), out_shape=parts, i...  4.43 us
    ppermute x4, starting transfers between devices, swap_high(): return lax.ppermute(array, ('rep', 'sp'), pairs)  3.49 us
  transfers between devices with their start and end apart: 35, of which 17 were waited for; matrix products, arithmetic and copies ran while one was open for 1% of the time, Pallas kernels for 20%

profile of v3, /device:TPU:0, one launch (start us, length us, event | category | flops | bytes accessed | tf_op | source)
XLA Modules:
  0.0 80.6 jit_solution(2788068256135955340)
XLA Ops:
  0.7 1.7 %edges.1 = bf16[384,256]{1,0:T(8,128)(2,1)} custom-call(bf16[48,96,256]{2,1,0:T(8,128)(2,1)} %bitcast.51, bf16[12,24,256]{2,1,0:T(8,128)(2,1)} %bitcast.59, bf16[48,96,256]{2,1,0:T(8,128)(2,1)} %bitcast.55, bf16[12,24,256]{2,1,0:T(8,128)(2,1)} %bitcast.63), custom_call_target="tpu_custom_call" | custom-call | tf_op jit(solution)/shard_map/edges/pallas_call | solution.py:467
  2.4 0.5 collective-permute-start
  3.0 5.9 %forward_inner.1 = (bf16[46,96,256]{2,1,0:T(8,128)(2,1)S(1)}, bf16[10,32,256]{2,1,0:T(8,128)(2,1)S(1)}, f32[4,256]{1,0:T(4,128)S(1)}) custom-call(bf16[48,96,256]{2,1,0:T(8,128)(2,1)S(1)} %bitcast.52, bf16[12,24,256]{2,1,0:T(8,128)(2,1)S(1)} %bitcast.60, bf16[9,256,256]{2,1,0:T(8,128)(2,1)S(1)} %copy-done.2), custom_call_target="tpu_custom_call" | custom-call | flops 5775556608 | bytes 4718592 | tf_op jit(solution)/shard_map/forward_inner/pallas_call | solution.py:636
  8.9 0.8 forward_outer.1
  9.6 0.4 collective-permute-start.1
  10.0 0.8 %collective-permute-done.1 = f32[4,256]{1,0:T(4,128)S(1)} collective-permute-done((f32[4,256]{1,0:T(4,128)S(1)}, f32[4,256]{1,0:T(4,128)S(1)}, u32[]{:S(2)}, u32[]{:S(2)}) %collective-permute-start.1) | collective-permute-done | bytes 4128 | tf_op jit(solution)/shard_map/ppermute | solution.py:425
  10.9 3.6 %collective-permute-start.2 = (f32[4,256]{1,0:T(4,128)S(1)}, f32[4,256]{1,0:T(4,128)S(1)}, u32[]{:S(2)}, u32[]{:S(2)}) collective-permute-start(f32[4,256]{1,0:T(4,128)S(1)} %add.124), channel_id=1, source_target_pairs={{0,7},{1,6},{2,5},{3,4},{4,3},{5,2},{6,1},{7,0},{8,15},{9,14},{10,... | collective-permute-start | bytes 12296 | tf_op jit(solution)/shard_map/ppermute | solution.py:495
  14.4 0.4 collective-permute-start.3
  14.9 0.1 collective-permute-start.4
  14.9 0.8 %collective-permute-done.2 = f32[4,256]{1,0:T(4,128)S(1)} collective-permute-done((f32[4,256]{1,0:T(4,128)S(1)}, f32[4,256]{1,0:T(4,128)S(1)}, u32[]{:S(2)}, u32[]{:S(2)}) %collective-permute-start.2) | collective-permute-done | bytes 4128 | tf_op jit(solution)/shard_map/ppermute | solution.py:495
  15.8 1.7 %collective-permute-done.3 = f32[4,256]{1,0:T(4,128)S(1)} collective-permute-done((f32[4,256]{1,0:T(4,128)S(1)}, f32[4,256]{1,0:T(4,128)S(1)}, u32[]{:S(2)}, u32[]{:S(2)}) %collective-permute-start.3) | collective-permute-done | bytes 4128 | tf_op jit(solution)/shard_map/ppermute | solution.py:495
  17.5 0.4 collective-permute-done.4
  17.9 3.5 %collective-permute-start.5 = (f32[4,256]{1,0:T(4,128)S(1)}, f32[4,256]{1,0:T(4,128)S(1)}, u32[]{:S(2)}, u32[]{:S(2)}) collective-permute-start(f32[4,256]{1,0:T(4,128)S(1)} %add_add_fusion.3), channel_id=1, source_target_pairs={{0,25},{1,24},{2,27},{3,26},{4,29},{5,28},{6,31},{7,30},{8,17},{9,... | collective-permute-start | bytes 12296 | tf_op jit(solution)/shard_map/ppermute | solution.py:495
  21.4 0.6 collective-permute-start.7
  21.9 1.0 %turn.1 = (bf16[256,4992]{1,0:T(8,128)(2,1)S(1)}, bf16[2304,256]{1,0:T(8,128)(2,1)S(1)}) custom-call(bf16[48,96,256]{2,1,0:T(8,128)(2,1)S(1)} %bitcast.54, bf16[12,24,256]{2,1,0:T(8,128)(2,1)S(1)} %bitcast.62, bf16[9,256,256]{2,1,0:T(8,128)(2,1)S(1)} %copy-done.2), custom_call_target="tpu_custom_call" | custom-call | flops 1732667008 | bytes 4718592 | tf_op jit(solution)/shard_map/turn/pallas_call | solution.py:671
  23.0 2.4 %collective-permute-done.6 = f32[4,256]{1,0:T(4,128)S(1)} collective-permute-done((f32[4,256]{1,0:T(4,128)S(1)}, f32[4,256]{1,0:T(4,128)S(1)}, u32[]{:S(2)}, u32[]{:S(2)}) %collective-permute-start.6) | collective-permute-done | bytes 4128 | tf_op jit(solution)/shard_map/ppermute | solution.py:495
  25.4 2.6 %slopes.1 = (f32[50,96,256]{2,1,0:T(8,128)S(1)}, f32[14,32,256]{2,1,0:T(8,128)S(1)}, f32[4,256]{1,0:T(4,128)S(1)}) custom-call(bf16[46,96,256]{2,1,0:T(8,128)(2,1)S(1)} %get-tuple-element.106.inner_four_ref, bf16[10,32,256]{2,1,0:T(8,128)(2,1)S(1)} %get-tuple-element.107.inner_six_ref, bf16[4,96,256]{2,1,0:T(8,128)(2,1)S(1)} %get-tuple-element.108.outer_four_ref, ...), custom_call_target="tpu_custom_call" | custom-call | flops 57755568 | bytes 4718592 | tf_op jit(solution)/shard_map/slopes/pallas_call | solution.py:685
  28.0 0.4 collective-permute-start.8
  28.4 0.9 %collective-permute-done.8 = f32[4,256]{1,0:T(4,128)S(1)} collective-permute-done((f32[4,256]{1,0:T(4,128)S(1)}, f32[4,256]{1,0:T(4,128)S(1)}, u32[]{:S(2)}, u32[]{:S(2)}) %collective-permute-start.8) | collective-permute-done | bytes 4128 | tf_op jit(solution)/shard_map/ppermute | solution.py:425
  29.2 1.4 %collective-permute-start.10 = (f32[4,256]{1,0:T(4,128)S(1)}, f32[4,256]{1,0:T(4,128)S(1)}, u32[]{:S(2)}, u32[]{:S(2)}) collective-permute-start(f32[4,256]{1,0:T(4,128)S(1)} %add.131), channel_id=1, source_target_pairs={{0,5},{1,4},{2,7},{3,6},{4,1},{5,0},{6,3},{7,2},{8,13},{9,12},{10,... | collective-permute-start | bytes 12296 | tf_op jit(solution)/shard_map/ppermute | solution.py:495
  30.7 0.3 collective-permute-start.11
  31.0 1.3 %collective-permute-start.9 = (f32[4,256]{1,0:T(4,128)S(1)}, f32[4,256]{1,0:T(4,128)S(1)}, u32[]{:S(2)}, u32[]{:S(2)}) collective-permute-start(f32[4,256]{1,0:T(4,128)S(1)} %add.131), channel_id=1, source_target_pairs={{0,7},{1,6},{2,5},{3,4},{4,3},{5,2},{6,1},{7,0},{8,15},{9,14},{10,... | collective-permute-start | bytes 12296 | tf_op jit(solution)/shard_map/ppermute | solution.py:495
  32.4 1.3 %collective-permute-done.11 = f32[4,256]{1,0:T(4,128)S(1)} collective-permute-done((f32[4,256]{1,0:T(4,128)S(1)}, f32[4,256]{1,0:T(4,128)S(1)}, u32[]{:S(2)}, u32[]{:S(2)}) %collective-permute-start.11) | collective-permute-done | bytes 4128 | tf_op jit(solution)/shard_map/ppermute | solution.py:495
  33.7 1.2 %collective-permute-done.9 = f32[4,256]{1,0:T(4,128)S(1)} collective-permute-done((f32[4,256]{1,0:T(4,128)S(1)}, f32[4,256]{1,0:T(4,128)S(1)}, u32[]{:S(2)}, u32[]{:S(2)}) %collective-permute-start.9) | collective-permute-done | bytes 4128 | tf_op jit(solution)/shard_map/ppermute | solution.py:495
  35.0 1.7 %collective-permute-start.12 = (f32[4,256]{1,0:T(4,128)S(1)}, f32[4,256]{1,0:T(4,128)S(1)}, u32[]{:S(2)}, u32[]{:S(2)}) collective-permute-start(f32[4,256]{1,0:T(4,128)S(1)} %add_add_fusion.1), channel_id=1, source_target_pairs={{0,25},{1,24},{2,27},{3,26},{4,29},{5,28},{6,31},{7,30},{8,17},{9,... | collective-permute-start | bytes 12296 | tf_op jit(solution)/shard_map/ppermute | solution.py:495
  36.7 0.1 collective-permute-start.13
  36.8 2.2 %collective-permute-start.14 = (f32[4,256]{1,0:T(4,128)S(1)}, f32[4,256]{1,0:T(4,128)S(1)}, u32[]{:S(2)}, u32[]{:S(2)}) collective-permute-start(f32[4,256]{1,0:T(4,128)S(1)} %add_add_fusion.1), channel_id=1, source_target_pairs={{0,9},{1,8},{2,11},{3,10},{4,13},{5,12},{6,15},{7,14},{8,1},{9,0},... | collective-permute-start | bytes 12296 | tf_op jit(solution)/shard_map/ppermute | solution.py:495
  39.0 0.8 %collective-permute-done.12 = f32[4,256]{1,0:T(4,128)S(1)} collective-permute-done((f32[4,256]{1,0:T(4,128)S(1)}, f32[4,256]{1,0:T(4,128)S(1)}, u32[]{:S(2)}, u32[]{:S(2)}) %collective-permute-start.12) | collective-permute-done | bytes 4128 | tf_op jit(solution)/shard_map/ppermute | solution.py:495
  39.8 0.8 collective-permute-done.13
  40.6 5.5 %backward.1 = (bf16[50,96,768]{2,1,0:T(8,128)(2,1)S(1)}, bf16[14,32,768]{2,1,0:T(8,128)(2,1)S(1)}, f32[4,128,256]{2,1,0:T(8,128)S(1)}, f32[1,4,128,256]{3,2,1,0:...) custom-call(bf16[256,4992]{1,0:T(8,128)(2,1)S(1)} %get-tuple-element.105.turned_ref, ...), custom_call_target="tpu_custom_call" | custom-call | flops 3465334016 | bytes 9437184 | tf_op jit(solution)/shard_map/backward/pallas_call | solution.py:712
  46.1 0.2 collective-permute-start.15
  46.3 2.3 %weights.1 = (f32[5,128,256]{2,1,0:T(8,128)S(1)}, f32[1,5,128,256]{3,2,1,0:T(8,128)S(1)}) custom-call(bf16[256,4992]{1,0:T(8,128)(2,1)S(1)} %get-tuple-element.105.turned_ref, bf16[50,96,768]{2,1,0:T(8,128)(2,1)S(1)} %get-tuple-element.153.three_four, bf16[14,32,768]{2,1,0:T(8,128)(2,1)S(1)} %get-tuple-element.123.three_six, ...), custom_call_target="tpu_custom_call" | custom-call | flops 3465334016 | bytes 9437184 | tf_op jit(solution)/shard_map/weights/pallas_call | solution.py:730
  48.6 0.4 collective-permute-start.16
  49.0 1.5 %collective-permute-start.20 = (bf16[128,256]{1,0:T(8,128)(2,1)S(1)}, bf16[128,256]{1,0:T(8,128)(2,1)S(1)}, u32[]{:S(2)}, u32[]{:S(2)}) collective-permute-start(bf16[128,256]{1,0:T(8,128)(2,1)S(1)} %get-tuple-element.182), channel_id=1, source_target_pairs={{0,6},{2,4},{4,2},{6,0},{8,14},{10,12},{12,10},{14,8},{16,22},{18,... | collective-permute-start | bytes 196616 | tf_op jit(solution)/shard_map/ppermute | solution.py:425
  50.5 1.5 %collective-permute-start.21 = (bf16[128,256]{1,0:T(8,128)(2,1)S(1)}, bf16[128,256]{1,0:T(8,128)(2,1)S(1)}, u32[]{:S(2)}, u32[]{:S(2)}) collective-permute-start(bf16[128,256]{1,0:T(8,128)(2,1)S(1)} %get-tuple-element.181), channel_id=1, source_target_pairs={{0,4},{2,6},{4,0},{6,2},{8,12},{10,14},{12,8},{14,10},{16,20},{18,... | collective-permute-start | bytes 196616 | tf_op jit(solution)/shard_map/ppermute | solution.py:425
  52.0 0.5 collective-permute-start.22
  52.6 0.1 fusion.6
  52.7 1.5 %collective-permute-start.17 = (bf16[160,256]{1,0:T(8,128)(2,1)S(1)}, bf16[160,256]{1,0:T(8,128)(2,1)S(1)}, u32[]{:S(2)}, u32[]{:S(2)}) collective-permute-start(bf16[160,256]{1,0:T(8,128)(2,1)S(1)} %get-tuple-element.179), channel_id=1, source_target_pairs={{0,6},{2,4},{4,2},{6,0},{8,14},{10,12},{12,10},{14,8},{16,22},{18,... | collective-permute-start | bytes 245768 | tf_op jit(solution)/shard_map/ppermute | solution.py:425
  54.2 1.5 %collective-permute-start.18 = (bf16[160,256]{1,0:T(8,128)(2,1)S(1)}, bf16[160,256]{1,0:T(8,128)(2,1)S(1)}, u32[]{:S(2)}, u32[]{:S(2)}) collective-permute-start(bf16[160,256]{1,0:T(8,128)(2,1)S(1)} %get-tuple-element.178), channel_id=1, source_target_pairs={{0,4},{2,6},{4,0},{6,2},{8,12},{10,14},{12,8},{14,10},{16,20},{18,... | collective-permute-start | bytes 245768 | tf_op jit(solution)/shard_map/ppermute | solution.py:425
  55.7 0.7 collective-permute-start.19
  56.4 0.2 collective-permute-done.22
  56.6 0.3 collective-permute-start.24
  56.9 2.0 %inputs.2.rest_0_ = bf16[16,96,256]{2,1,0:T(8,128)(2,1)S(1)} custom-call(bf16[50,96,768]{2,1,0:T(8,128)(2,1)S(1)} %get-tuple-element.153.three_four, bf16[14,32,768]{2,1,0:T(8,128)(2,1)S(1)} %get-tuple-element.123.three_six, bf16[2304,256]{1,0:T(8,128)(2,1)S(1)} %get-tuple-element.139.turned), custom_call_target="tpu_custom_call" | custom-call | flops 1732667008 | bytes 1179648 | tf_op jit(solution)/shard_map/inputs/pallas_call | solution.py:753
  58.9 0.3 collective-permute-done.18
  59.2 0.9 %collective-permute-done.19 = bf16[160,256]{1,0:T(8,128)(2,1)S(1)} collective-permute-done((bf16[160,256]{1,0:T(8,128)(2,1)S(1)}, bf16[160,256]{1,0:T(8,128)(2,1)S(1)}, u32[]{:S(2)}, u32[]{:S(2)}) %collective-permute-start.19) | collective-permute-done | bytes 81952 | tf_op jit(solution)/shard_map/ppermute | solution.py:425
  60.2 0.4 collective-permute-start.23
  60.6 0.5 collective-permute-done.24
  61.1 1.6 %collective-permute-start.27 = (bf16[128,256]{1,0:T(8,128)(2,1)S(1)}, bf16[128,256]{1,0:T(8,128)(2,1)S(1)}, u32[]{:S(2)}, u32[]{:S(2)}) collective-permute-start(bf16[128,256]{1,0:T(8,128)(2,1)S(1)} %add_convert_fusion.6), channel_id=1, source_target_pairs={{0,17},{1,8},{2,19},{3,10},{4,21},{5,12},{6,23},{7,14},{8,1},{9,24... | collective-permute-start | bytes 196616 | tf_op jit(solution)/shard_map/ppermute | solution.py:572
  62.6 2.5 %inputs.3 = (bf16[16,96,256]{2,1,0:T(8,128)(2,1)S(1)}, bf16[12,24,256]{2,1,0:T(8,128)(2,1)S(1)}) custom-call(bf16[50,96,768]{2,1,0:T(8,128)(2,1)S(1)} %get-tuple-element.153.three_four, bf16[14,32,768]{2,1,0:T(8,128)(2,1)S(1)} %get-tuple-element.123.three_six, bf16[2304,256]{1,0:T(8,128)(2,1)S(1)} %get-tuple-element.139.turned), custom_call_target="tpu_custom_call" | custom-call | flops 1732667008 | bytes 1179648 | tf_op jit(solution)/shard_map/inputs/pallas_call | solution.py:753
  65.1 1.2 %collective-permute-start.25 = (bf16[160,256]{1,0:T(8,128)(2,1)S(1)}, bf16[160,256]{1,0:T(8,128)(2,1)S(1)}, u32[]{:S(2)}, u32[]{:S(2)}) collective-permute-start(bf16[160,256]{1,0:T(8,128)(2,1)S(1)} %add_convert_fusion.1), channel_id=1, source_target_pairs={{0,17},{1,8},{2,19},{3,10},{4,21},{5,12},{6,23},{7,14},{8,1},{9,24... | collective-permute-start | bytes 245768 | tf_op jit(solution)/shard_map/ppermute | solution.py:572
  66.4 1.7 %collective-permute-done.27 = bf16[128,256]{1,0:T(8,128)(2,1)S(1)} collective-permute-done((bf16[128,256]{1,0:T(8,128)(2,1)S(1)}, bf16[128,256]{1,0:T(8,128)(2,1)S(1)}, u32[]{:S(2)}, u32[]{:S(2)}) %collective-permute-start.27) | collective-permute-done | bytes 65568 | tf_op jit(solution)/shard_map/ppermute | solution.py:572
  68.0 0.3 collective-permute-start.31
  68.3 0.9 %collective-permute-start.28 = (bf16[128,256]{1,0:T(8,128)(2,1)S(1)}, bf16[128,256]{1,0:T(8,128)(2,1)S(1)}, u32[]{:S(2)}, u32[]{:S(2)}) collective-permute-start(bf16[128,256]{1,0:T(8,128)(2,1)S(1)} %add_convert_fusion.5), channel_id=1, source_target_pairs={{0,6},{1,7},{2,4},{3,5},{4,2},{5,3},{6,0},{7,1},{8,15},{9,14},{10,... | collective-permute-start | bytes 196616 | tf_op jit(solution)/shard_map/ppermute | solution.py:582
  69.2 1.5 %collective-permute-start.29 = (bf16[128,256]{1,0:T(8,128)(2,1)S(1)}, bf16[128,256]{1,0:T(8,128)(2,1)S(1)}, u32[]{:S(2)}, u32[]{:S(2)}) collective-permute-start(bf16[128,256]{1,0:T(8,128)(2,1)S(1)} %add_convert_fusion.5), channel_id=1, source_target_pairs={{0,4},{1,5},{2,6},{3,7},{4,0},{5,1},{6,2},{7,3},{8,13},{9,12},{10,... | collective-permute-start | bytes 196616 | tf_op jit(solution)/shard_map/ppermute | solution.py:582
  70.7 1.1 %collective-permute-start.30 = (bf16[128,256]{1,0:T(8,128)(2,1)S(1)}, bf16[128,256]{1,0:T(8,128)(2,1)S(1)}, u32[]{:S(2)}, u32[]{:S(2)}) collective-permute-start(bf16[128,256]{1,0:T(8,128)(2,1)S(1)} %add_convert_fusion.5), channel_id=1, source_target_pairs={{0,2},{1,3},{2,0},{3,1},{4,6},{5,7},{6,4},{7,5},{8,11},{9,10},{10,... | collective-permute-start | bytes 196616 | tf_op jit(solution)/shard_map/ppermute | solution.py:582
  71.9 0.3 collective-permute-start.26
  72.2 0.9 %collective-permute-start.32 = (bf16[160,256]{1,0:T(8,128)(2,1)S(1)}, bf16[160,256]{1,0:T(8,128)(2,1)S(1)}, u32[]{:S(2)}, u32[]{:S(2)}) collective-permute-start(bf16[160,256]{1,0:T(8,128)(2,1)S(1)} %add_convert_fusion), channel_id=1, source_target_pairs={{0,6},{1,7},{2,4},{3,5},{4,2},{5,3},{6,0},{7,1},{8,15},{9,14},{10,... | collective-permute-start | bytes 245768 | tf_op jit(solution)/shard_map/ppermute | solution.py:582
  73.1 0.1 collective-permute-done.26
  73.2 1.4 %collective-permute-start.33 = (bf16[160,256]{1,0:T(8,128)(2,1)S(1)}, bf16[160,256]{1,0:T(8,128)(2,1)S(1)}, u32[]{:S(2)}, u32[]{:S(2)}) collective-permute-start(bf16[160,256]{1,0:T(8,128)(2,1)S(1)} %add_convert_fusion), channel_id=1, source_target_pairs={{0,4},{1,5},{2,6},{3,7},{4,0},{5,1},{6,2},{7,3},{8,13},{9,12},{10,... | collective-permute-start | bytes 245768 | tf_op jit(solution)/shard_map/ppermute | solution.py:582
  74.7 1.2 %collective-permute-start.34 = (bf16[160,256]{1,0:T(8,128)(2,1)S(1)}, bf16[160,256]{1,0:T(8,128)(2,1)S(1)}, u32[]{:S(2)}, u32[]{:S(2)}) collective-permute-start(bf16[160,256]{1,0:T(8,128)(2,1)S(1)} %add_convert_fusion), channel_id=1, source_target_pairs={{0,2},{1,3},{2,0},{3,1},{4,6},{5,7},{6,4},{7,5},{8,11},{9,10},{10,... | collective-permute-start | bytes 245768 | tf_op jit(solution)/shard_map/ppermute | solution.py:582
  75.8 2.9 %inputs_last.1 = (bf16[48,96,256]{2,1,0:T(8,128)(2,1)}, bf16[12,24,256]{2,1,0:T(8,128)(2,1)}) custom-call(bf16[50,96,768]{2,1,0:T(8,128)(2,1)S(1)} %get-tuple-element.153.three_four, bf16[2304,256]{1,0:T(8,128)(2,1)S(1)} %get-tuple-element.139.turned, bf16[12,24,256]{2,1,0:T(8,128)(2,1)S(1)} %get-tuple-element.154.six_ref, ...), custom_call_target="tpu_custom_call" | custom-call | flops 2310222592 | bytes 2359296 | tf_op jit(solution)/shard_map/inputs_last/pallas_call | solution.py:799
  78.8 0.1 broadcast_in_dim.9
  79.1 0.4 collective-permute-done.33
  79.6 1.0 %copy-done.7 = f32[36,32,256]{2,1,0:T(8,128)} copy-done((f32[36,32,256]{2,1,0:T(8,128)}, f32[36,32,256]{2,1,0:T(8,128)S(1)}, u32[]{:S(2)}) %copy-start.7) | copy-done | bytes 1179672
  (57 shorter events, 0.5 us)
Async XLA Ops:
  0.7 2.3 %copy-start = (bf16[1,48,96,256]{3,2,1,0:T(8,128)(2,1)S(1)}, bf16[1,48,96,256]{3,2,1,0:T(8,128)(2,1)}, u32[]{:S(2)}) copy-start(bf16[1,48,96,256]{3,2,1,0:T(8,128)(2,1)} %param.7) | copy-start | bytes 7077892
  0.7 2.3 %copy-start.2 = (bf16[9,256,256]{2,1,0:T(8,128)(2,1)S(1)}, bf16[9,256,256]{2,1,0:T(8,128)(2,1)}, u32[]{:S(2)}) copy-start(bf16[9,256,256]{2,1,0:T(8,128)(2,1)} %w_ref.5) | copy-start | bytes 3538948
  0.7 2.3 %copy-start.3 = (bf16[1,12,24,256]{3,2,1,0:T(8,128)(2,1)S(1)}, bf16[1,12,24,256]{3,2,1,0:T(8,128)(2,1)}, u32[]{:S(2)}) copy-start(bf16[1,12,24,256]{3,2,1,0:T(8,128)(2,1)} %param.8) | copy-start | bytes 442372
  2.4 6.4 %collective-permute-start = (bf16[384,256]{1,0:T(8,128)(2,1)}, bf16[384,256]{1,0:T(8,128)(2,1)S(1)}, u32[]{:S(2)}, u32[]{:S(2)}) collective-permute-start(bf16[384,256]{1,0:T(8,128)(2,1)} %edges.1), channel_id=1, source_target_pairs={{0,1},{1,0},{2,3},{3,2},{4,5},{5,4},{6,7},{7,6},{8,9},{9,8},{10,11... | collective-permute-start | bytes 589832 | tf_op jit(solution)/shard_map/ppermute | solution.py:425
  9.6 1.2 %collective-permute-start.1 = (f32[4,256]{1,0:T(4,128)S(1)}, f32[4,256]{1,0:T(4,128)S(1)}, u32[]{:S(2)}, u32[]{:S(2)}) collective-permute-start(f32[4,256]{1,0:T(4,128)S(1)} %get-tuple-element.94), channel_id=1, source_target_pairs={{0,1},{1,0},{2,3},{3,2},{4,5},{5,4},{6,7},{7,6},{8,9},{9,8},{10,11... | collective-permute-start | bytes 12296 | tf_op jit(solution)/shard_map/ppermute | solution.py:425
  10.9 4.9 %collective-permute-start.2 = (f32[4,256]{1,0:T(4,128)S(1)}, f32[4,256]{1,0:T(4,128)S(1)}, u32[]{:S(2)}, u32[]{:S(2)}) collective-permute-start(f32[4,256]{1,0:T(4,128)S(1)} %add.124), channel_id=1, source_target_pairs={{0,7},{1,6},{2,5},{3,4},{4,3},{5,2},{6,1},{7,0},{8,15},{9,14},{10,... | collective-permute-start | bytes 12296 | tf_op jit(solution)/shard_map/ppermute | solution.py:495
  14.4 3.0 %collective-permute-start.3 = (f32[4,256]{1,0:T(4,128)S(1)}, f32[4,256]{1,0:T(4,128)S(1)}, u32[]{:S(2)}, u32[]{:S(2)}) collective-permute-start(f32[4,256]{1,0:T(4,128)S(1)} %add.124), channel_id=1, source_target_pairs={{0,5},{1,4},{2,7},{3,6},{4,1},{5,0},{6,3},{7,2},{8,13},{9,12},{10,... | collective-permute-start | bytes 12296 | tf_op jit(solution)/shard_map/ppermute | solution.py:495
  14.9 3.0 %collective-permute-start.4 = (f32[4,256]{1,0:T(4,128)S(1)}, f32[4,256]{1,0:T(4,128)S(1)}, u32[]{:S(2)}, u32[]{:S(2)}) collective-permute-start(f32[4,256]{1,0:T(4,128)S(1)} %add.124), channel_id=1, source_target_pairs={{0,3},{1,2},{2,1},{3,0},{4,7},{5,6},{6,5},{7,4},{8,11},{9,10},{10,... | collective-permute-start | bytes 12296 | tf_op jit(solution)/shard_map/ppermute | solution.py:495
  17.9 7.4 %copy-start.4 = (bf16[1,12,24,256]{3,2,1,0:T(8,128)(2,1)S(1)}, bf16[1,12,24,256]{3,2,1,0:T(8,128)(2,1)}, u32[]{:S(2)}) copy-start(bf16[1,12,24,256]{3,2,1,0:T(8,128)(2,1)} %param.13) | copy-start | bytes 442372
  17.9 7.4 %copy-start.5 = (f32[2,256]{1,0:T(2,128)S(1)}, f32[2,256]{1,0:T(2,128)}, u32[]{:S(2)}) copy-start(f32[2,256]{1,0:T(2,128)} %gain_ref.3) | copy-start | bytes 6148
  17.9 7.5 %copy-start.6 = (f32[2,256]{1,0:T(2,128)S(1)}, f32[2,256]{1,0:T(2,128)}, u32[]{:S(2)}) copy-start(f32[2,256]{1,0:T(2,128)} %shift_ref.3) | copy-start | bytes 6148
  17.9 5.0 %collective-permute-start.5 = (f32[4,256]{1,0:T(4,128)S(1)}, f32[4,256]{1,0:T(4,128)S(1)}, u32[]{:S(2)}, u32[]{:S(2)}) collective-permute-start(f32[4,256]{1,0:T(4,128)S(1)} %add_add_fusion.3), channel_id=1, source_target_pairs={{0,25},{1,24},{2,27},{3,26},{4,29},{5,28},{6,31},{7,30},{8,17},{9,... | collective-permute-start | bytes 12296 | tf_op jit(solution)/shard_map/ppermute | solution.py:495
  21.4 3.9 %collective-permute-start.6 = (f32[4,256]{1,0:T(4,128)S(1)}, f32[4,256]{1,0:T(4,128)S(1)}, u32[]{:S(2)}, u32[]{:S(2)}) collective-permute-start(f32[4,256]{1,0:T(4,128)S(1)} %add_add_fusion.3), channel_id=1, source_target_pairs={{0,17},{1,16},{2,19},{3,18},{4,21},{5,20},{6,23},{7,22},{8,25},{9,... | collective-permute-start | bytes 12296 | tf_op jit(solution)/shard_map/ppermute | solution.py:495
  21.4 3.9 %collective-permute-start.7 = (f32[4,256]{1,0:T(4,128)S(1)}, f32[4,256]{1,0:T(4,128)S(1)}, u32[]{:S(2)}, u32[]{:S(2)}) collective-permute-start(f32[4,256]{1,0:T(4,128)S(1)} %add_add_fusion.3), channel_id=1, source_target_pairs={{0,9},{1,8},{2,11},{3,10},{4,13},{5,12},{6,15},{7,14},{8,1},{9,0},... | collective-permute-start | bytes 12296 | tf_op jit(solution)/shard_map/ppermute | solution.py:495
  21.9 3.4 %copy-start.1 = (bf16[1,48,96,256]{3,2,1,0:T(8,128)(2,1)S(1)}, bf16[1,48,96,256]{3,2,1,0:T(8,128)(2,1)}, u32[]{:S(2)}) copy-start(bf16[1,48,96,256]{3,2,1,0:T(8,128)(2,1)} %param.12) | copy-start | bytes 7077892
  28.0 1.2 %collective-permute-start.8 = (f32[4,256]{1,0:T(4,128)S(1)}, f32[4,256]{1,0:T(4,128)S(1)}, u32[]{:S(2)}, u32[]{:S(2)}) collective-permute-start(f32[4,256]{1,0:T(4,128)S(1)} %get-tuple-element.113), channel_id=1, source_target_pairs={{0,1},{1,0},{2,3},{3,2},{4,5},{5,4},{6,7},{7,6},{8,9},{9,8},{10,11... | collective-permute-start | bytes 12296 | tf_op jit(solution)/shard_map/ppermute | solution.py:425
  29.2 3.1 %collective-permute-start.10 = (f32[4,256]{1,0:T(4,128)S(1)}, f32[4,256]{1,0:T(4,128)S(1)}, u32[]{:S(2)}, u32[]{:S(2)}) collective-permute-start(f32[4,256]{1,0:T(4,128)S(1)} %add.131), channel_id=1, source_target_pairs={{0,5},{1,4},{2,7},{3,6},{4,1},{5,0},{6,3},{7,2},{8,13},{9,12},{10,... | collective-permute-start | bytes 12296 | tf_op jit(solution)/shard_map/ppermute | solution.py:495
  30.7 3.0 %collective-permute-start.11 = (f32[4,256]{1,0:T(4,128)S(1)}, f32[4,256]{1,0:T(4,128)S(1)}, u32[]{:S(2)}, u32[]{:S(2)}) collective-permute-start(f32[4,256]{1,0:T(4,128)S(1)} %add.131), channel_id=1, source_target_pairs={{0,3},{1,2},{2,1},{3,0},{4,7},{5,6},{6,5},{7,4},{8,11},{9,10},{10,... | collective-permute-start | bytes 12296 | tf_op jit(solution)/shard_map/ppermute | solution.py:495
  31.0 3.9 %collective-permute-start.9 = (f32[4,256]{1,0:T(4,128)S(1)}, f32[4,256]{1,0:T(4,128)S(1)}, u32[]{:S(2)}, u32[]{:S(2)}) collective-permute-start(f32[4,256]{1,0:T(4,128)S(1)} %add.131), channel_id=1, source_target_pairs={{0,7},{1,6},{2,5},{3,4},{4,3},{5,2},{6,1},{7,0},{8,15},{9,14},{10,... | collective-permute-start | bytes 12296 | tf_op jit(solution)/shard_map/ppermute | solution.py:495
  35.0 4.8 %collective-permute-start.12 = (f32[4,256]{1,0:T(4,128)S(1)}, f32[4,256]{1,0:T(4,128)S(1)}, u32[]{:S(2)}, u32[]{:S(2)}) collective-permute-start(f32[4,256]{1,0:T(4,128)S(1)} %add_add_fusion.1), channel_id=1, source_target_pairs={{0,25},{1,24},{2,27},{3,26},{4,29},{5,28},{6,31},{7,30},{8,17},{9,... | collective-permute-start | bytes 12296 | tf_op jit(solution)/shard_map/ppermute | solution.py:495
  36.7 3.9 %collective-permute-start.13 = (f32[4,256]{1,0:T(4,128)S(1)}, f32[4,256]{1,0:T(4,128)S(1)}, u32[]{:S(2)}, u32[]{:S(2)}) collective-permute-start(f32[4,256]{1,0:T(4,128)S(1)} %add_add_fusion.1), channel_id=1, source_target_pairs={{0,17},{1,16},{2,19},{3,18},{4,21},{5,20},{6,23},{7,22},{8,25},{9,... | collective-permute-start | bytes 12296 | tf_op jit(solution)/shard_map/ppermute | solution.py:495
  36.8 3.8 %collective-permute-start.14 = (f32[4,256]{1,0:T(4,128)S(1)}, f32[4,256]{1,0:T(4,128)S(1)}, u32[]{:S(2)}, u32[]{:S(2)}) collective-permute-start(f32[4,256]{1,0:T(4,128)S(1)} %add_add_fusion.1), channel_id=1, source_target_pairs={{0,9},{1,8},{2,11},{3,10},{4,13},{5,12},{6,15},{7,14},{8,1},{9,0},... | collective-permute-start | bytes 12296 | tf_op jit(solution)/shard_map/ppermute | solution.py:495
  46.1 2.5 %collective-permute-start.15 = (f32[4,128,256]{2,1,0:T(8,128)S(1)}, f32[4,128,256]{2,1,0:T(8,128)S(1)}, u32[]{:S(2)}, u32[]{:S(2)}) collective-permute-start(f32[4,128,256]{2,1,0:T(8,128)S(1)} %bitcast.66), channel_id=1, source_target_pairs={{0,1},{1,0},{2,3},{3,2},{4,5},{5,4},{6,7},{7,6},{8,9},{9,8},{10,11... | collective-permute-start | bytes 1572872 | tf_op jit(solution)/shard_map/ppermute | solution.py:425
  48.6 4.0 %collective-permute-start.16 = (f32[5,128,256]{2,1,0:T(8,128)S(1)}, f32[5,128,256]{2,1,0:T(8,128)S(1)}, u32[]{:S(2)}, u32[]{:S(2)}) collective-permute-start(f32[5,128,256]{2,1,0:T(8,128)S(1)} %bitcast.65), channel_id=1, source_target_pairs={{0,1},{1,0},{2,3},{3,2},{4,5},{5,4},{6,7},{7,6},{8,9},{9,8},{10,11... | collective-permute-start | bytes 1966088 | tf_op jit(solution)/shard_map/ppermute | solution.py:425
  49.0 6.7 %collective-permute-start.20 = (bf16[128,256]{1,0:T(8,128)(2,1)S(1)}, bf16[128,256]{1,0:T(8,128)(2,1)S(1)}, u32[]{:S(2)}, u32[]{:S(2)}) collective-permute-start(bf16[128,256]{1,0:T(8,128)(2,1)S(1)} %get-tuple-element.182), channel_id=1, source_target_pairs={{0,6},{2,4},{4,2},{6,0},{8,14},{10,12},{12,10},{14,8},{16,22},{18,... | collective-permute-start | bytes 196616 | tf_op jit(solution)/shard_map/ppermute | solution.py:425
  50.5 5.9 %collective-permute-start.21 = (bf16[128,256]{1,0:T(8,128)(2,1)S(1)}, bf16[128,256]{1,0:T(8,128)(2,1)S(1)}, u32[]{:S(2)}, u32[]{:S(2)}) collective-permute-start(bf16[128,256]{1,0:T(8,128)(2,1)S(1)} %get-tuple-element.181), channel_id=1, source_target_pairs={{0,4},{2,6},{4,0},{6,2},{8,12},{10,14},{12,8},{14,10},{16,20},{18,... | collective-permute-start | bytes 196616 | tf_op jit(solution)/shard_map/ppermute | solution.py:425
  52.0 4.5 %collective-permute-start.22 = (bf16[128,256]{1,0:T(8,128)(2,1)S(1)}, bf16[128,256]{1,0:T(8,128)(2,1)S(1)}, u32[]{:S(2)}, u32[]{:S(2)}) collective-permute-start(bf16[128,256]{1,0:T(8,128)(2,1)S(1)} %get-tuple-element.180), channel_id=1, source_target_pairs={{0,2},{2,0},{4,6},{6,4},{8,10},{10,8},{12,14},{14,12},{16,18},{18,... | collective-permute-start | bytes 196616 | tf_op jit(solution)/shard_map/ppermute | solution.py:425
  52.7 6.3 %collective-permute-start.17 = (bf16[160,256]{1,0:T(8,128)(2,1)S(1)}, bf16[160,256]{1,0:T(8,128)(2,1)S(1)}, u32[]{:S(2)}, u32[]{:S(2)}) collective-permute-start(bf16[160,256]{1,0:T(8,128)(2,1)S(1)} %get-tuple-element.179), channel_id=1, source_target_pairs={{0,6},{2,4},{4,2},{6,0},{8,14},{10,12},{12,10},{14,8},{16,22},{18,... | collective-permute-start | bytes 245768 | tf_op jit(solution)/shard_map/ppermute | solution.py:425
  54.2 5.1 %collective-permute-start.18 = (bf16[160,256]{1,0:T(8,128)(2,1)S(1)}, bf16[160,256]{1,0:T(8,128)(2,1)S(1)}, u32[]{:S(2)}, u32[]{:S(2)}) collective-permute-start(bf16[160,256]{1,0:T(8,128)(2,1)S(1)} %get-tuple-element.178), channel_id=1, source_target_pairs={{0,4},{2,6},{4,0},{6,2},{8,12},{10,14},{12,8},{14,10},{16,20},{18,... | collective-permute-start | bytes 245768 | tf_op jit(solution)/shard_map/ppermute | solution.py:425
  55.7 4.4 %collective-permute-start.19 = (bf16[160,256]{1,0:T(8,128)(2,1)S(1)}, bf16[160,256]{1,0:T(8,128)(2,1)S(1)}, u32[]{:S(2)}, u32[]{:S(2)}) collective-permute-start(bf16[160,256]{1,0:T(8,128)(2,1)S(1)} %get-tuple-element.177), channel_id=1, source_target_pairs={{0,2},{2,0},{4,6},{6,4},{8,10},{10,8},{12,14},{14,12},{16,18},{18,... | collective-permute-start | bytes 245768 | tf_op jit(solution)/shard_map/ppermute | solution.py:425
  56.6 4.5 %collective-permute-start.24 = (bf16[128,256]{1,0:T(8,128)(2,1)S(1)}, bf16[128,256]{1,0:T(8,128)(2,1)S(1)}, u32[]{:S(2)}, u32[]{:S(2)}) collective-permute-start(bf16[128,256]{1,0:T(8,128)(2,1)S(1)} %fusion.3), channel_id=1, source_target_pairs={{0,9},{1,16},{2,11},{3,18},{4,13},{5,20},{6,15},{7,22},{8,25},{9,0... | collective-permute-start | bytes 196616 | tf_op jit(solution)/shard_map/ppermute | solution.py:572
  60.2 4.9 %collective-permute-start.23 = (bf16[160,256]{1,0:T(8,128)(2,1)S(1)}, bf16[160,256]{1,0:T(8,128)(2,1)S(1)}, u32[]{:S(2)}, u32[]{:S(2)}) collective-permute-start(bf16[160,256]{1,0:T(8,128)(2,1)S(1)} %fusion.1), channel_id=1, source_target_pairs={{0,9},{1,16},{2,11},{3,18},{4,13},{5,20},{6,15},{7,22},{8,25},{9,0... | collective-permute-start | bytes 245768 | tf_op jit(solution)/shard_map/ppermute | solution.py:572
  61.1 6.9 %collective-permute-start.27 = (bf16[128,256]{1,0:T(8,128)(2,1)S(1)}, bf16[128,256]{1,0:T(8,128)(2,1)S(1)}, u32[]{:S(2)}, u32[]{:S(2)}) collective-permute-start(bf16[128,256]{1,0:T(8,128)(2,1)S(1)} %add_convert_fusion.6), channel_id=1, source_target_pairs={{0,17},{1,8},{2,19},{3,10},{4,21},{5,12},{6,23},{7,14},{8,1},{9,24... | collective-permute-start | bytes 196616 | tf_op jit(solution)/shard_map/ppermute | solution.py:572
  65.1 6.7 %collective-permute-start.25 = (bf16[160,256]{1,0:T(8,128)(2,1)S(1)}, bf16[160,256]{1,0:T(8,128)(2,1)S(1)}, u32[]{:S(2)}, u32[]{:S(2)}) collective-permute-start(bf16[160,256]{1,0:T(8,128)(2,1)S(1)} %add_convert_fusion.1), channel_id=1, source_target_pairs={{0,17},{1,8},{2,19},{3,10},{4,21},{5,12},{6,23},{7,14},{8,1},{9,24... | collective-permute-start | bytes 245768 | tf_op jit(solution)/shard_map/ppermute | solution.py:572
  68.0 4.1 %collective-permute-start.31 = (bf16[128,256]{1,0:T(8,128)(2,1)S(1)}, bf16[128,256]{1,0:T(8,128)(2,1)S(1)}, u32[]{:S(2)}, u32[]{:S(2)}) collective-permute-start(bf16[128,256]{1,0:T(8,128)(2,1)S(1)} %add_convert_fusion.5), channel_id=1, source_target_pairs={{0,1},{1,0},{2,3},{3,2},{4,5},{5,4},{6,7},{7,6},{8,9},{9,8},{10,11... | collective-permute-start | bytes 196616 | tf_op jit(solution)/shard_map/ppermute | solution.py:425
  68.3 6.3 %collective-permute-start.28 = (bf16[128,256]{1,0:T(8,128)(2,1)S(1)}, bf16[128,256]{1,0:T(8,128)(2,1)S(1)}, u32[]{:S(2)}, u32[]{:S(2)}) collective-permute-start(bf16[128,256]{1,0:T(8,128)(2,1)S(1)} %add_convert_fusion.5), channel_id=1, source_target_pairs={{0,6},{1,7},{2,4},{3,5},{4,2},{5,3},{6,0},{7,1},{8,15},{9,14},{10,... | collective-permute-start | bytes 196616 | tf_op jit(solution)/shard_map/ppermute | solution.py:582
  69.2 9.6 %collective-permute-start.29 = (bf16[128,256]{1,0:T(8,128)(2,1)S(1)}, bf16[128,256]{1,0:T(8,128)(2,1)S(1)}, u32[]{:S(2)}, u32[]{:S(2)}) collective-permute-start(bf16[128,256]{1,0:T(8,128)(2,1)S(1)} %add_convert_fusion.5), channel_id=1, source_target_pairs={{0,4},{1,5},{2,6},{3,7},{4,0},{5,1},{6,2},{7,3},{8,13},{9,12},{10,... | collective-permute-start | bytes 196616 | tf_op jit(solution)/shard_map/ppermute | solution.py:582
  70.7 8.1 %collective-permute-start.30 = (bf16[128,256]{1,0:T(8,128)(2,1)S(1)}, bf16[128,256]{1,0:T(8,128)(2,1)S(1)}, u32[]{:S(2)}, u32[]{:S(2)}) collective-permute-start(bf16[128,256]{1,0:T(8,128)(2,1)S(1)} %add_convert_fusion.5), channel_id=1, source_target_pairs={{0,2},{1,3},{2,0},{3,1},{4,6},{5,7},{6,4},{7,5},{8,11},{9,10},{10,... | collective-permute-start | bytes 196616 | tf_op jit(solution)/shard_map/ppermute | solution.py:582
  71.9 1.3 %collective-permute-start.26 = (bf16[160,256]{1,0:T(8,128)(2,1)S(1)}, bf16[160,256]{1,0:T(8,128)(2,1)S(1)}, u32[]{:S(2)}, u32[]{:S(2)}) collective-permute-start(bf16[160,256]{1,0:T(8,128)(2,1)S(1)} %add_convert_fusion), channel_id=1, source_target_pairs={{0,1},{1,0},{2,3},{3,2},{4,5},{5,4},{6,7},{7,6},{8,9},{9,8},{10,11... | collective-permute-start | bytes 245768 | tf_op jit(solution)/shard_map/ppermute | solution.py:425
  72.2 6.8 %collective-permute-start.32 = (bf16[160,256]{1,0:T(8,128)(2,1)S(1)}, bf16[160,256]{1,0:T(8,128)(2,1)S(1)}, u32[]{:S(2)}, u32[]{:S(2)}) collective-permute-start(bf16[160,256]{1,0:T(8,128)(2,1)S(1)} %add_convert_fusion), channel_id=1, source_target_pairs={{0,6},{1,7},{2,4},{3,5},{4,2},{5,3},{6,0},{7,1},{8,15},{9,14},{10,... | collective-permute-start | bytes 245768 | tf_op jit(solution)/shard_map/ppermute | solution.py:582
  73.2 6.3 %collective-permute-start.33 = (bf16[160,256]{1,0:T(8,128)(2,1)S(1)}, bf16[160,256]{1,0:T(8,128)(2,1)S(1)}, u32[]{:S(2)}, u32[]{:S(2)}) collective-permute-start(bf16[160,256]{1,0:T(8,128)(2,1)S(1)} %add_convert_fusion), channel_id=1, source_target_pairs={{0,4},{1,5},{2,6},{3,7},{4,0},{5,1},{6,2},{7,3},{8,13},{9,12},{10,... | collective-permute-start | bytes 245768 | tf_op jit(solution)/shard_map/ppermute | solution.py:582
  74.7 4.9 %collective-permute-start.34 = (bf16[160,256]{1,0:T(8,128)(2,1)S(1)}, bf16[160,256]{1,0:T(8,128)(2,1)S(1)}, u32[]{:S(2)}, u32[]{:S(2)}) collective-permute-start(bf16[160,256]{1,0:T(8,128)(2,1)S(1)} %add_convert_fusion), channel_id=1, source_target_pairs={{0,2},{1,3},{2,0},{3,1},{4,6},{5,7},{6,4},{7,5},{8,11},{9,10},{10,... | collective-permute-start | bytes 245768 | tf_op jit(solution)/shard_map/ppermute | solution.py:582
  79.6 1.0 %copy-start.7 = (f32[36,32,256]{2,1,0:T(8,128)}, f32[36,32,256]{2,1,0:T(8,128)S(1)}, u32[]{:S(2)}) copy-start(f32[36,32,256]{2,1,0:T(8,128)S(1)} %convert_dynamic-update-slice_fusion) | copy-start | bytes 3538948

commit v4 on v3

--- a/solution.py
+++ b/solution.py
@@ -329,7 +329,7 @@
             if step == 0:
                 own_ref[tap] = part
             else:
-                sent_ref[step - 1, tap] = part
+                sent_ref[step - 1, tap] = part.astype(sent_ref.dtype)
 
 
 def backward_kernel(
@@ -548,7 +548,7 @@
     def piece(k):
         total = piece_of(parts[0], found.digits[k])
         for part in parts[1:]:
-            total = total + piece_of(part, found.digits[k])
+            total = total + piece_of(part, found.digits[k]).astype(F32)
         return total
 
     return piece(0), [piece(k).astype(BF16) for k in FAR_FIRST]
@@ -703,16 +703,16 @@
     wide_four, wide_six = (
         jax.ShapeDtypeStruct(framed.shape[:2] + (3 * chan,), BF16) for framed in (framed_four, framed_six)
     )
-    def shares(taps):
+    def shares(taps, dtype):
         return (
             jax.ShapeDtypeStruct((taps, share, chan), F32),
-            jax.ShapeDtypeStruct((sp_count - 1, taps, share, chan), F32),
+            jax.ShapeDtypeStruct((sp_count - 1, taps, share, chan), dtype),
         )
 
     three_four, three_six, own_a, sent_a, rest, grad_gain, grad_shift = pl.pallas_call(
         functools.partial(backward_kernel, counts, sp_count, (cols_four, cols_six)),
         out_shape=(wide_four, wide_six)
-        + shares(FIRST_TAPS)
+        + shares(FIRST_TAPS, BF16)
         + (jax.ShapeDtypeStruct((chan, (EARLY_TAPS - FIRST_TAPS) * chan), F32),)
         + (jax.ShapeDtypeStruct((2, chan), F32),) * 2,
         in_specs=[vmem] * 11,
@@ -729,7 +729,7 @@
     met_a = [swap(sent_a[step], "sp", step + 1) for step in range(sp_count - 1)]
     own_b, sent_b = pl.pallas_call(
         functools.partial(weight_kernel, sp_count),
-        out_shape=shares(9 - FIRST_TAPS),
+        out_shape=shares(9 - FIRST_TAPS, F32),
         in_specs=[vmem] * 4,
         out_specs=(vmem, vmem),
         scratch_shapes=[pltpu.VMEM((chan, (9 - EARLY_TAPS) * chan), F32)],

time: 80.8 us -> 80.8 us (level)
  no operation moved by 1% of the time
where the time goes in v4:
time: 80.8 us; the launch traced here: 80.6 us
  starting transfers between devices  35.5 us (44%)
  Pallas kernels  27.2 us (34%)
  waiting for transfers between devices  15.3 us (19%)
  local copies, waits for them, and re-layouts  1.16 us (1%)
  between operations  1.02 us (1%)
    ppermute x12, starting transfers between devices, swap_across(): return lax.ppermute(array, ('rep', 'sp'), pairs)  15.2 us
    ppermute x13, starting transfers between devices, swap(): return lax.ppermute(array, axis, [(i, i ^ stride) for i in range(count)])  9.75 us
    ppermute x12, waiting for transfers between devices, swap_across(): return lax.ppermute(array, ('rep', 'sp'), pairs)  9.51 us
    ppermute x6, starting transfers between devices, bring(): return lax.ppermute(array, ('rep', 'sp'), pairs)  7.01 us
    pallas_call x1, Pallas kernels, local(): pl.pallas_call(inner_kernel, out_shape=(jax.ShapeDtypeStruct((rows_four -...  5.87 us
    pallas_call x1, Pallas kernels, local(): pl.pallas_call(functools.partial(backward_kernel, counts, sp_count, (cols...  5.51 us
    pallas_call x2, Pallas kernels, inputs(): pl.pallas_call(functools.partial(input_kernel, group), out_shape=parts, i...  4.43 us
    ppermute x4, starting transfers between devices, swap_high(): return lax.ppermute(array, ('rep', 'sp'), pairs)  3.5 us
  transfers between devices with their start and end apart: 35, of which 17 were waited for; matrix products, arithmetic and copies ran while one was open for 1% of the time, Pallas kernels for 20%

profile of v4, /device:TPU:0, one launch (start us, length us, event | category | flops | bytes accessed | tf_op | source)
XLA Modules:
  0.0 80.6 jit_solution(1309848307220273345)
XLA Ops:
  0.7 1.7 %edges.1 = bf16[384,256]{1,0:T(8,128)(2,1)} custom-call(bf16[48,96,256]{2,1,0:T(8,128)(2,1)} %bitcast.51, bf16[12,24,256]{2,1,0:T(8,128)(2,1)} %bitcast.59, bf16[48,96,256]{2,1,0:T(8,128)(2,1)} %bitcast.55, bf16[12,24,256]{2,1,0:T(8,128)(2,1)} %bitcast.63), custom_call_target="tpu_custom_call" | custom-call | tf_op jit(solution)/shard_map/edges/pallas_call | solution.py:467
  2.4 0.5 collective-permute-start
  3.0 5.9 %forward_inner.1 = (bf16[46,96,256]{2,1,0:T(8,128)(2,1)S(1)}, bf16[10,32,256]{2,1,0:T(8,128)(2,1)S(1)}, f32[4,256]{1,0:T(4,128)S(1)}) custom-call(bf16[48,96,256]{2,1,0:T(8,128)(2,1)S(1)} %bitcast.52, bf16[12,24,256]{2,1,0:T(8,128)(2,1)S(1)} %bitcast.60, bf16[9,256,256]{2,1,0:T(8,128)(2,1)S(1)} %copy-done.2), custom_call_target="tpu_custom_call" | custom-call | flops 5775556608 | bytes 4718592 | tf_op jit(solution)/shard_map/forward_inner/pallas_call | solution.py:636
  8.9 0.8 forward_outer.1
  9.6 0.4 collective-permute-start.1
  10.0 0.8 %collective-permute-done.1 = f32[4,256]{1,0:T(4,128)S(1)} collective-permute-done((f32[4,256]{1,0:T(4,128)S(1)}, f32[4,256]{1,0:T(4,128)S(1)}, u32[]{:S(2)}, u32[]{:S(2)}) %collective-permute-start.1) | collective-permute-done | bytes 4128 | tf_op jit(solution)/shard_map/ppermute | solution.py:425
  10.9 3.6 %collective-permute-start.2 = (f32[4,256]{1,0:T(4,128)S(1)}, f32[4,256]{1,0:T(4,128)S(1)}, u32[]{:S(2)}, u32[]{:S(2)}) collective-permute-start(f32[4,256]{1,0:T(4,128)S(1)} %add.124), channel_id=1, source_target_pairs={{0,7},{1,6},{2,5},{3,4},{4,3},{5,2},{6,1},{7,0},{8,15},{9,14},{10,... | collective-permute-start | bytes 12296 | tf_op jit(solution)/shard_map/ppermute | solution.py:495
  14.4 0.4 collective-permute-start.3
  14.9 0.1 collective-permute-start.4
  14.9 0.8 %collective-permute-done.2 = f32[4,256]{1,0:T(4,128)S(1)} collective-permute-done((f32[4,256]{1,0:T(4,128)S(1)}, f32[4,256]{1,0:T(4,128)S(1)}, u32[]{:S(2)}, u32[]{:S(2)}) %collective-permute-start.2) | collective-permute-done | bytes 4128 | tf_op jit(solution)/shard_map/ppermute | solution.py:495
  15.8 1.7 %collective-permute-done.3 = f32[4,256]{1,0:T(4,128)S(1)} collective-permute-done((f32[4,256]{1,0:T(4,128)S(1)}, f32[4,256]{1,0:T(4,128)S(1)}, u32[]{:S(2)}, u32[]{:S(2)}) %collective-permute-start.3) | collective-permute-done | bytes 4128 | tf_op jit(solution)/shard_map/ppermute | solution.py:495
  17.5 0.4 collective-permute-done.4
  17.9 3.5 %collective-permute-start.5 = (f32[4,256]{1,0:T(4,128)S(1)}, f32[4,256]{1,0:T(4,128)S(1)}, u32[]{:S(2)}, u32[]{:S(2)}) collective-permute-start(f32[4,256]{1,0:T(4,128)S(1)} %add_add_fusion.3), channel_id=1, source_target_pairs={{0,25},{1,24},{2,27},{3,26},{4,29},{5,28},{6,31},{7,30},{8,17},{9,... | collective-permute-start | bytes 12296 | tf_op jit(solution)/shard_map/ppermute | solution.py:495
  21.4 0.6 collective-permute-start.7
  21.9 1.0 %turn.1 = (bf16[256,4992]{1,0:T(8,128)(2,1)S(1)}, bf16[2304,256]{1,0:T(8,128)(2,1)S(1)}) custom-call(bf16[48,96,256]{2,1,0:T(8,128)(2,1)S(1)} %bitcast.54, bf16[12,24,256]{2,1,0:T(8,128)(2,1)S(1)} %bitcast.62, bf16[9,256,256]{2,1,0:T(8,128)(2,1)S(1)} %copy-done.2), custom_call_target="tpu_custom_call" | custom-call | flops 1732667008 | bytes 4718592 | tf_op jit(solution)/shard_map/turn/pallas_call | solution.py:671
  23.0 2.4 %collective-permute-done.6 = f32[4,256]{1,0:T(4,128)S(1)} collective-permute-done((f32[4,256]{1,0:T(4,128)S(1)}, f32[4,256]{1,0:T(4,128)S(1)}, u32[]{:S(2)}, u32[]{:S(2)}) %collective-permute-start.6) | collective-permute-done | bytes 4128 | tf_op jit(solution)/shard_map/ppermute | solution.py:495
  25.4 2.6 %slopes.1 = (f32[50,96,256]{2,1,0:T(8,128)S(1)}, f32[14,32,256]{2,1,0:T(8,128)S(1)}, f32[4,256]{1,0:T(4,128)S(1)}) custom-call(bf16[46,96,256]{2,1,0:T(8,128)(2,1)S(1)} %get-tuple-element.106.inner_four_ref, bf16[10,32,256]{2,1,0:T(8,128)(2,1)S(1)} %get-tuple-element.107.inner_six_ref, bf16[4,96,256]{2,1,0:T(8,128)(2,1)S(1)} %get-tuple-element.108.outer_four_ref, ...), custom_call_target="tpu_custom_call" | custom-call | flops 57755568 | bytes 4718592 | tf_op jit(solution)/shard_map/slopes/pallas_call | solution.py:685
  28.0 0.4 collective-permute-start.8
  28.4 0.9 %collective-permute-done.8 = f32[4,256]{1,0:T(4,128)S(1)} collective-permute-done((f32[4,256]{1,0:T(4,128)S(1)}, f32[4,256]{1,0:T(4,128)S(1)}, u32[]{:S(2)}, u32[]{:S(2)}) %collective-permute-start.8) | collective-permute-done | bytes 4128 | tf_op jit(solution)/shard_map/ppermute | solution.py:425
  29.2 1.4 %collective-permute-start.10 = (f32[4,256]{1,0:T(4,128)S(1)}, f32[4,256]{1,0:T(4,128)S(1)}, u32[]{:S(2)}, u32[]{:S(2)}) collective-permute-start(f32[4,256]{1,0:T(4,128)S(1)} %add.131), channel_id=1, source_target_pairs={{0,5},{1,4},{2,7},{3,6},{4,1},{5,0},{6,3},{7,2},{8,13},{9,12},{10,... | collective-permute-start | bytes 12296 | tf_op jit(solution)/shard_map/ppermute | solution.py:495
  30.7 0.3 collective-permute-start.11
  31.0 1.3 %collective-permute-start.9 = (f32[4,256]{1,0:T(4,128)S(1)}, f32[4,256]{1,0:T(4,128)S(1)}, u32[]{:S(2)}, u32[]{:S(2)}) collective-permute-start(f32[4,256]{1,0:T(4,128)S(1)} %add.131), channel_id=1, source_target_pairs={{0,7},{1,6},{2,5},{3,4},{4,3},{5,2},{6,1},{7,0},{8,15},{9,14},{10,... | collective-permute-start | bytes 12296 | tf_op jit(solution)/shard_map/ppermute | solution.py:495
  32.4 1.3 %collective-permute-done.11 = f32[4,256]{1,0:T(4,128)S(1)} collective-permute-done((f32[4,256]{1,0:T(4,128)S(1)}, f32[4,256]{1,0:T(4,128)S(1)}, u32[]{:S(2)}, u32[]{:S(2)}) %collective-permute-start.11) | collective-permute-done | bytes 4128 | tf_op jit(solution)/shard_map/ppermute | solution.py:495
  33.7 1.2 %collective-permute-done.9 = f32[4,256]{1,0:T(4,128)S(1)} collective-permute-done((f32[4,256]{1,0:T(4,128)S(1)}, f32[4,256]{1,0:T(4,128)S(1)}, u32[]{:S(2)}, u32[]{:S(2)}) %collective-permute-start.9) | collective-permute-done | bytes 4128 | tf_op jit(solution)/shard_map/ppermute | solution.py:495
  35.0 1.7 %collective-permute-start.12 = (f32[4,256]{1,0:T(4,128)S(1)}, f32[4,256]{1,0:T(4,128)S(1)}, u32[]{:S(2)}, u32[]{:S(2)}) collective-permute-start(f32[4,256]{1,0:T(4,128)S(1)} %add_add_fusion.1), channel_id=1, source_target_pairs={{0,25},{1,24},{2,27},{3,26},{4,29},{5,28},{6,31},{7,30},{8,17},{9,... | collective-permute-start | bytes 12296 | tf_op jit(solution)/shard_map/ppermute | solution.py:495
  36.7 0.1 collective-permute-start.13
  36.8 2.2 %collective-permute-start.14 = (f32[4,256]{1,0:T(4,128)S(1)}, f32[4,256]{1,0:T(4,128)S(1)}, u32[]{:S(2)}, u32[]{:S(2)}) collective-permute-start(f32[4,256]{1,0:T(4,128)S(1)} %add_add_fusion.1), channel_id=1, source_target_pairs={{0,9},{1,8},{2,11},{3,10},{4,13},{5,12},{6,15},{7,14},{8,1},{9,0},... | collective-permute-start | bytes 12296 | tf_op jit(solution)/shard_map/ppermute | solution.py:495
  39.0 0.8 %collective-permute-done.12 = f32[4,256]{1,0:T(4,128)S(1)} collective-permute-done((f32[4,256]{1,0:T(4,128)S(1)}, f32[4,256]{1,0:T(4,128)S(1)}, u32[]{:S(2)}, u32[]{:S(2)}) %collective-permute-start.12) | collective-permute-done | bytes 4128 | tf_op jit(solution)/shard_map/ppermute | solution.py:495
  39.8 0.8 collective-permute-done.13
  40.6 5.5 %backward.1 = (bf16[50,96,768]{2,1,0:T(8,128)(2,1)S(1)}, bf16[14,32,768]{2,1,0:T(8,128)(2,1)S(1)}, f32[4,128,256]{2,1,0:T(8,128)S(1)}, bf16[1,4,128,256]{3,2,1,0...) custom-call(bf16[256,4992]{1,0:T(8,128)(2,1)S(1)} %get-tuple-element.105.turned_ref, ...), custom_call_target="tpu_custom_call" | custom-call | flops 3465334016 | bytes 9437184 | tf_op jit(solution)/shard_map/backward/pallas_call | solution.py:712
  46.1 0.2 collective-permute-start.15
  46.3 2.3 %weights.1 = (f32[5,128,256]{2,1,0:T(8,128)S(1)}, f32[1,5,128,256]{3,2,1,0:T(8,128)S(1)}) custom-call(bf16[256,4992]{1,0:T(8,128)(2,1)S(1)} %get-tuple-element.105.turned_ref, bf16[50,96,768]{2,1,0:T(8,128)(2,1)S(1)} %get-tuple-element.153.three_four, bf16[14,32,768]{2,1,0:T(8,128)(2,1)S(1)} %get-tuple-element.123.three_six, ...), custom_call_target="tpu_custom_call" | custom-call | flops 3465334016 | bytes 9437184 | tf_op jit(solution)/shard_map/weights/pallas_call | solution.py:730
  48.6 0.4 collective-permute-start.16
  49.0 1.5 %collective-permute-start.20 = (bf16[128,256]{1,0:T(8,128)(2,1)S(1)}, bf16[128,256]{1,0:T(8,128)(2,1)S(1)}, u32[]{:S(2)}, u32[]{:S(2)}) collective-permute-start(bf16[128,256]{1,0:T(8,128)(2,1)S(1)} %get-tuple-element.182), channel_id=1, source_target_pairs={{0,6},{2,4},{4,2},{6,0},{8,14},{10,12},{12,10},{14,8},{16,22},{18,... | collective-permute-start | bytes 196616 | tf_op jit(solution)/shard_map/ppermute | solution.py:425
  50.5 1.5 %collective-permute-start.21 = (bf16[128,256]{1,0:T(8,128)(2,1)S(1)}, bf16[128,256]{1,0:T(8,128)(2,1)S(1)}, u32[]{:S(2)}, u32[]{:S(2)}) collective-permute-start(bf16[128,256]{1,0:T(8,128)(2,1)S(1)} %get-tuple-element.181), channel_id=1, source_target_pairs={{0,4},{2,6},{4,0},{6,2},{8,12},{10,14},{12,8},{14,10},{16,20},{18,... | collective-permute-start | bytes 196616 | tf_op jit(solution)/shard_map/ppermute | solution.py:425
  52.0 0.5 collective-permute-start.22
  52.6 0.1 fusion.6
  52.6 1.5 %collective-permute-start.17 = (bf16[160,256]{1,0:T(8,128)(2,1)S(1)}, bf16[160,256]{1,0:T(8,128)(2,1)S(1)}, u32[]{:S(2)}, u32[]{:S(2)}) collective-permute-start(bf16[160,256]{1,0:T(8,128)(2,1)S(1)} %get-tuple-element.179), channel_id=1, source_target_pairs={{0,6},{2,4},{4,2},{6,0},{8,14},{10,12},{12,10},{14,8},{16,22},{18,... | collective-permute-start | bytes 245768 | tf_op jit(solution)/shard_map/ppermute | solution.py:425
  54.2 1.5 %collective-permute-start.18 = (bf16[160,256]{1,0:T(8,128)(2,1)S(1)}, bf16[160,256]{1,0:T(8,128)(2,1)S(1)}, u32[]{:S(2)}, u32[]{:S(2)}) collective-permute-start(bf16[160,256]{1,0:T(8,128)(2,1)S(1)} %get-tuple-element.178), channel_id=1, source_target_pairs={{0,4},{2,6},{4,0},{6,2},{8,12},{10,14},{12,8},{14,10},{16,20},{18,... | collective-permute-start | bytes 245768 | tf_op jit(solution)/shard_map/ppermute | solution.py:425
  55.7 0.7 collective-permute-start.19
  56.4 0.2 collective-permute-done.22
  56.6 0.3 collective-permute-start.24
  56.9 2.0 %inputs.2.rest_0_ = bf16[16,96,256]{2,1,0:T(8,128)(2,1)S(1)} custom-call(bf16[50,96,768]{2,1,0:T(8,128)(2,1)S(1)} %get-tuple-element.153.three_four, bf16[14,32,768]{2,1,0:T(8,128)(2,1)S(1)} %get-tuple-element.123.three_six, bf16[2304,256]{1,0:T(8,128)(2,1)S(1)} %get-tuple-element.139.turned), custom_call_target="tpu_custom_call" | custom-call | flops 1732667008 | bytes 1179648 | tf_op jit(solution)/shard_map/inputs/pallas_call | solution.py:753
  58.9 0.3 collective-permute-done.18
  59.2 0.9 %collective-permute-done.19 = bf16[160,256]{1,0:T(8,128)(2,1)S(1)} collective-permute-done((bf16[160,256]{1,0:T(8,128)(2,1)S(1)}, bf16[160,256]{1,0:T(8,128)(2,1)S(1)}, u32[]{:S(2)}, u32[]{:S(2)}) %collective-permute-start.19) | collective-permute-done | bytes 81952 | tf_op jit(solution)/shard_map/ppermute | solution.py:425
  60.2 0.4 collective-permute-start.23
  60.6 0.5 collective-permute-done.24
  61.1 1.6 %collective-permute-start.27 = (bf16[128,256]{1,0:T(8,128)(2,1)S(1)}, bf16[128,256]{1,0:T(8,128)(2,1)S(1)}, u32[]{:S(2)}, u32[]{:S(2)}) collective-permute-start(bf16[128,256]{1,0:T(8,128)(2,1)S(1)} %add_convert_fusion.6), channel_id=1, source_target_pairs={{0,17},{1,8},{2,19},{3,10},{4,21},{5,12},{6,23},{7,14},{8,1},{9,24... | collective-permute-start | bytes 196616 | tf_op jit(solution)/shard_map/ppermute | solution.py:572
  62.6 2.5 %inputs.3 = (bf16[16,96,256]{2,1,0:T(8,128)(2,1)S(1)}, bf16[12,24,256]{2,1,0:T(8,128)(2,1)S(1)}) custom-call(bf16[50,96,768]{2,1,0:T(8,128)(2,1)S(1)} %get-tuple-element.153.three_four, bf16[14,32,768]{2,1,0:T(8,128)(2,1)S(1)} %get-tuple-element.123.three_six, bf16[2304,256]{1,0:T(8,128)(2,1)S(1)} %get-tuple-element.139.turned), custom_call_target="tpu_custom_call" | custom-call | flops 1732667008 | bytes 1179648 | tf_op jit(solution)/shard_map/inputs/pallas_call | solution.py:753
  65.1 1.2 %collective-permute-start.25 = (bf16[160,256]{1,0:T(8,128)(2,1)S(1)}, bf16[160,256]{1,0:T(8,128)(2,1)S(1)}, u32[]{:S(2)}, u32[]{:S(2)}) collective-permute-start(bf16[160,256]{1,0:T(8,128)(2,1)S(1)} %add_convert_fusion.1), channel_id=1, source_target_pairs={{0,17},{1,8},{2,19},{3,10},{4,21},{5,12},{6,23},{7,14},{8,1},{9,24... | collective-permute-start | bytes 245768 | tf_op jit(solution)/shard_map/ppermute | solution.py:572
  66.4 1.7 %collective-permute-done.27 = bf16[128,256]{1,0:T(8,128)(2,1)S(1)} collective-permute-done((bf16[128,256]{1,0:T(8,128)(2,1)S(1)}, bf16[128,256]{1,0:T(8,128)(2,1)S(1)}, u32[]{:S(2)}, u32[]{:S(2)}) %collective-permute-start.27) | collective-permute-done | bytes 65568 | tf_op jit(solution)/shard_map/ppermute | solution.py:572
  68.0 0.3 collective-permute-start.31
  68.3 0.8 %collective-permute-start.28 = (bf16[128,256]{1,0:T(8,128)(2,1)S(1)}, bf16[128,256]{1,0:T(8,128)(2,1)S(1)}, u32[]{:S(2)}, u32[]{:S(2)}) collective-permute-start(bf16[128,256]{1,0:T(8,128)(2,1)S(1)} %add_convert_fusion.5), channel_id=1, source_target_pairs={{0,6},{1,7},{2,4},{3,5},{4,2},{5,3},{6,0},{7,1},{8,15},{9,14},{10,... | collective-permute-start | bytes 196616 | tf_op jit(solution)/shard_map/ppermute | solution.py:582
  69.2 1.5 %collective-permute-start.29 = (bf16[128,256]{1,0:T(8,128)(2,1)S(1)}, bf16[128,256]{1,0:T(8,128)(2,1)S(1)}, u32[]{:S(2)}, u32[]{:S(2)}) collective-permute-start(bf16[128,256]{1,0:T(8,128)(2,1)S(1)} %add_convert_fusion.5), channel_id=1, source_target_pairs={{0,4},{1,5},{2,6},{3,7},{4,0},{5,1},{6,2},{7,3},{8,13},{9,12},{10,... | collective-permute-start | bytes 196616 | tf_op jit(solution)/shard_map/ppermute | solution.py:582
  70.7 1.1 %collective-permute-start.30 = (bf16[128,256]{1,0:T(8,128)(2,1)S(1)}, bf16[128,256]{1,0:T(8,128)(2,1)S(1)}, u32[]{:S(2)}, u32[]{:S(2)}) collective-permute-start(bf16[128,256]{1,0:T(8,128)(2,1)S(1)} %add_convert_fusion.5), channel_id=1, source_target_pairs={{0,2},{1,3},{2,0},{3,1},{4,6},{5,7},{6,4},{7,5},{8,11},{9,10},{10,... | collective-permute-start | bytes 196616 | tf_op jit(solution)/shard_map/ppermute | solution.py:582
  71.9 0.3 collective-permute-start.26
  72.2 0.9 %collective-permute-start.32 = (bf16[160,256]{1,0:T(8,128)(2,1)S(1)}, bf16[160,256]{1,0:T(8,128)(2,1)S(1)}, u32[]{:S(2)}, u32[]{:S(2)}) collective-permute-start(bf16[160,256]{1,0:T(8,128)(2,1)S(1)} %add_convert_fusion), channel_id=1, source_target_pairs={{0,6},{1,7},{2,4},{3,5},{4,2},{5,3},{6,0},{7,1},{8,15},{9,14},{10,... | collective-permute-start | bytes 245768 | tf_op jit(solution)/shard_map/ppermute | solution.py:582
  73.1 0.1 collective-permute-done.26
  73.2 1.4 %collective-permute-start.33 = (bf16[160,256]{1,0:T(8,128)(2,1)S(1)}, bf16[160,256]{1,0:T(8,128)(2,1)S(1)}, u32[]{:S(2)}, u32[]{:S(2)}) collective-permute-start(bf16[160,256]{1,0:T(8,128)(2,1)S(1)} %add_convert_fusion), channel_id=1, source_target_pairs={{0,4},{1,5},{2,6},{3,7},{4,0},{5,1},{6,2},{7,3},{8,13},{9,12},{10,... | collective-permute-start | bytes 245768 | tf_op jit(solution)/shard_map/ppermute | solution.py:582
  74.7 1.2 %collective-permute-start.34 = (bf16[160,256]{1,0:T(8,128)(2,1)S(1)}, bf16[160,256]{1,0:T(8,128)(2,1)S(1)}, u32[]{:S(2)}, u32[]{:S(2)}) collective-permute-start(bf16[160,256]{1,0:T(8,128)(2,1)S(1)} %add_convert_fusion), channel_id=1, source_target_pairs={{0,2},{1,3},{2,0},{3,1},{4,6},{5,7},{6,4},{7,5},{8,11},{9,10},{10,... | collective-permute-start | bytes 245768 | tf_op jit(solution)/shard_map/ppermute | solution.py:582
  75.9 2.9 %inputs_last.1 = (bf16[48,96,256]{2,1,0:T(8,128)(2,1)}, bf16[12,24,256]{2,1,0:T(8,128)(2,1)}) custom-call(bf16[50,96,768]{2,1,0:T(8,128)(2,1)S(1)} %get-tuple-element.153.three_four, bf16[2304,256]{1,0:T(8,128)(2,1)S(1)} %get-tuple-element.139.turned, bf16[12,24,256]{2,1,0:T(8,128)(2,1)S(1)} %get-tuple-element.154.six_ref, ...), custom_call_target="tpu_custom_call" | custom-call | flops 2310222592 | bytes 2359296 | tf_op jit(solution)/shard_map/inputs_last/pallas_call | solution.py:799
  78.8 0.1 broadcast_in_dim.9
  79.1 0.4 collective-permute-done.33
  79.6 1.0 %copy-done.7 = f32[36,32,256]{2,1,0:T(8,128)} copy-done((f32[36,32,256]{2,1,0:T(8,128)}, f32[36,32,256]{2,1,0:T(8,128)S(1)}, u32[]{:S(2)}) %copy-start.7) | copy-done | bytes 1179672
  (57 shorter events, 0.5 us)
Async XLA Ops:
  0.7 2.3 %copy-start = (bf16[1,48,96,256]{3,2,1,0:T(8,128)(2,1)S(1)}, bf16[1,48,96,256]{3,2,1,0:T(8,128)(2,1)}, u32[]{:S(2)}) copy-start(bf16[1,48,96,256]{3,2,1,0:T(8,128)(2,1)} %param.7) | copy-start | bytes 7077892
  0.7 2.3 %copy-start.2 = (bf16[9,256,256]{2,1,0:T(8,128)(2,1)S(1)}, bf16[9,256,256]{2,1,0:T(8,128)(2,1)}, u32[]{:S(2)}) copy-start(bf16[9,256,256]{2,1,0:T(8,128)(2,1)} %w_ref.5) | copy-start | bytes 3538948
  0.7 2.3 %copy-start.3 = (bf16[1,12,24,256]{3,2,1,0:T(8,128)(2,1)S(1)}, bf16[1,12,24,256]{3,2,1,0:T(8,128)(2,1)}, u32[]{:S(2)}) copy-start(bf16[1,12,24,256]{3,2,1,0:T(8,128)(2,1)} %param.8) | copy-start | bytes 442372
  2.4 6.4 %collective-permute-start = (bf16[384,256]{1,0:T(8,128)(2,1)}, bf16[384,256]{1,0:T(8,128)(2,1)S(1)}, u32[]{:S(2)}, u32[]{:S(2)}) collective-permute-start(bf16[384,256]{1,0:T(8,128)(2,1)} %edges.1), channel_id=1, source_target_pairs={{0,1},{1,0},{2,3},{3,2},{4,5},{5,4},{6,7},{7,6},{8,9},{9,8},{10,11... | collective-permute-start | bytes 589832 | tf_op jit(solution)/shard_map/ppermute | solution.py:425
  9.6 1.2 %collective-permute-start.1 = (f32[4,256]{1,0:T(4,128)S(1)}, f32[4,256]{1,0:T(4,128)S(1)}, u32[]{:S(2)}, u32[]{:S(2)}) collective-permute-start(f32[4,256]{1,0:T(4,128)S(1)} %get-tuple-element.94), channel_id=1, source_target_pairs={{0,1},{1,0},{2,3},{3,2},{4,5},{5,4},{6,7},{7,6},{8,9},{9,8},{10,11... | collective-permute-start | bytes 12296 | tf_op jit(solution)/shard_map/ppermute | solution.py:425
  10.9 4.9 %collective-permute-start.2 = (f32[4,256]{1,0:T(4,128)S(1)}, f32[4,256]{1,0:T(4,128)S(1)}, u32[]{:S(2)}, u32[]{:S(2)}) collective-permute-start(f32[4,256]{1,0:T(4,128)S(1)} %add.124), channel_id=1, source_target_pairs={{0,7},{1,6},{2,5},{3,4},{4,3},{5,2},{6,1},{7,0},{8,15},{9,14},{10,... | collective-permute-start | bytes 12296 | tf_op jit(solution)/shard_map/ppermute | solution.py:495
  14.4 3.0 %collective-permute-start.3 = (f32[4,256]{1,0:T(4,128)S(1)}, f32[4,256]{1,0:T(4,128)S(1)}, u32[]{:S(2)}, u32[]{:S(2)}) collective-permute-start(f32[4,256]{1,0:T(4,128)S(1)} %add.124), channel_id=1, source_target_pairs={{0,5},{1,4},{2,7},{3,6},{4,1},{5,0},{6,3},{7,2},{8,13},{9,12},{10,... | collective-permute-start | bytes 12296 | tf_op jit(solution)/shard_map/ppermute | solution.py:495
  14.9 3.0 %collective-permute-start.4 = (f32[4,256]{1,0:T(4,128)S(1)}, f32[4,256]{1,0:T(4,128)S(1)}, u32[]{:S(2)}, u32[]{:S(2)}) collective-permute-start(f32[4,256]{1,0:T(4,128)S(1)} %add.124), channel_id=1, source_target_pairs={{0,3},{1,2},{2,1},{3,0},{4,7},{5,6},{6,5},{7,4},{8,11},{9,10},{10,... | collective-permute-start | bytes 12296 | tf_op jit(solution)/shard_map/ppermute | solution.py:495
  17.9 7.4 %copy-start.4 = (bf16[1,12,24,256]{3,2,1,0:T(8,128)(2,1)S(1)}, bf16[1,12,24,256]{3,2,1,0:T(8,128)(2,1)}, u32[]{:S(2)}) copy-start(bf16[1,12,24,256]{3,2,1,0:T(8,128)(2,1)} %param.13) | copy-start | bytes 442372
  17.9 7.4 %copy-start.5 = (f32[2,256]{1,0:T(2,128)S(1)}, f32[2,256]{1,0:T(2,128)}, u32[]{:S(2)}) copy-start(f32[2,256]{1,0:T(2,128)} %gain_ref.3) | copy-start | bytes 6148
  17.9 7.5 %copy-start.6 = (f32[2,256]{1,0:T(2,128)S(1)}, f32[2,256]{1,0:T(2,128)}, u32[]{:S(2)}) copy-start(f32[2,256]{1,0:T(2,128)} %shift_ref.3) | copy-start | bytes 6148
  17.9 5.0 %collective-permute-start.5 = (f32[4,256]{1,0:T(4,128)S(1)}, f32[4,256]{1,0:T(4,128)S(1)}, u32[]{:S(2)}, u32[]{:S(2)}) collective-permute-start(f32[4,256]{1,0:T(4,128)S(1)} %add_add_fusion.3), channel_id=1, source_target_pairs={{0,25},{1,24},{2,27},{3,26},{4,29},{5,28},{6,31},{7,30},{8,17},{9,... | collective-permute-start | bytes 12296 | tf_op jit(solution)/shard_map/ppermute | solution.py:495
  21.4 3.9 %collective-permute-start.6 = (f32[4,256]{1,0:T(4,128)S(1)}, f32[4,256]{1,0:T(4,128)S(1)}, u32[]{:S(2)}, u32[]{:S(2)}) collective-permute-start(f32[4,256]{1,0:T(4,128)S(1)} %add_add_fusion.3), channel_id=1, source_target_pairs={{0,17},{1,16},{2,19},{3,18},{4,21},{5,20},{6,23},{7,22},{8,25},{9,... | collective-permute-start | bytes 12296 | tf_op jit(solution)/shard_map/ppermute | solution.py:495
  21.4 3.9 %collective-permute-start.7 = (f32[4,256]{1,0:T(4,128)S(1)}, f32[4,256]{1,0:T(4,128)S(1)}, u32[]{:S(2)}, u32[]{:S(2)}) collective-permute-start(f32[4,256]{1,0:T(4,128)S(1)} %add_add_fusion.3), channel_id=1, source_target_pairs={{0,9},{1,8},{2,11},{3,10},{4,13},{5,12},{6,15},{7,14},{8,1},{9,0},... | collective-permute-start | bytes 12296 | tf_op jit(solution)/shard_map/ppermute | solution.py:495
  21.9 3.4 %copy-start.1 = (bf16[1,48,96,256]{3,2,1,0:T(8,128)(2,1)S(1)}, bf16[1,48,96,256]{3,2,1,0:T(8,128)(2,1)}, u32[]{:S(2)}) copy-start(bf16[1,48,96,256]{3,2,1,0:T(8,128)(2,1)} %param.12) | copy-start | bytes 7077892
  28.0 1.2 %collective-permute-start.8 = (f32[4,256]{1,0:T(4,128)S(1)}, f32[4,256]{1,0:T(4,128)S(1)}, u32[]{:S(2)}, u32[]{:S(2)}) collective-permute-start(f32[4,256]{1,0:T(4,128)S(1)} %get-tuple-element.113), channel_id=1, source_target_pairs={{0,1},{1,0},{2,3},{3,2},{4,5},{5,4},{6,7},{7,6},{8,9},{9,8},{10,11... | collective-permute-start | bytes 12296 | tf_op jit(solution)/shard_map/ppermute | solution.py:425
  29.2 3.1 %collective-permute-start.10 = (f32[4,256]{1,0:T(4,128)S(1)}, f32[4,256]{1,0:T(4,128)S(1)}, u32[]{:S(2)}, u32[]{:S(2)}) collective-permute-start(f32[4,256]{1,0:T(4,128)S(1)} %add.131), channel_id=1, source_target_pairs={{0,5},{1,4},{2,7},{3,6},{4,1},{5,0},{6,3},{7,2},{8,13},{9,12},{10,... | collective-permute-start | bytes 12296 | tf_op jit(solution)/shard_map/ppermute | solution.py:495
  30.7 3.0 %collective-permute-start.11 = (f32[4,256]{1,0:T(4,128)S(1)}, f32[4,256]{1,0:T(4,128)S(1)}, u32[]{:S(2)}, u32[]{:S(2)}) collective-permute-start(f32[4,256]{1,0:T(4,128)S(1)} %add.131), channel_id=1, source_target_pairs={{0,3},{1,2},{2,1},{3,0},{4,7},{5,6},{6,5},{7,4},{8,11},{9,10},{10,... | collective-permute-start | bytes 12296 | tf_op jit(solution)/shard_map/ppermute | solution.py:495
  31.0 3.9 %collective-permute-start.9 = (f32[4,256]{1,0:T(4,128)S(1)}, f32[4,256]{1,0:T(4,128)S(1)}, u32[]{:S(2)}, u32[]{:S(2)}) collective-permute-start(f32[4,256]{1,0:T(4,128)S(1)} %add.131), channel_id=1, source_target_pairs={{0,7},{1,6},{2,5},{3,4},{4,3},{5,2},{6,1},{7,0},{8,15},{9,14},{10,... | collective-permute-start | bytes 12296 | tf_op jit(solution)/shard_map/ppermute | solution.py:495
  35.0 4.8 %collective-permute-start.12 = (f32[4,256]{1,0:T(4,128)S(1)}, f32[4,256]{1,0:T(4,128)S(1)}, u32[]{:S(2)}, u32[]{:S(2)}) collective-permute-start(f32[4,256]{1,0:T(4,128)S(1)} %add_add_fusion.1), channel_id=1, source_target_pairs={{0,25},{1,24},{2,27},{3,26},{4,29},{5,28},{6,31},{7,30},{8,17},{9,... | collective-permute-start | bytes 12296 | tf_op jit(solution)/shard_map/ppermute | solution.py:495
  36.7 3.9 %collective-permute-start.13 = (f32[4,256]{1,0:T(4,128)S(1)}, f32[4,256]{1,0:T(4,128)S(1)}, u32[]{:S(2)}, u32[]{:S(2)}) collective-permute-start(f32[4,256]{1,0:T(4,128)S(1)} %add_add_fusion.1), channel_id=1, source_target_pairs={{0,17},{1,16},{2,19},{3,18},{4,21},{5,20},{6,23},{7,22},{8,25},{9,... | collective-permute-start | bytes 12296 | tf_op jit(solution)/shard_map/ppermute | solution.py:495
  36.8 3.8 %collective-permute-start.14 = (f32[4,256]{1,0:T(4,128)S(1)}, f32[4,256]{1,0:T(4,128)S(1)}, u32[]{:S(2)}, u32[]{:S(2)}) collective-permute-start(f32[4,256]{1,0:T(4,128)S(1)} %add_add_fusion.1), channel_id=1, source_target_pairs={{0,9},{1,8},{2,11},{3,10},{4,13},{5,12},{6,15},{7,14},{8,1},{9,0},... | collective-permute-start | bytes 12296 | tf_op jit(solution)/shard_map/ppermute | solution.py:495
  46.1 2.5 %collective-permute-start.15 = (bf16[4,128,256]{2,1,0:T(8,128)(2,1)S(1)}, bf16[4,128,256]{2,1,0:T(8,128)(2,1)S(1)}, u32[]{:S(2)}, u32[]{:S(2)}) collective-permute-start(bf16[4,128,256]{2,1,0:T(8,128)(2,1)S(1)} %bitcast.66), channel_id=1, source_target_pairs={{0,1},{1,0},{2,3},{3,2},{4,5},{5,4},{6,7},{7,6},{8,9},{9,8},{10,11... | collective-permute-start | bytes 786440 | tf_op jit(solution)/shard_map/ppermute | solution.py:425
  48.6 4.0 %collective-permute-start.16 = (f32[5,128,256]{2,1,0:T(8,128)S(1)}, f32[5,128,256]{2,1,0:T(8,128)S(1)}, u32[]{:S(2)}, u32[]{:S(2)}) collective-permute-start(f32[5,128,256]{2,1,0:T(8,128)S(1)} %bitcast.65), channel_id=1, source_target_pairs={{0,1},{1,0},{2,3},{3,2},{4,5},{5,4},{6,7},{7,6},{8,9},{9,8},{10,11... | collective-permute-start | bytes 1966088 | tf_op jit(solution)/shard_map/ppermute | solution.py:425
  49.0 6.7 %collective-permute-start.20 = (bf16[128,256]{1,0:T(8,128)(2,1)S(1)}, bf16[128,256]{1,0:T(8,128)(2,1)S(1)}, u32[]{:S(2)}, u32[]{:S(2)}) collective-permute-start(bf16[128,256]{1,0:T(8,128)(2,1)S(1)} %get-tuple-element.182), channel_id=1, source_target_pairs={{0,6},{2,4},{4,2},{6,0},{8,14},{10,12},{12,10},{14,8},{16,22},{18,... | collective-permute-start | bytes 196616 | tf_op jit(solution)/shard_map/ppermute | solution.py:425
  50.5 5.9 %collective-permute-start.21 = (bf16[128,256]{1,0:T(8,128)(2,1)S(1)}, bf16[128,256]{1,0:T(8,128)(2,1)S(1)}, u32[]{:S(2)}, u32[]{:S(2)}) collective-permute-start(bf16[128,256]{1,0:T(8,128)(2,1)S(1)} %get-tuple-element.181), channel_id=1, source_target_pairs={{0,4},{2,6},{4,0},{6,2},{8,12},{10,14},{12,8},{14,10},{16,20},{18,... | collective-permute-start | bytes 196616 | tf_op jit(solution)/shard_map/ppermute | solution.py:425
  52.0 4.5 %collective-permute-start.22 = (bf16[128,256]{1,0:T(8,128)(2,1)S(1)}, bf16[128,256]{1,0:T(8,128)(2,1)S(1)}, u32[]{:S(2)}, u32[]{:S(2)}) collective-permute-start(bf16[128,256]{1,0:T(8,128)(2,1)S(1)} %get-tuple-element.180), channel_id=1, source_target_pairs={{0,2},{2,0},{4,6},{6,4},{8,10},{10,8},{12,14},{14,12},{16,18},{18,... | collective-permute-start | bytes 196616 | tf_op jit(solution)/shard_map/ppermute | solution.py:425
  52.6 6.3 %collective-permute-start.17 = (bf16[160,256]{1,0:T(8,128)(2,1)S(1)}, bf16[160,256]{1,0:T(8,128)(2,1)S(1)}, u32[]{:S(2)}, u32[]{:S(2)}) collective-permute-start(bf16[160,256]{1,0:T(8,128)(2,1)S(1)} %get-tuple-element.179), channel_id=1, source_target_pairs={{0,6},{2,4},{4,2},{6,0},{8,14},{10,12},{12,10},{14,8},{16,22},{18,... | collective-permute-start | bytes 245768 | tf_op jit(solution)/shard_map/ppermute | solution.py:425
  54.2 5.1 %collective-permute-start.18 = (bf16[160,256]{1,0:T(8,128)(2,1)S(1)}, bf16[160,256]{1,0:T(8,128)(2,1)S(1)}, u32[]{:S(2)}, u32[]{:S(2)}) collective-permute-start(bf16[160,256]{1,0:T(8,128)(2,1)S(1)} %get-tuple-element.178), channel_id=1, source_target_pairs={{0,4},{2,6},{4,0},{6,2},{8,12},{10,14},{12,8},{14,10},{16,20},{18,... | collective-permute-start | bytes 245768 | tf_op jit(solution)/shard_map/ppermute | solution.py:425
  55.7 4.4 %collective-permute-start.19 = (bf16[160,256]{1,0:T(8,128)(2,1)S(1)}, bf16[160,256]{1,0:T(8,128)(2,1)S(1)}, u32[]{:S(2)}, u32[]{:S(2)}) collective-permute-start(bf16[160,256]{1,0:T(8,128)(2,1)S(1)} %get-tuple-element.177), channel_id=1, source_target_pairs={{0,2},{2,0},{4,6},{6,4},{8,10},{10,8},{12,14},{14,12},{16,18},{18,... | collective-permute-start | bytes 245768 | tf_op jit(solution)/shard_map/ppermute | solution.py:425
  56.6 4.5 %collective-permute-start.24 = (bf16[128,256]{1,0:T(8,128)(2,1)S(1)}, bf16[128,256]{1,0:T(8,128)(2,1)S(1)}, u32[]{:S(2)}, u32[]{:S(2)}) collective-permute-start(bf16[128,256]{1,0:T(8,128)(2,1)S(1)} %fusion.3), channel_id=1, source_target_pairs={{0,9},{1,16},{2,11},{3,18},{4,13},{5,20},{6,15},{7,22},{8,25},{9,0... | collective-permute-start | bytes 196616 | tf_op jit(solution)/shard_map/ppermute | solution.py:572
  60.2 4.9 %collective-permute-start.23 = (bf16[160,256]{1,0:T(8,128)(2,1)S(1)}, bf16[160,256]{1,0:T(8,128)(2,1)S(1)}, u32[]{:S(2)}, u32[]{:S(2)}) collective-permute-start(bf16[160,256]{1,0:T(8,128)(2,1)S(1)} %fusion.1), channel_id=1, source_target_pairs={{0,9},{1,16},{2,11},{3,18},{4,13},{5,20},{6,15},{7,22},{8,25},{9,0... | collective-permute-start | bytes 245768 | tf_op jit(solution)/shard_map/ppermute | solution.py:572
  61.1 6.9 %collective-permute-start.27 = (bf16[128,256]{1,0:T(8,128)(2,1)S(1)}, bf16[128,256]{1,0:T(8,128)(2,1)S(1)}, u32[]{:S(2)}, u32[]{:S(2)}) collective-permute-start(bf16[128,256]{1,0:T(8,128)(2,1)S(1)} %add_convert_fusion.6), channel_id=1, source_target_pairs={{0,17},{1,8},{2,19},{3,10},{4,21},{5,12},{6,23},{7,14},{8,1},{9,24... | collective-permute-start | bytes 196616 | tf_op jit(solution)/shard_map/ppermute | solution.py:572
  65.1 6.7 %collective-permute-start.25 = (bf16[160,256]{1,0:T(8,128)(2,1)S(1)}, bf16[160,256]{1,0:T(8,128)(2,1)S(1)}, u32[]{:S(2)}, u32[]{:S(2)}) collective-permute-start(bf16[160,256]{1,0:T(8,128)(2,1)S(1)} %add_convert_fusion.1), channel_id=1, source_target_pairs={{0,17},{1,8},{2,19},{3,10},{4,21},{5,12},{6,23},{7,14},{8,1},{9,24... | collective-permute-start | bytes 245768 | tf_op jit(solution)/shard_map/ppermute | solution.py:572
  68.0 4.1 %collective-permute-start.31 = (bf16[128,256]{1,0:T(8,128)(2,1)S(1)}, bf16[128,256]{1,0:T(8,128)(2,1)S(1)}, u32[]{:S(2)}, u32[]{:S(2)}) collective-permute-start(bf16[128,256]{1,0:T(8,128)(2,1)S(1)} %add_convert_fusion.5), channel_id=1, source_target_pairs={{0,1},{1,0},{2,3},{3,2},{4,5},{5,4},{6,7},{7,6},{8,9},{9,8},{10,11... | collective-permute-start | bytes 196616 | tf_op jit(solution)/shard_map/ppermute | solution.py:425
  68.3 6.3 %collective-permute-start.28 = (bf16[128,256]{1,0:T(8,128)(2,1)S(1)}, bf16[128,256]{1,0:T(8,128)(2,1)S(1)}, u32[]{:S(2)}, u32[]{:S(2)}) collective-permute-start(bf16[128,256]{1,0:T(8,128)(2,1)S(1)} %add_convert_fusion.5), channel_id=1, source_target_pairs={{0,6},{1,7},{2,4},{3,5},{4,2},{5,3},{6,0},{7,1},{8,15},{9,14},{10,... | collective-permute-start | bytes 196616 | tf_op jit(solution)/shard_map/ppermute | solution.py:582
  69.2 9.6 %collective-permute-start.29 = (bf16[128,256]{1,0:T(8,128)(2,1)S(1)}, bf16[128,256]{1,0:T(8,128)(2,1)S(1)}, u32[]{:S(2)}, u32[]{:S(2)}) collective-permute-start(bf16[128,256]{1,0:T(8,128)(2,1)S(1)} %add_convert_fusion.5), channel_id=1, source_target_pairs={{0,4},{1,5},{2,6},{3,7},{4,0},{5,1},{6,2},{7,3},{8,13},{9,12},{10,... | collective-permute-start | bytes 196616 | tf_op jit(solution)/shard_map/ppermute | solution.py:582
  70.7 8.1 %collective-permute-start.30 = (bf16[128,256]{1,0:T(8,128)(2,1)S(1)}, bf16[128,256]{1,0:T(8,128)(2,1)S(1)}, u32[]{:S(2)}, u32[]{:S(2)}) collective-permute-start(bf16[128,256]{1,0:T(8,128)(2,1)S(1)} %add_convert_fusion.5), channel_id=1, source_target_pairs={{0,2},{1,3},{2,0},{3,1},{4,6},{5,7},{6,4},{7,5},{8,11},{9,10},{10,... | collective-permute-start | bytes 196616 | tf_op jit(solution)/shard_map/ppermute | solution.py:582
  71.9 1.3 %collective-permute-start.26 = (bf16[160,256]{1,0:T(8,128)(2,1)S(1)}, bf16[160,256]{1,0:T(8,128)(2,1)S(1)}, u32[]{:S(2)}, u32[]{:S(2)}) collective-permute-start(bf16[160,256]{1,0:T(8,128)(2,1)S(1)} %add_convert_fusion), channel_id=1, source_target_pairs={{0,1},{1,0},{2,3},{3,2},{4,5},{5,4},{6,7},{7,6},{8,9},{9,8},{10,11... | collective-permute-start | bytes 245768 | tf_op jit(solution)/shard_map/ppermute | solution.py:425
  72.2 6.8 %collective-permute-start.32 = (bf16[160,256]{1,0:T(8,128)(2,1)S(1)}, bf16[160,256]{1,0:T(8,128)(2,1)S(1)}, u32[]{:S(2)}, u32[]{:S(2)}) collective-permute-start(bf16[160,256]{1,0:T(8,128)(2,1)S(1)} %add_convert_fusion), channel_id=1, source_target_pairs={{0,6},{1,7},{2,4},{3,5},{4,2},{5,3},{6,0},{7,1},{8,15},{9,14},{10,... | collective-permute-start | bytes 245768 | tf_op jit(solution)/shard_map/ppermute | solution.py:582
  73.2 6.3 %collective-permute-start.33 = (bf16[160,256]{1,0:T(8,128)(2,1)S(1)}, bf16[160,256]{1,0:T(8,128)(2,1)S(1)}, u32[]{:S(2)}, u32[]{:S(2)}) collective-permute-start(bf16[160,256]{1,0:T(8,128)(2,1)S(1)} %add_convert_fusion), channel_id=1, source_target_pairs={{0,4},{1,5},{2,6},{3,7},{4,0},{5,1},{6,2},{7,3},{8,13},{9,12},{10,... | collective-permute-start | bytes 245768 | tf_op jit(solution)/shard_map/ppermute | solution.py:582
  74.7 4.9 %collective-permute-start.34 = (bf16[160,256]{1,0:T(8,128)(2,1)S(1)}, bf16[160,256]{1,0:T(8,128)(2,1)S(1)}, u32[]{:S(2)}, u32[]{:S(2)}) collective-permute-start(bf16[160,256]{1,0:T(8,128)(2,1)S(1)} %add_convert_fusion), channel_id=1, source_target_pairs={{0,2},{1,3},{2,0},{3,1},{4,6},{5,7},{6,4},{7,5},{8,11},{9,10},{10,... | collective-permute-start | bytes 245768 | tf_op jit(solution)/shard_map/ppermute | solution.py:582
  79.6 1.0 %copy-start.7 = (f32[36,32,256]{2,1,0:T(8,128)}, f32[36,32,256]{2,1,0:T(8,128)S(1)}, u32[]{:S(2)}) copy-start(f32[36,32,256]{2,1,0:T(8,128)S(1)} %convert_dynamic-update-slice_fusion) | copy-start | bytes 3538948
